TPU v7x, 32 devices: a whole 2x2x4 slice. The times are simulated.
32 devices in a mesh: section: 2 (over x), dp: 16 (over z, y, core).
Axes of the slice: x: 2, y: 2, z: 4, core: 2. Of those that a mesh axis runs over, the one named last changes fastest.
Arguments:
- tokens: bfloat16 [64, 256, 640], P('dp'), may hold values from -6 to 6
- lengths: int32 [64], P('dp'), may hold values from 64 to 256
- cotangent: bfloat16 [64, 256, 640], P('dp'), may hold values from -6 to 6
- w_qkv: bfloat16 [2, 640, 1920], P('section', 'dp'), may hold values from -0.25 to 0.25
- w_out: bfloat16 [2, 640, 640], P('section', 'dp'), may hold values from -1 to 1
- w_up: bfloat16 [2, 640, 5120], P('section', 'dp'), may hold values from -0.25 to 0.25
- w_down: bfloat16 [2, 5120, 640], P('section', 'dp'), may hold values from -0.078125 to 0.078125
- norm_gain: bfloat16 [2, 2, 640], P('section', None, 'dp'), may hold values from 0.25 to 1.75
- norm_bias: bfloat16 [2, 2, 640], P('section', None, 'dp'), may hold values from -1 to 1
- bias_vec: bfloat16 [2, 4, 640], P('section', None, 'dp'), may hold values from -1 to 1
- up_bias: bfloat16 [2, 5120], P('section', 'dp'), may hold values from -1 to 1
Outputs:
- hidden_out: bfloat16 [2, 64, 256, 640], P('section', 'dp')
- input_grads: float32 [2, 64, 256, 640], P('section', 'dp')
- grad_qkv: float32 [2, 640, 1920], P('section', 'dp')
- grad_out: float32 [2, 640, 640], P('section', 'dp')
- grad_up: float32 [2, 640, 5120], P('section', 'dp')
- grad_down: float32 [2, 5120, 640], P('section', 'dp')
- grad_gain: float32 [2, 2, 640], P('section', None, 'dp')
- grad_norm_bias: float32 [2, 2, 640], P('section', None, 'dp')
- grad_bias_vec: float32 [2, 4, 640], P('section', None, 'dp')
- grad_up_bias: float32 [2, 5120], P('section', 'dp')
All inputs are finite; a program needn't handle non-finite values.
Results may differ from a plain program's by a relative error of at most 0.015.
Values may be sent and summed in bfloat16 or wider, within the bound.
No kernel may reach another device: no remote copies, remote signals or barrier semaphores. Data moves between devices by JAX's collectives and lax.ppermute only.
A program may use at most 320 MiB of HBM per device.

v0:
```python
import jax
import jax.numpy as jnp
from jax import lax
from jax.sharding import PartitionSpec as P

HEADS = 20
HEAD_DIM = 32


def from_behind(value, axis, steps):
    count = lax.axis_size(axis)
    leading, last = (max(0, -steps), min(count, count - steps))
    return lax.ppermute(value, axis, [(source, source + steps) for source in range(leading, last)])


def layer_norm(values, gain, shift):
    centered = values - jnp.mean(values, axis=-1, keepdims=True)
    spread = jnp.mean(centered * centered, axis=-1, keepdims=True)
    return centered * lax.rsqrt(spread + 1e-05) * gain + shift


def exact_gelu(values):
    return jax.nn.gelu(values, approximate=False)


def forward_pieces(hidden, window_len, params):
    w_qkv, w_out, w_up, w_down, gains, shifts, biases, up_bias = params
    seq_len, width = hidden.shape
    normed = layer_norm(hidden, gains[0], shifts[0]).astype(jnp.bfloat16)
    bias_qkv = jnp.concatenate([biases[0], jnp.zeros_like(biases[0]), biases[1]])
    qkv = (jnp.dot(normed, w_qkv, preferred_element_type=jnp.float32) + bias_qkv).astype(
        jnp.bfloat16
    )
    query = qkv[:, :width].reshape(seq_len, HEADS, HEAD_DIM)
    key_part = qkv[:, width : 2 * width].reshape(seq_len, HEADS, HEAD_DIM)
    value = qkv[:, 2 * width :].reshape(seq_len, HEADS, HEAD_DIM)
    raw = jnp.einsum("qhe,khe->hqk", query, key_part, preferred_element_type=jnp.float32)
    valid = (jnp.arange(seq_len) < window_len)[None, None, :]
    scores = jnp.where(valid, raw * HEAD_DIM ** (-0.5), -1e30)
    highest = jnp.max(scores, axis=-1, keepdims=True)
    expo = jnp.exp(scores - highest)
    probs = expo / jnp.sum(expo, axis=-1, keepdims=True)
    probs_low = probs.astype(jnp.bfloat16)
    mixed = jnp.einsum("hqk,khe->qhe", probs_low, value, preferred_element_type=jnp.float32)
    mixed = mixed.reshape(seq_len, width).astype(jnp.bfloat16)
    middle = hidden + jnp.dot(mixed, w_out, preferred_element_type=jnp.float32) + biases[2]
    normed_two = layer_norm(middle, gains[1], shifts[1]).astype(jnp.bfloat16)
    pre = jnp.dot(normed_two, w_up, preferred_element_type=jnp.float32) + up_bias
    act = exact_gelu(pre).astype(jnp.bfloat16)
    result = middle + jnp.dot(act, w_down, preferred_element_type=jnp.float32) + biases[3]
    kept = (normed, query, key_part, value, probs, probs_low, mixed, middle, normed_two, pre, act)
    return (kept, result)


def backward_pieces(hidden, window_len, params, grad_result):
    w_qkv, w_out, w_up, w_down, gains, shifts, biases, up_bias = params
    kept, _ = forward_pieces(hidden, window_len, params)
    normed, query, key_part, value, probs, probs_low, mixed, middle, normed_two, pre, act = kept
    seq_len, width = hidden.shape
    grad_low = grad_result.astype(jnp.bfloat16)
    g_down = jnp.einsum("sf,sd->fd", act, grad_low, preferred_element_type=jnp.float32)
    g_bdown = jnp.sum(grad_low.astype(jnp.float32), axis=0)
    d_act = jnp.einsum("sd,fd->sf", grad_low, w_down, preferred_element_type=jnp.float32)
    _, gelu_back = jax.vjp(exact_gelu, pre)
    d_pre = gelu_back(d_act)[0].astype(jnp.bfloat16)
    g_up = jnp.einsum("sd,sf->df", normed_two, d_pre, preferred_element_type=jnp.float32)
    g_bup = jnp.sum(d_pre.astype(jnp.float32), axis=0)
    d_norm_two = jnp.einsum("sf,df->sd", d_pre, w_up, preferred_element_type=jnp.float32)
    _, norm_back_two = jax.vjp(layer_norm, middle, gains[1], shifts[1])
    d_middle, g_gain_two, g_shift_two = norm_back_two(d_norm_two)
    d_middle = d_middle + grad_result
    d_branch = d_middle.astype(jnp.bfloat16)
    g_out = jnp.einsum("sd,se->de", mixed, d_branch, preferred_element_type=jnp.float32)
    g_bout = jnp.sum(d_branch.astype(jnp.float32), axis=0)
    d_mixed = jnp.einsum("se,de->sd", d_branch, w_out, preferred_element_type=jnp.float32)
    d_mixed = d_mixed.astype(jnp.bfloat16).reshape(seq_len, HEADS, HEAD_DIM)
    g_value = jnp.einsum("hqk,qhe->khe", probs_low, d_mixed, preferred_element_type=jnp.float32)
    d_probs = jnp.einsum("qhe,khe->hqk", d_mixed, value, preferred_element_type=jnp.float32)
    d_scores = probs * (d_probs - jnp.sum(probs * d_probs, axis=-1, keepdims=True))
    d_raw = (d_scores * HEAD_DIM ** (-0.5)).astype(jnp.bfloat16)
    g_query = jnp.einsum("hqk,khe->qhe", d_raw, key_part, preferred_element_type=jnp.float32)
    g_key = jnp.einsum("hqk,qhe->khe", d_raw, query, preferred_element_type=jnp.float32)
    d_qkv = jnp.concatenate(
        [
            g_query.reshape(seq_len, width),
            g_key.reshape(seq_len, width),
            g_value.reshape(seq_len, width),
        ],
        axis=1,
    ).astype(jnp.bfloat16)
    g_qkv = jnp.einsum("sd,se->de", normed, d_qkv, preferred_element_type=jnp.float32)
    d_wide = d_qkv.astype(jnp.float32)
    g_bquery = jnp.sum(d_wide[:, :width], axis=0)
    g_bvalue = jnp.sum(d_wide[:, 2 * width :], axis=0)
    d_norm_one = jnp.einsum("se,de->sd", d_qkv, w_qkv, preferred_element_type=jnp.float32)
    _, norm_back_one = jax.vjp(layer_norm, hidden, gains[0], shifts[0])
    d_hidden, g_gain_one, g_shift_one = norm_back_one(d_norm_one)
    grad_in = d_hidden + d_middle
    grads = (
        g_qkv,
        g_out,
        g_up,
        g_down,
        jnp.stack([g_gain_one, g_gain_two]),
        jnp.stack([g_shift_one, g_shift_two]),
        jnp.stack([g_bquery, g_bvalue, g_bout, g_bdown]),
        g_bup,
    )
    return (grad_in, grads)


def on_device(
    tokens, lengths, cotangent, w_qkv, w_out, w_up, w_down, norm_gain, norm_bias, bias_vec, up_bias
):
    shards = (w_qkv, w_out, w_up, w_down, norm_gain, norm_bias, bias_vec, up_bias)
    gathered = (
        lax.all_gather(shards[0], "dp", axis=1, tiled=True),
        lax.all_gather(shards[1], "dp", axis=1, tiled=True),
        lax.all_gather(shards[2], "dp", axis=1, tiled=True),
        lax.all_gather(shards[3], "dp", axis=1, tiled=True),
        lax.all_gather(shards[4], "dp", axis=2, tiled=True),
        lax.all_gather(shards[5], "dp", axis=2, tiled=True),
        lax.all_gather(shards[6], "dp", axis=2, tiled=True),
        lax.all_gather(shards[7], "dp", axis=1, tiled=True),
    )
    params = (
        gathered[0][0],
        gathered[1][0],
        gathered[2][0],
        gathered[3][0],
        gathered[4][0].astype(jnp.float32),
        gathered[5][0].astype(jnp.float32),
        gathered[6][0].astype(jnp.float32),
        gathered[7][0].astype(jnp.float32),
    )
    section_id = lax.axis_index("section")
    micro = tokens.shape[0]
    stored = jnp.zeros(tokens.shape, jnp.bfloat16)
    outputs = jnp.zeros(tokens.shape, jnp.bfloat16)
    sending = jnp.zeros(tokens.shape[1:], jnp.bfloat16)
    for tick in range(micro + 1):
        slot_id = tick - section_id
        active = (slot_id >= 0) & (slot_id < micro)
        place = jnp.clip(slot_id, 0, micro - 1)
        if tick > 0:
            arrived = from_behind(sending, "section", 1)
        else:
            arrived = jnp.zeros_like(sending)
        layer_in = jnp.where(section_id == 0, tokens[min(tick, micro - 1)], arrived)
        _, result = forward_pieces(layer_in.astype(jnp.float32), lengths[place], params)
        sending = result.astype(jnp.bfloat16)
        stored = jnp.where(
            active, lax.dynamic_update_index_in_dim(stored, layer_in, place, 0), stored
        )
        outputs = jnp.where(
            active, lax.dynamic_update_index_in_dim(outputs, sending, place, 0), outputs
        )
    regathered = (
        lax.all_gather(shards[0], "dp", axis=1, tiled=True),
        lax.all_gather(shards[1], "dp", axis=1, tiled=True),
        lax.all_gather(shards[2], "dp", axis=1, tiled=True),
        lax.all_gather(shards[3], "dp", axis=1, tiled=True),
        lax.all_gather(shards[4], "dp", axis=2, tiled=True),
        lax.all_gather(shards[5], "dp", axis=2, tiled=True),
        lax.all_gather(shards[6], "dp", axis=2, tiled=True),
        lax.all_gather(shards[7], "dp", axis=1, tiled=True),
    )
    again = (
        regathered[0][0],
        regathered[1][0],
        regathered[2][0],
        regathered[3][0],
        regathered[4][0].astype(jnp.float32),
        regathered[5][0].astype(jnp.float32),
        regathered[6][0].astype(jnp.float32),
        regathered[7][0].astype(jnp.float32),
    )
    shard_sums = tuple((jnp.zeros(piece.shape, jnp.float32) for piece in shards))
    input_grads = jnp.zeros(tokens.shape, jnp.float32)
    returning = jnp.zeros(tokens.shape[1:], jnp.bfloat16)
    for tick in range(micro + 1):
        slot_id = tick - (1 - section_id)
        active = (slot_id >= 0) & (slot_id < micro)
        place = jnp.clip(slot_id, 0, micro - 1)
        if tick > 0:
            arrived = from_behind(returning, "section", -1)
        else:
            arrived = jnp.zeros_like(returning)
        upstream = jnp.where(section_id == 1, cotangent[min(tick, micro - 1)], arrived).astype(
            jnp.float32
        )
        layer_in = stored[place].astype(jnp.float32)
        grad_in, grads = backward_pieces(layer_in, lengths[place], again, upstream)
        weight = active.astype(jnp.float32)
        grads = tuple((term * weight for term in grads))
        returning = grad_in.astype(jnp.bfloat16)
        input_grads = jnp.where(
            active, lax.dynamic_update_index_in_dim(input_grads, grad_in, place, 0), input_grads
        )
        shaped = tuple((term[None] for term in grads))
        parts = (
            lax.psum_scatter(shaped[0], "dp", scatter_dimension=1, tiled=True),
            lax.psum_scatter(shaped[1], "dp", scatter_dimension=1, tiled=True),
            lax.psum_scatter(shaped[2], "dp", scatter_dimension=1, tiled=True),
            lax.psum_scatter(shaped[3], "dp", scatter_dimension=1, tiled=True),
            lax.psum_scatter(shaped[4], "dp", scatter_dimension=2, tiled=True),
            lax.psum_scatter(shaped[5], "dp", scatter_dimension=2, tiled=True),
            lax.psum_scatter(shaped[6], "dp", scatter_dimension=2, tiled=True),
            lax.psum_scatter(shaped[7], "dp", scatter_dimension=1, tiled=True),
        )
        shard_sums = tuple((left + right for left, right in zip(shard_sums, parts)))
    return (
        outputs[None],
        input_grads[None],
        shard_sums[0],
        shard_sums[1],
        shard_sums[2],
        shard_sums[3],
        shard_sums[4],
        shard_sums[5],
        shard_sums[6],
        shard_sums[7],
    )


def solution(mesh):
    in_specs = (
        P("dp", None, None),
        P("dp"),
        P("dp", None, None),
        P("section", "dp", None),
        P("section", "dp", None),
        P("section", "dp", None),
        P("section", "dp", None),
        P("section", None, "dp"),
        P("section", None, "dp"),
        P("section", None, "dp"),
        P("section", "dp"),
    )
    out_specs = (
        P("section", "dp", None, None),
        P("section", "dp", None, None),
        P("section", "dp", None),
        P("section", "dp", None),
        P("section", "dp", None),
        P("section", "dp", None),
        P("section", None, "dp"),
        P("section", None, "dp"),
        P("section", None, "dp"),
        P("section", "dp"),
    )
    return jax.shard_map(
        on_device, mesh=mesh, in_specs=in_specs, out_specs=out_specs, check_vma=False
    )
```

profile of v0, /device:TPU:0, one launch (start us, length us, event | category | flops | bytes accessed | tf_op | source)
XLA Modules:
  0.0 1312.5 jit_solution(14952238487262265051)
XLA Ops:
  10.3 24.7 %all_gather.32 = bf16[1,2,640]{1,0,2:T(2,128)(2,1)S(1)} all-gather(bf16[1,2,40]{1,0,2:T(2,128)(2,1)S(1)} %copy.224), channel_id=1, replica_groups=mesh['section'=2,'dp'=16] {'dp'}, dimensions={2}, use_global_device_ids=true | all-gather | bytes 2720 | tf_op jit(solution)/shard_map/all_gather | solution.py:121
  36.1 19.1 %all_gather.35 = bf16[1,4,640]{1,0,2:T(2,128)(2,1)S(1)} all-gather(bf16[1,4,40]{1,0,2:T(2,128)(2,1)S(1)} %copy.226), channel_id=1, replica_groups=mesh['section'=2,'dp'=16] {'dp'}, dimensions={2}, use_global_device_ids=true | all-gather | bytes 5440 | tf_op jit(solution)/shard_map/all_gather | solution.py:123
  56.3 19.9 %all_gather.33 = bf16[1,2,640]{1,0,2:T(2,128)(2,1)S(1)} all-gather(bf16[1,2,40]{1,0,2:T(2,128)(2,1)S(1)} %copy.225), channel_id=1, replica_groups=mesh['section'=2,'dp'=16] {'dp'}, dimensions={2}, use_global_device_ids=true | all-gather | bytes 2720 | tf_op jit(solution)/shard_map/all_gather | solution.py:122
  79.5 59.3 %all-reduce = bf16[5120]{0:T(1024)(128)(2,1)S(1)} all-reduce(bf16[5120]{0:T(1024)(128)(2,1)S(1)} %dynamic-update-slice.17), channel_id=1, replica_groups=mesh['section'=2,'dp'=16] {'dp'}, use_global_device_ids=true, to_apply=%add | all-reduce | flops 5120 | bytes 20480
  159.3 23.3 %all_gather.36 = bf16[1,640,640]{2,1,0:T(8,128)(2,1)S(1)} all-gather(bf16[1,40,640]{2,1,0:T(8,128)(2,1)S(1)} %copy-done.134), channel_id=1, replica_groups=mesh['section'=2,'dp'=16] {'dp'}, dimensions={1}, use_global_device_ids=true | all-gather | bytes 870400 | tf_op jit(solution)/shard_map/all_gather | solution.py:118
  196.5 20.5 %bitcast_dynamic-update-slice_fusion.2 = (bf16[4,256,640]{2,1,0:T(8,128)(2,1)S(1)}, bf16[256,640]{1,0:T(8,128)(2,1)}) fusion(bf16[4,256,640]{2,1,0:T(8,128)(2,1)S(1)} %broadcast.957.clone, s32[]{:T(128)S(6)} %min.31, pred[]{:T(512)S(6)} %and.31, f32[640]{0:T(1024)S(1)} %get-tuple-element.68, f32[256,640]{1,0:T(8,128)} %copy-done.130, ...), kind=kOutput, calls=%fused_computation.954 | convolution fusion | flops 3443425280 | bytes 15108101 | tf_op jit(solution)/shard_map/dot_general | solution.py:50
  250.1 20.3 %fusion.914 = (bf16[4,256,640]{2,1,0:T(8,128)(2,1)S(1)}, bf16[256,640]{1,0:T(8,128)(2,1)}) fusion(bf16[4,256,640]{2,1,0:T(8,128)(2,1)S(1)} %get-tuple-element.166, s32[]{:T(128)S(6)} %min.32, pred[]{:T(512)S(6)} %and.32, f32[640]{0:T(1024)S(1)} %get-tuple-element.68, f32[256,640]{1,0:T(8,128)} %copy-done.72, ...), kind=kOutput, calls=%fused_computation.952 | convolution fusion | flops 3443425280 | bytes 15435781 | tf_op jit(solution)/shard_map/dot_general | solution.py:50
  303.7 20.2 %fusion.913 = (bf16[4,256,640]{2,1,0:T(8,128)(2,1)S(1)}, bf16[256,640]{1,0:T(8,128)(2,1)}) fusion(bf16[4,256,640]{2,1,0:T(8,128)(2,1)S(1)} %get-tuple-element.172, s32[]{:T(128)S(6)} %min.33, pred[]{:T(512)S(6)} %and.33, f32[640]{0:T(1024)S(1)} %get-tuple-element.68, f32[256,640]{1,0:T(8,128)} %copy-done.73, ...), kind=kOutput, calls=%fused_computation.949 | convolution fusion | flops 3443425280 | bytes 15435781 | tf_op jit(solution)/shard_map/dot_general | solution.py:50
  356.4 20.5 %fusion.912 = (bf16[4,256,640]{2,1,0:T(8,128)(2,1)S(1)}, bf16[256,640]{1,0:T(8,128)(2,1)}) fusion(bf16[4,256,640]{2,1,0:T(8,128)(2,1)S(1)} %get-tuple-element.178, s32[]{:T(128)S(6)} %min.34, pred[]{:T(512)S(6)} %and.34, f32[640]{0:T(1024)S(1)} %get-tuple-element.68, f32[256,640]{1,0:T(8,128)} %copy-done.74, ...), kind=kOutput, calls=%fused_computation.945 | convolution fusion | flops 3443425280 | bytes 15435781 | tf_op jit(solution)/shard_map/dot_general | solution.py:50
  405.1 14.8 %fusion.110 = (f32[256,5120]{1,0:T(8,128)S(1)}, f32[256,5120]{1,0:T(8,128)S(1)}) fusion(f32[5120]{0:T(1024)} %add.1046, bf16[1,640,5120]{2,1,0:T(8,128)(2,1)} %all-gather.6.cloned.1.call-done, f32[256,640]{1,0:T(8,128)S(1)} %get-tuple-element.193, f32[256]{0:T(256)S(1)} %fusion.1063, f32[256]{0:T(256)S(1)} %broadcast_multiply_fusion.8, ...), kind=kOutput, calls=%fused_computation.102 | convolution fusion | flops 1761116160 | bytes 17722368 | tf_op jit(solution)/shard_map/dot_general | solution.py:48
  420.0 12.4 convert_reduce_fusion.4
  447.6 9.4 fusion.658
  457.0 9.4 fusion.661
  469.8 11.7 fusion.245
  508.5 14.6 %fusion.111 = (f32[256,5120]{1,0:T(8,128)S(1)}, f32[256,5120]{1,0:T(8,128)S(1)}) fusion(f32[5120]{0:T(1024)} %add.1046, bf16[1,640,5120]{2,1,0:T(8,128)(2,1)} %all-gather.6.cloned.1.call-done, f32[256,640]{1,0:T(8,128)S(1)} %get-tuple-element.201, f32[256]{0:T(256)S(1)} %fusion.1065, f32[256]{0:T(256)S(1)} %broadcast_multiply_fusion.6, ...), kind=kOutput, calls=%fused_computation.103 | convolution fusion | flops 1761116160 | bytes 17722368 | tf_op jit(solution)/shard_map/dot_general | solution.py:48
  552.3 9.4 fusion.652
  599.7 14.6 %fusion.112 = (f32[256,5120]{1,0:T(8,128)S(1)}, f32[256,5120]{1,0:T(8,128)S(1)}) fusion(f32[5120]{0:T(1024)} %add.1046, bf16[1,640,5120]{2,1,0:T(8,128)(2,1)} %all-gather.6.cloned.1.call-done, f32[256,640]{1,0:T(8,128)S(1)} %get-tuple-element.209, f32[256]{0:T(256)S(1)} %fusion.1067, f32[256]{0:T(256)S(1)} %broadcast_multiply_fusion.4, ...), kind=kOutput, calls=%fused_computation.104 | convolution fusion | flops 1761116160 | bytes 17722368 | tf_op jit(solution)/shard_map/dot_general | solution.py:48
  644.3 9.4 fusion.646
  653.6 9.4 fusion.649
  691.7 14.6 %fusion.113 = (f32[256,5120]{1,0:T(8,128)S(1)}, f32[256,5120]{1,0:T(8,128)S(1)}) fusion(f32[5120]{0:T(1024)} %add.1046, bf16[1,640,5120]{2,1,0:T(8,128)(2,1)} %all-gather.6.cloned.1.call-done, f32[256,640]{1,0:T(8,128)S(1)} %get-tuple-element.217, f32[256]{0:T(256)S(1)} %fusion.1069, f32[256]{0:T(256)S(1)} %broadcast_multiply_fusion.2, ...), kind=kOutput, calls=%fused_computation.105 | convolution fusion | flops 1761116160 | bytes 17722368 | tf_op jit(solution)/shard_map/dot_general | solution.py:48
  735.6 9.8 fusion.640
  745.4 9.7 fusion.643
  794.0 14.9 %convert_reduce_fusion = (f32[5120]{0:T(1024)S(1)}, bf16[256,5120]{1,0:T(8,128)(2,1)}) fusion(f32[256,5120]{1,0:T(8,128)S(1)} %fusion.92, bf16[256,640]{1,0:T(8,128)(2,1)S(1)} %get-tuple-element.78, bf16[1,5120,640]{2,1,0:T(8,128)(2,1)S(1)} %bitcast.1005), kind=kOutput, calls=%fused_computation.107 | convolution fusion | flops 1774709760 | bytes 14766080 | tf_op jit(solution)/shard_map/sd,fd->sf/dot_general | solution.py:63
  850.0 11.0 add_bitcast_fusion.2
  861.3 11.9 fusion.246
  873.2 11.8 fusion.247
  892.6 25.3 %add_bitcast_fusion = f32[1,5120,640]{2,1,0:T(8,128)} fusion(f32[5120,640]{1,0:T(8,128)} %fusion.248, f32[5120,640]{1,0:T(8,128)} %fusion.247, f32[5120,640]{1,0:T(8,128)} %fusion.246, f32[5120,640]{1,0:T(8,128)S(1)} %bitcast.881, bf16[256,640]{1,0:T(8,128)(2,1)S(1)} %get-tuple-element.78, f32[]{:T(128)S(6)} %convert_element_type.670, ...), kind=kOutput, calls=%fused_computation.15 | convolution fusion | flops 1792409600 | bytes 71106576 | tf_op jit(solution)/shard_map/sf,sd->fd/dot_general | solution.py:61
  948.1 25.0 %add_bitcast_fusion.1 = f32[1,640,5120]{2,1,0:T(8,128)} fusion(f32[640,5120]{1,0:T(8,128)} %fusion.1268, f32[640,5120]{1,0:T(8,128)} %fusion.1267, f32[640,5120]{1,0:T(8,128)} %fusion.1266, f32[640,5120]{1,0:T(8,128)} %fusion.1265, bf16[256,5120]{1,0:T(8,128)(2,1)S(1)} %copy-done.54, f32[]{:T(128)S(6)} %convert_element_type.670, ...), kind=kOutput, calls=%fused_computation.16 | convolution fusion | flops 1708032000 | bytes 68819984 | tf_op jit(solution)/shard_map/sd,sf->df/dot_general | solution.py:66
  995.4 20.4 %fusion.720 = bf16[1,4,256,640]{3,2,1,0:T(8,128)(2,1)} fusion(bf16[1,4,256,640]{3,2,1,0:T(8,128)(2,1)} %copy.334, s32[]{:T(128)S(6)} %min.35, f32[256,640]{1,0:T(8,128)} %copy-done.71, bf16[1,5120,640]{2,1,0:T(8,128)(2,1)} %all-gather.8.cloned.1.call-done, f32[5120]{0:T(1024)} %add.1046, bf16[1,640,5120]{2,1,0:T(8,128)(2,1)} %all-gather.6.cloned.1.call-done, ...), kind=kOutput, calls=%fused_computation.661 | convolution fusion | flops 3443425280 | bytes 15103493 | tf_op jit(solution)/shard_map/dot_general | solution.py:50
  1031.1 59.9 %all-reduce.6 = (f32[1,2,640]{2,1,0:T(2,128)S(1)}, f32[1,2,640]{2,1,0:T(2,128)S(1)}, f32[1,4,640]{2,1,0:T(4,128)S(1)}) all-reduce(f32[1,2,640]{2,1,0:T(2,128)S(1)} %fusion.1042, f32[1,2,640]{2,1,0:T(2,128)S(1)} %fusion.1046, f32[1,4,640]{2,1,0:T(4,128)S(1)} %fusion.1028), channel_id=38, replica_groups=mesh['section'=2,'dp'=16] {'dp'}, use_global_device_ids=true, to_apply=%region_107.108.clone | all-reduce | flops 5120 | bytes 40960
  1096.8 66.0 %reduce-scatter.19.cloned.1.call-done = f32[1,320,640]{2,1,0:T(8,128)} async-done(((f32[1,5120,640]{2,1,0:T(8,128)}), f32[1,320,640]{2,1,0:T(8,128)}) %reduce-scatter.19.cloned.1.call-update) | async-done | bytes 819216 | tf_op jit(solution)/shard_map/reduce_scatter | solution.py:205
  1162.8 142.7 %reduce-scatter.17.cloned.1.call-done = f32[1,40,5120]{2,1,0:T(8,128)} async-done(((f32[1,640,5120]{2,1,0:T(8,128)}), f32[1,40,5120]{2,1,0:T(8,128)}) %reduce-scatter.17.cloned.1.call-update) | async-done | bytes 819216 | tf_op jit(solution)/shard_map/reduce_scatter | solution.py:204
  (809 shorter events, 527.8 us)
Async XLA Ops:
  7.2 144.2 %copy-start.47 = (bf16[4,256,640]{2,1,0:T(8,128)(2,1)S(1)}, bf16[4,256,640]{2,1,0:T(8,128)(2,1)}, u32[]{:S(2)}) copy-start(bf16[4,256,640]{2,1,0:T(8,128)(2,1)} %param.11) | copy-start | bytes 3932164
  7.2 152.1 %copy-start.134 = (bf16[1,40,640]{2,1,0:T(8,128)(2,1)S(1)}, bf16[1,40,640]{2,1,0:T(8,128)(2,1)}, u32[]{:S(2)}) copy-start(bf16[1,40,640]{2,1,0:T(8,128)(2,1)} %param.15) | copy-start | bytes 153604
  7.2 175.4 %all-gather.4.cloned.1.call-start = ((), (), s32[]{:S(2)}) async-start(), calls=%async_computation.5 | async-start | bytes 2611200 | tf_op jit(solution)/shard_map/all_gather | solution.py:117
  7.9 188.4 %all-gather.6.cloned.1.call-start = ((), (), s32[]{:S(2)}) async-start(), calls=%async_computation.6 | async-start | bytes 6963200 | tf_op jit(solution)/shard_map/all_gather | solution.py:119
  8.7 187.7 %all-gather.8.cloned.1.call-start = ((), (), s32[]{:S(2)}) async-start(), calls=%async_computation.7 | async-start | bytes 6963200 | tf_op jit(solution)/shard_map/all_gather | solution.py:120
  9.4 1085.8 %reduce-scatter.21.cloned.1.call-start = ((), (), s32[]{:S(2)}) async-start(), calls=%async_computation.10 | async-start | bytes 2785280
  150.7 205.7 %copy-start.195 = (f32[640]{0:T(1024)}, f32[640]{0:T(1024)S(1)}, u32[]{:S(2)}) copy-start(f32[640]{0:T(1024)S(1)} %get-tuple-element.68) | copy-start | bytes 7684
  155.4 693.9 %copy-start.50 = (f32[640]{0:T(1024)}, f32[640]{0:T(1024)S(1)}, u32[]{:S(2)}) copy-start(f32[640]{0:T(1024)S(1)} %get-tuple-element.65) | copy-start | bytes 7684
  159.3 623.8 %copy-start.48 = (f32[640]{0:T(1024)}, f32[640]{0:T(1024)S(1)}, u32[]{:S(2)}) copy-start(f32[640]{0:T(1024)S(1)} %get-tuple-element.66) | copy-start | bytes 7684
  159.3 690.0 %copy-start.75 = (f32[640]{0:T(1024)}, f32[640]{0:T(1024)S(1)}, u32[]{:S(2)}) copy-start(f32[640]{0:T(1024)S(1)} %get-tuple-element.67) | copy-start | bytes 7684
  182.6 639.3 %copy-start = (bf16[1,640,640]{2,1,0:T(8,128)(2,1)}, bf16[1,640,640]{2,1,0:T(8,128)(2,1)S(1)}, u32[]{:S(2)}) copy-start(bf16[1,640,640]{2,1,0:T(8,128)(2,1)S(1)} %all_gather.36) | copy-start | bytes 2457604
  217.0 11.1 collective-permute-start
  270.4 11.2 collective-permute-start.1
  323.9 10.5 collective-permute-start.2
  376.9 9.3 collective-permute-start.3
  388.1 461.2 %copy-start.2 = (bf16[4,256,640]{2,1,0:T(8,128)(2,1)}, bf16[4,256,640]{2,1,0:T(8,128)(2,1)S(1)}, u32[]{:S(2)}) copy-start(bf16[4,256,640]{2,1,0:T(8,128)(2,1)S(1)} %get-tuple-element.111) | copy-start | bytes 3932164
  504.5 39.4 %copy-start.8 = (f32[256,640]{1,0:T(8,128)}, f32[256,640]{1,0:T(8,128)S(1)}, u32[]{:S(2)}) copy-start(f32[256,640]{1,0:T(8,128)S(1)} %get-tuple-element.201) | copy-start | bytes 1966084
  506.7 20.2 %collective-permute-start.4 = (bf16[256,640]{1,0:T(8,128)(2,1)S(1)}, bf16[256,640]{1,0:T(8,128)(2,1)S(1)}, u32[]{:S(2)}, u32[]{:S(2)}) collective-permute-start(bf16[256,640]{1,0:T(8,128)(2,1)S(1)} %get-tuple-element.107), channel_id=1, source_target_pairs={{16,0},{17,1},{18,2},{19,3},{20,4},{21,5},{22,6},{23,7},{24,8},{25... | collective-permute-start | bytes 983048 | tf_op jit(solution)/shard_map/ppermute | solution.py:13
  528.3 68.8 %copy-start.28 = (bf16[256,640]{1,0:T(8,128)(2,1)}, bf16[256,640]{1,0:T(8,128)(2,1)S(1)}, u32[]{:S(2)}) copy-start(bf16[256,640]{1,0:T(8,128)(2,1)S(1)} %get-tuple-element.90) | copy-start | bytes 983044
  598.2 19.8 %collective-permute-start.5 = (bf16[256,640]{1,0:T(8,128)(2,1)S(1)}, bf16[256,640]{1,0:T(8,128)(2,1)S(1)}, u32[]{:S(2)}, u32[]{:S(2)}) collective-permute-start(bf16[256,640]{1,0:T(8,128)(2,1)S(1)} %get-tuple-element.103), channel_id=1, source_target_pairs={{16,0},{17,1},{18,2},{19,3},{20,4},{21,5},{22,6},{23,7},{24,8},{25... | collective-permute-start | bytes 983048 | tf_op jit(solution)/shard_map/ppermute | solution.py:13
  620.0 69.1 %copy-start.30 = (bf16[256,640]{1,0:T(8,128)(2,1)}, bf16[256,640]{1,0:T(8,128)(2,1)S(1)}, u32[]{:S(2)}) copy-start(bf16[256,640]{1,0:T(8,128)(2,1)S(1)} %get-tuple-element.86) | copy-start | bytes 983044
  690.3 19.9 %collective-permute-start.6 = (bf16[256,640]{1,0:T(8,128)(2,1)S(1)}, bf16[256,640]{1,0:T(8,128)(2,1)S(1)}, u32[]{:S(2)}, u32[]{:S(2)}) collective-permute-start(bf16[256,640]{1,0:T(8,128)(2,1)S(1)} %get-tuple-element.99), channel_id=1, source_target_pairs={{16,0},{17,1},{18,2},{19,3},{20,4},{21,5},{22,6},{23,7},{24,8},{25... | collective-permute-start | bytes 983048 | tf_op jit(solution)/shard_map/ppermute | solution.py:13
  763.7 85.5 %copy-start.161 = (f32[256]{0:T(256)}, f32[256]{0:T(256)S(1)}, u32[]{:S(2)}) copy-start(f32[256]{0:T(256)S(1)} %fusion.1070) | copy-start | bytes 3076
  781.5 10.7 collective-permute-start.7
  794.0 98.7 %copy-start.52 = (bf16[256,640]{1,0:T(8,128)(2,1)}, bf16[256,640]{1,0:T(8,128)(2,1)S(1)}, u32[]{:S(2)}) copy-start(bf16[256,640]{1,0:T(8,128)(2,1)S(1)} %get-tuple-element.78) | copy-start | bytes 983044
  811.2 285.6 %reduce-scatter.25.cloned.1.call-start = ((), (), s32[]{:S(2)}) async-start(), calls=%async_computation.12 | async-start | bytes 1740800
  824.3 272.5 %reduce-scatter.23.cloned.1.call-start = ((), (), s32[]{:S(2)}) async-start(), calls=%async_computation.11 | async-start | bytes 5222400
  861.0 301.7 %reduce-scatter.19.cloned.1.call-start = ((), (), s32[]{:S(2)}) async-start(), calls=%async_computation.9 | async-start | bytes 13926400 | tf_op jit(solution)/shard_map/reduce_scatter | solution.py:205
  918.0 387.4 %reduce-scatter.17.cloned.1.call-start = ((), (), s32[]{:S(2)}) async-start(), calls=%async_computation.8 | async-start | bytes 13926400 | tf_op jit(solution)/shard_map/reduce_scatter | solution.py:204
  1029.0 63.9 %copy-start.27 = (f32[256,640]{1,0:T(8,128)S(1)}, f32[256,640]{1,0:T(8,128)}, u32[]{:S(2)}) copy-start(f32[256,640]{1,0:T(8,128)} %copy-done.26) | copy-start | bytes 1966084
  1029.0 63.9 %copy-start.53 = (bf16[256,640]{1,0:T(8,128)(2,1)S(1)}, bf16[256,640]{1,0:T(8,128)(2,1)}, u32[]{:S(2)}) copy-start(bf16[256,640]{1,0:T(8,128)(2,1)} %copy-done.52) | copy-start | bytes 983044
  1029.0 63.9 %copy-start.180 = (f32[256]{0:T(256)S(1)}, f32[256]{0:T(256)}, u32[]{:S(2)}) copy-start(f32[256]{0:T(256)} %copy-done.179) | copy-start | bytes 3076
  (200 other events, 1962.6 us)
Sparse Core Ops, SparseCore 0:
  10.2 46.3 all-gather.3
  58.9 63.8 all-gather.5
  125.0 68.5 all-gather.7
  811.3 64.3 reduce-scatter.20
  879.9 58.3 reduce-scatter.24
  943.3 76.4 reduce-scatter.22
  1024.5 138.2 reduce-scatter.18
  1168.0 137.4 reduce-scatter.16
where the time goes:
time: 1320 us; the launch traced here: 1310 us
  matrix products  676 us (51%)
  waiting for transfers between devices  227 us (17%)
  blocking collectives  206 us (16%)
  local copies, waits for them, and re-layouts  99.1 us (8%)
  other arithmetic  60.8 us (5%)
  starting transfers between devices  24.4 us (2%)
  between operations  19.1 us (1%)
    reduce_scatter x1, waiting for transfers between devices, on_device(): lax.psum_scatter(shaped[2], 'dp', scatter_dimension=1, tiled=True)  143 us
    unnamed x2, blocking collectives  119 us
    dot_general x5, matrix products, forward_pieces(): jnp.dot(act, w_down, preferred_element_type=jnp.float32)  102 us
    dot_general x5, matrix products, backward_pieces(): jnp.einsum('sf,sd->fd', act, grad_low, preferred_element_type=jnp.float32)  68.2 us
    reduce_scatter x1, waiting for transfers between devices, on_device(): lax.psum_scatter(shaped[3], 'dp', scatter_dimension=1, tiled=True)  66 us
    dot_general x5, matrix products, forward_pieces(): jnp.dot(normed_two, w_up, preferred_element_type=jnp.float32) + up_bias  63.7 us
    dot_general x5, matrix products, backward_pieces(): jnp.einsum('sd,sf->df', normed_two, d_pre, preferred_element_type=jnp.flo...  53.8 us
    dot_general x5, matrix products, backward_pieces(): jnp.einsum('sd,fd->sf', grad_low, w_down, preferred_element_type=jnp.floa...  53.6 us
  transfers between devices with their start and end apart: 16, of which 6 were waited for; matrix products, arithmetic and copies ran while one was open for 25% of the time, Pallas kernels for 0%

commit v1 on v0

v1 whole, which is shorter than its diff:
```python
import jax
import jax.numpy as jnp
from jax import lax
from jax.experimental import pallas as pl
from jax.experimental.pallas import tpu as pltpu
from jax.sharding import PartitionSpec as P

HEADS = 20
HEAD_DIM = 32
GROUP = 128 // HEAD_DIM
SCALE = HEAD_DIM ** -0.5
VMEM_LIMIT = 56 * 1024 * 1024
F32 = jnp.float32
BF16 = jnp.bfloat16


def dot(a, b, dims=((1,), (0,))):
    return lax.dot_general(a, b, (dims, ((), ())), preferred_element_type=F32)


def gelu_pair(u):
    mag = jnp.abs(u)
    t = 1.0 / (1.0 + (0.3275911 * 0.7071067811865476) * mag)
    e = jnp.exp(-0.5 * (u * u))
    poly = t * (0.5 * 0.254829592 + t * (0.5 * -0.284496736 + t * (0.5 * 1.421413741 + t * (0.5 * -1.453152027 + t * (0.5 * 1.061405429)))))
    tail = poly * e
    phi_cap = jnp.where(u < 0, tail, 1.0 - tail)
    return u * phi_cap, phi_cap + (0.3989422804014327 * u) * e


def normed(v, gain, shift):
    centered = v - jnp.mean(v, axis=-1, keepdims=True)
    spread = jnp.mean(centered * centered, axis=-1, keepdims=True)
    hat = centered * lax.rsqrt(spread + 1e-05)
    return hat * gain + shift


def norm_back(v, gain, grad):
    centered = v - jnp.mean(v, axis=-1, keepdims=True)
    spread = jnp.mean(centered * centered, axis=-1, keepdims=True)
    inv = lax.rsqrt(spread + 1e-05)
    hat = centered * inv
    g = grad * gain
    back = inv * (g - jnp.mean(g, axis=-1, keepdims=True) - hat * jnp.mean(g * hat, axis=-1, keepdims=True))
    return back, jnp.sum(grad * hat, axis=0, keepdims=True), jnp.sum(grad, axis=0, keepdims=True)


def attn_fwd_body(save, len_ref, h_ref, wqkv_ref, vec_ref, *outs):
    if save:
        m_ref, c_ref, qkv_ref, p_ref, o_ref, a_ref = outs
    else:
        m_ref, c_ref = outs
    width = h_ref.shape[2]
    seq = h_ref.shape[1]
    length = len_ref[pl.program_id(0)]
    h = h_ref[0].astype(F32)
    vec = vec_ref[...]
    a = normed(h, vec[0:1], vec[2:3]).astype(BF16)
    q_all = (dot(a, wqkv_ref[:, :width]) + vec[4:5]).astype(BF16)
    k_all = dot(a, wqkv_ref[:, width:2 * width]).astype(BF16)
    v_all = (dot(a, wqkv_ref[:, 2 * width:3 * width]) + vec[5:6]).astype(BF16)
    if save:
        a_ref[0] = a
        qkv_ref[0, :, :width] = q_all
        qkv_ref[0, :, width:2 * width] = k_all
        qkv_ref[0, :, 2 * width:] = v_all
    valid = lax.broadcasted_iota(jnp.int32, (1, seq), 1) < length
    head_of = lax.broadcasted_iota(jnp.int32, (1, 128), 1) // HEAD_DIM
    mixed = []
    for g in range(width // 128):
        at = slice(128 * g, 128 * g + 128)
        q, k, v = q_all[:, at], k_all[:, at], v_all[:, at]
        acc = None
        for j in range(GROUP):
            mine = head_of == j
            s = dot(jnp.where(mine, q, jnp.zeros_like(q)), k, ((1,), (1,)))
            s = jnp.where(valid, s * SCALE, -1e30)
            e = jnp.exp(s - jnp.max(s, axis=1, keepdims=True))
            pb = (e * (1.0 / jnp.sum(e, axis=1, keepdims=True))).astype(BF16)
            if save:
                p_ref[0, GROUP * g + j] = pb
            part = dot(pb, jnp.where(mine, v, jnp.zeros_like(v)))
            acc = part if acc is None else acc + part
        mixed.append(acc.astype(BF16))
    o = jnp.concatenate(mixed, axis=1)
    if save:
        o_ref[0] = o
    m = h + dot(o, wqkv_ref[:, 3 * width:4 * width]) + vec[6:7]
    m_ref[0] = m
    c_ref[0] = normed(m, vec[1:2], vec[3:4]).astype(BF16)


def whole(shape):
    return pl.BlockSpec(shape, lambda *_: (0,) * len(shape))


def attn_fwd(h, lengths, proj, vec, save):
    n, seq, width = h.shape
    row = lambda *tail: pl.BlockSpec((1,) + tail, lambda i, *_: (i,) + (0,) * len(tail))
    shapes = [((seq, width), F32), ((seq, width), BF16)]
    if save:
        shapes += [((seq, 3 * width), BF16), ((HEADS, seq, seq), BF16), ((seq, width), BF16), ((seq, width), BF16)]
    return pl.pallas_call(
        lambda *refs: attn_fwd_body(save, *refs),
        grid_spec=pltpu.PrefetchScalarGridSpec(
            num_scalar_prefetch=1,
            grid=(n,),
            in_specs=[row(seq, width), whole(proj.shape), whole(vec.shape)],
            out_specs=[row(*s) for s, _ in shapes],
        ),
        out_shape=[jax.ShapeDtypeStruct((n,) + s, d) for s, d in shapes],
        compiler_params=pltpu.CompilerParams(vmem_limit_bytes=VMEM_LIMIT),
        name="attention_forward",
    )(lengths, h, proj, vec)


def mlp_fwd_body(save, rows, c_ref, m_ref, wup_ref, wdown_ref, bup_ref, vec_ref, *outs):
    if save:
        y_ref, g_ref, gp_ref, acc_ref = outs
    else:
        y_ref, acc_ref = outs
    step = pl.program_id(0)

    @pl.when(step == 0)
    def _():
        acc_ref[...] = m_ref[...] + vec_ref[7:8]

    for r in range(c_ref.shape[0] // rows):
        at = slice(r * rows, r * rows + rows)
        u = dot(c_ref[at], wup_ref[...]) + bup_ref[...]
        act, slope = gelu_pair(u)
        act = act.astype(BF16)
        if save:
            g_ref[at] = act
            gp_ref[at] = slope.astype(BF16)
        acc_ref[at] += dot(act, wdown_ref[...])

    @pl.when(step == pl.num_programs(0) - 1)
    def _():
        y_ref[...] = acc_ref[...].astype(BF16)


def mlp_fwd(c, m, wup, wdown, bup, vec, save, chunk=512, rows=256):
    n, width = c.shape
    ff = wup.shape[1]
    outs = [jax.ShapeDtypeStruct((n, width), BF16)]
    specs = [whole((n, width))]
    if save:
        outs += [jax.ShapeDtypeStruct((n, ff), BF16)] * 2
        specs += [pl.BlockSpec((n, chunk), lambda i: (0, i))] * 2
    return pl.pallas_call(
        lambda *refs: mlp_fwd_body(save, rows, *refs),
        grid=(ff // chunk,),
        in_specs=[whole(c.shape), whole(m.shape), pl.BlockSpec((width, chunk), lambda i: (0, i)),
                  pl.BlockSpec((chunk, width), lambda i: (i, 0)), pl.BlockSpec((1, chunk), lambda i: (0, i)), whole(vec.shape)],
        out_specs=specs,
        out_shape=outs,
        scratch_shapes=[pltpu.VMEM((n, width), F32)],
        compiler_params=pltpu.CompilerParams(vmem_limit_bytes=VMEM_LIMIT),
        name="feed_forward",
    )(c, m, wup, wdown, bup, vec)


def mlp_bwd_body(grads, rows, dz_ref, gp_ref, wup_ref, wdown_ref, *rest):
    if grads:
        g_ref, c_ref, dc_ref, gup_ref, gdown_ref, gbu_ref, du_ref, ct_ref = rest
    else:
        dc_ref, = rest
    step = pl.program_id(0)
    n = dz_ref.shape[0]
    width = dz_ref.shape[1]

    @pl.when(step == 0)
    def _():
        dc_ref[...] = jnp.zeros_like(dc_ref)
        if grads:
            ct_ref[:width] = c_ref[...].T
            ct_ref[width:] = jnp.ones_like(ct_ref[width:])

    for r in range(n // rows):
        at = slice(r * rows, r * rows + rows)
        dg = dot(dz_ref[at], wdown_ref[...], ((1,), (1,)))
        du = (dg * gp_ref[at].astype(F32)).astype(BF16)
        if grads:
            du_ref[at] = du
        dc_ref[at] += dot(du, wup_ref[...], ((1,), (1,)))
    if grads:
        gup = dot(ct_ref[...], du_ref[...])
        gup_ref[...] = gup[:width].astype(BF16)
        gbu_ref[...] = gup[width:width + 8]
        gdown_ref[...] = dot(g_ref[...], dz_ref[...], ((0,), (0,))).astype(BF16)


def mlp_bwd(dz, gp, wup, wdown, g=None, c=None, chunk=512, rows=256):
    n, width = dz.shape
    ff = wup.shape[1]
    grads = g is not None
    col = pl.BlockSpec((n, chunk), lambda i: (0, i))
    args = [dz, gp, wup, wdown]
    in_specs = [whole(dz.shape), col, pl.BlockSpec((width, chunk), lambda i: (0, i)), pl.BlockSpec((chunk, width), lambda i: (i, 0))]
    outs = [jax.ShapeDtypeStruct((n, width), F32)]
    specs = [whole((n, width))]
    scratch = []
    if grads:
        args += [g, c]
        in_specs += [col, whole(c.shape)]
        outs += [jax.ShapeDtypeStruct((width, ff), BF16), jax.ShapeDtypeStruct((ff, width), BF16), jax.ShapeDtypeStruct((8, ff), F32)]
        specs += [pl.BlockSpec((width, chunk), lambda i: (0, i)), pl.BlockSpec((chunk, width), lambda i: (i, 0)), pl.BlockSpec((8, chunk), lambda i: (0, i))]
        scratch = [pltpu.VMEM((n, chunk), BF16), pltpu.VMEM((width + 16, n), BF16)]
    return pl.pallas_call(
        lambda *refs: mlp_bwd_body(grads, rows, *refs),
        grid=(ff // chunk,),
        in_specs=in_specs,
        out_specs=specs,
        out_shape=outs,
        scratch_shapes=scratch,
        compiler_params=pltpu.CompilerParams(vmem_limit_bytes=VMEM_LIMIT),
        name="feed_forward_back",
    )(*args)


def attn_bwd_body(dc_ref, dz_ref, m_ref, h_ref, qkv_ref, p_ref, proj_ref, vec_ref, dh_ref, dr_ref, dqkv_ref, small_ref):
    width = h_ref.shape[2]
    vec = vec_ref[...]

    @pl.when(pl.program_id(0) == 0)
    def _():
        small_ref[...] = jnp.zeros_like(small_ref)

    dz = dz_ref[0].astype(F32)
    back, g_gain1, g_shift1 = norm_back(m_ref[0], vec[1:2], dc_ref[0])
    dm = dz + back
    dr = dm.astype(BF16)
    dr_ref[0] = dr
    do_all = dot(dr, proj_ref[:, 3 * width:4 * width], ((1,), (1,))).astype(BF16)
    head_of = lax.broadcasted_iota(jnp.int32, (1, 128), 1) // HEAD_DIM
    dq_all, dk_all, dv_all = [], [], []
    for g in range(width // 128):
        at = slice(128 * g, 128 * g + 128)
        q = qkv_ref[0, :, 128 * g:128 * g + 128]
        k = qkv_ref[0, :, width + 128 * g:width + 128 * g + 128]
        v = qkv_ref[0, :, 2 * width + 128 * g:2 * width + 128 * g + 128]
        do = do_all[:, at]
        do_t, q_t = do.T, q.T
        dq = None
        dk_t, dv_t = [], []
        for j in range(GROUP):
            mine = head_of == j
            zero = jnp.zeros_like(do)
            pb = p_ref[0, GROUP * g + j]
            rows = slice(HEAD_DIM * j, HEAD_DIM * j + HEAD_DIM)
            dv_t.append(dot(do_t[rows], pb))
            dp = dot(jnp.where(mine, do, zero), v, ((1,), (1,)))
            p = pb.astype(F32)
            t = p * dp
            ds = ((t - p * jnp.sum(t, axis=1, keepdims=True)) * SCALE).astype(BF16)
            part = dot(ds, jnp.where(mine, k, zero))
            dq = part if dq is None else dq + part
            dk_t.append(dot(q_t[rows], ds))
        dq_all.append(dq.astype(BF16))
        dk_all.append(jnp.concatenate(dk_t, axis=0).astype(BF16).T)
        dv_all.append(jnp.concatenate(dv_t, axis=0).astype(BF16).T)
    dqkv = jnp.concatenate(dq_all + dk_all + dv_all, axis=1)
    dqkv_ref[0] = dqkv
    da = dot(dqkv, proj_ref[:, :3 * width], ((1,), (1,)))
    back, g_gain0, g_shift0 = norm_back(h_ref[0].astype(F32), vec[0:1], da)
    dh_ref[0] = dm + back
    total = lambda x: jnp.sum(x.astype(F32), axis=0, keepdims=True)
    small_ref[...] += jnp.concatenate(
        [g_gain0, g_gain1, g_shift0, g_shift1, total(dqkv[:, :width]), total(dqkv[:, 2 * width:]), total(dr), total(dz)], axis=0)


def attn_bwd(dc, dz, m, h, qkv, p, proj, vec):
    n, seq, width = h.shape
    row = lambda *tail: pl.BlockSpec((1,) + tail, lambda i, *_: (i,) + (0,) * len(tail))
    shapes = [((seq, width), F32), ((seq, width), BF16), ((seq, 3 * width), BF16)]
    return pl.pallas_call(
        attn_bwd_body,
        grid=(n,),
        in_specs=[row(seq, width), row(seq, width), row(seq, width), row(seq, width), row(seq, 3 * width), row(HEADS, seq, seq),
                  whole(proj.shape), whole(vec.shape)],
        out_specs=[row(*s) for s, _ in shapes] + [whole((8, width))],
        out_shape=[jax.ShapeDtypeStruct((n,) + s, d) for s, d in shapes] + [jax.ShapeDtypeStruct((8, width), F32)],
        compiler_params=pltpu.CompilerParams(vmem_limit_bytes=VMEM_LIMIT),
        name="attention_back",
    )(dc, dz, m, h, qkv, p, proj, vec)


def proj_grad_body(a_ref, dqkv_ref, o_ref, dr_ref, table_ref, out_ref, at_ref):
    step = pl.program_id(0)
    width = a_ref.shape[1]

    @pl.when(step == 0)
    def _():
        at_ref[...] = a_ref[...].T
        out_ref[:, 3 * width:4 * width] = dot(o_ref[...], dr_ref[...], ((0,), (0,))).astype(BF16)
        out_ref[:, 4 * width:] = table_ref[...].astype(BF16)

    out_ref[:, pl.ds(pl.multiple_of(step * width, 128), width)] = dot(at_ref[...], dqkv_ref[...]).astype(BF16)


def proj_grad(a, dqkv, o, dr, table):
    n, width = a.shape
    shape = (width, 4 * width + table.shape[1])
    return pl.pallas_call(
        proj_grad_body,
        grid=(3,),
        in_specs=[whole(a.shape), pl.BlockSpec((n, width), lambda i: (0, i)), whole(o.shape), whole(dr.shape), whole(table.shape)],
        out_specs=whole(shape),
        out_shape=jax.ShapeDtypeStruct(shape, BF16),
        scratch_shapes=[pltpu.VMEM((width, n), BF16)],
        compiler_params=pltpu.CompilerParams(vmem_limit_bytes=VMEM_LIMIT),
        name="projection_gradients",
    )(a, dqkv, o, dr, table)


def places(count):
    return count // 4, 2, 2


def hop(value, kind, step=1):
    zs, ys, cores = places(lax.axis_size("dp"))
    pairs = []
    for z in range(zs):
        for y in range(ys):
            for c in range(cores):
                to = {"core": (z, y, c ^ 1), "y": (z, y ^ 1, c), "z": ((z + step) % zs, y, c)}[kind]
                pairs.append(((z * ys + y) * cores + c, (to[0] * ys + to[1]) * cores + to[2]))
    return lax.ppermute(value, "dp", pairs)


def pick(value, index, axis):
    return lax.dynamic_index_in_dim(value, index, axis, keepdims=False)


def scatter_sum(grad, rows):
    count = lax.axis_size("dp")
    zs, ys, cores = places(count)
    me = lax.axis_index("dp")
    c, y, z = me % cores, (me // cores) % ys, me // (cores * ys)
    columns = grad.shape[1]
    parts = grad.reshape(zs, ys, cores, rows, columns)
    got = hop(pick(parts, 1 - c, 2), "core")
    parts = (pick(parts, c, 2).astype(F32) + got.astype(F32)).astype(BF16)
    got = hop(pick(parts, 1 - y, 1), "y")
    parts = (pick(parts, y, 1).astype(F32) + got.astype(F32)).astype(BF16)
    total = pick(parts, z, 0).astype(F32)
    for step in range(1, zs):
        total = total + hop(pick(parts, (z + step) % zs, 0), "z", step).astype(F32)
    return total


def on_device(tokens, lengths, cotangent, w_qkv, w_out, w_up, w_down, norm_gain, norm_bias, bias_vec, up_bias):
    section = lax.axis_index("section")
    windows, seq, width = tokens.shape
    n = windows * seq
    shard = w_qkv.shape[1]
    per_row = up_bias.shape[1] // shard
    ff = w_up.shape[2]
    table = jnp.concatenate([norm_gain[0], norm_bias[0], bias_vec[0]], axis=0).T
    table = jnp.concatenate([table, up_bias.reshape(shard, per_row)], axis=1)
    used = table.shape[1]
    table = jnp.pad(table, ((0, 0), (0, 128 - used)))
    packed = jnp.concatenate([w_qkv[0], w_out[0], table], axis=1)
    proj = lax.all_gather(packed, "dp", axis=0, tiled=True)
    wup = lax.all_gather(w_up[0], "dp", axis=0, tiled=True)
    wdown = lax.all_gather(w_down[0], "dp", axis=0, tiled=True)
    small = proj[:, 4 * width:4 * width + used]
    vec = small[:, :8].T.astype(F32)
    bup = small[:, 8:].reshape(1, ff).astype(F32)

    m, c = attn_fwd(tokens, lengths, proj, vec, False)
    first, = mlp_fwd(c.reshape(n, width), m.reshape(n, width), wup, wdown, bup, vec, False)
    arrived = lax.ppermute(first.reshape(tokens.shape), "section", [(0, 1)])
    h = jnp.where(section == 0, tokens, arrived)

    m, c, qkv, p, o, a = attn_fwd(h, lengths, proj, vec, True)
    c = c.reshape(n, width)
    y, g, gp = mlp_fwd(c, m.reshape(n, width), wup, wdown, bup, vec, True)

    dc, = mlp_bwd(cotangent.reshape(n, width), gp, wup, wdown)
    dh = attn_bwd(dc.reshape(windows, seq, width), cotangent, m, h, qkv, p, proj, vec)[0]
    arrived = lax.ppermute(dh.astype(BF16), "section", [(1, 0)])
    dz = jnp.where(section == 1, cotangent, arrived)

    dc, g_up, g_down, g_bup = mlp_bwd(dz.reshape(n, width), gp, wup, wdown, g, c)
    sum_down = scatter_sum(g_down, w_down.shape[1])
    sum_up = scatter_sum(g_up, shard)
    dh, dr, dqkv, smalls = attn_bwd(dc.reshape(windows, seq, width), dz, m, h, qkv, p, proj, vec)
    g_table = jnp.concatenate([smalls.T, g_bup[0].reshape(width, per_row)], axis=1)
    g_table = jnp.pad(g_table, ((0, 0), (0, 128 - used)))
    g_proj = proj_grad(a.reshape(n, width), dqkv.reshape(n, 3 * width), o.reshape(n, width), dr.reshape(n, width), g_table)
    sum_proj = scatter_sum(g_proj, shard)
    vectors = sum_proj[:, 4 * width:4 * width + 8].T
    return (
        y.reshape((1,) + tokens.shape),
        dh[None],
        sum_proj[None, :, :3 * width],
        sum_proj[None, :, 3 * width:4 * width],
        sum_up[None],
        sum_down[None],
        vectors[None, 0:2],
        vectors[None, 2:4],
        vectors[None, 4:8],
        sum_proj[:, 4 * width + 8:4 * width + used].reshape(1, -1),
    )


def solution(mesh):
    sharded = [P("section", "dp", None)] * 4 + [P("section", None, "dp")] * 3 + [P("section", "dp")]
    windows = P("dp", None, None)
    out = P("section", "dp", None, None)
    return jax.shard_map(
        on_device, mesh=mesh, in_specs=(windows, P("dp"), windows, *sharded), out_specs=(out, out, *sharded), check_vma=False
    )
```

time: 1320 us -> 704 us (0.53)
  matrix products: 676 us -> 0 us
  Pallas kernels: 0 us -> 282 us
  blocking collectives: 206 us -> 0 us
  waiting for transfers between devices: 227 us -> 324 us
  local copies, waits for them, and re-layouts: 99.1 us -> 30.5 us
  other arithmetic: 60.8 us -> 24.7 us
    dot_general x100 -> x0, matrix products: 623 us -> none  [the longest x5 102 us: forward_pieces(): jnp.dot(act, w_down, preferred_element_type=jnp.float32)]
    pallas_call x0 -> x9, Pallas kernels: none -> 282 us  [the longest x2 76.5 us: mlp_fwd(): pl.pallas_call(lambda *refs: mlp_fwd_body(save, rows, *refs), grid=(ff //...]
    reduce_scatter x2 -> x0, waiting for transfers between devices: 209 us -> none  [the longest x1 143 us: on_device(): lax.psum_scatter(shaped[2], 'dp', scatter_dimension=1, tiled=True)]
    ppermute x8 -> x17, waiting for transfers between devices: 16.1 us -> 176 us  [the longest x15 117 us: hop(): return lax.ppermute(value, 'dp', pairs)]
    all_gather x3, waiting for transfers between devices: 0.04 us -> 146 us  [the longest x1 64.3 us: on_device(): wdown = lax.all_gather(w_down[0], 'dp', axis=0, tiled=True)]
    unnamed x2 -> x0, blocking collectives: 119 us -> none
    all_gather x4 -> x0, blocking collectives: 87 us -> none  [the longest x1 24.7 us: on_device(): lax.all_gather(shards[4], 'dp', axis=2, tiled=True)]
    slice x43 -> x5, local copies, waits for them, and re-layouts: 62.2 us -> 2.39 us  [the longest x1 0.97 us: on_device(): g_bup[0].reshape(width, per_row)]
  transfers between devices with their start and end apart: 16 -> 20, of which waited for: 6 -> 12; matrix products, arithmetic and copies ran while one was open for 25% -> 5% of each run, Pallas kernels for 0% -> 4%
where the time goes in v1:
time: 704 us; the launch traced here: 697 us
  waiting for transfers between devices  324 us (46%)
  Pallas kernels  282 us (40%)
  local copies, waits for them, and re-layouts  30.5 us (4%)
  other arithmetic  24.7 us (4%)
  starting transfers between devices  22.2 us (3%)
  between operations  14.2 us (2%)
    ppermute x15, waiting for transfers between devices, hop(): return lax.ppermute(value, 'dp', pairs)  117 us
    pallas_call x2, Pallas kernels, mlp_fwd(): pl.pallas_call(lambda *refs: mlp_fwd_body(save, rows, *refs), grid=(ff //...  76.5 us
    pallas_call x2, Pallas kernels, attn_bwd(): pl.pallas_call(attn_bwd_body, grid=(n,), in_specs=[row(seq, width), row(s...  70.7 us
    pallas_call x2, Pallas kernels, mlp_bwd(): pl.pallas_call(lambda *refs: mlp_bwd_body(grads, rows, *refs), grid=(ff /...  67.3 us
    all_gather x1, waiting for transfers between devices, on_device(): wdown = lax.all_gather(w_down[0], 'dp', axis=0, tiled=True)  64.3 us
    pallas_call x2, Pallas kernels, attn_fwd(): pl.pallas_call(lambda *refs: attn_fwd_body(save, *refs), grid_spec=pltpu....  58 us
    all_gather x1, waiting for transfers between devices, on_device(): proj = lax.all_gather(packed, 'dp', axis=0, tiled=True)  47.9 us
    all_gather x1, waiting for transfers between devices, on_device(): wup = lax.all_gather(w_up[0], 'dp', axis=0, tiled=True)  33.5 us
  transfers between devices with their start and end apart: 20, of which 12 were waited for; matrix products, arithmetic and copies ran while one was open for 5% of the time, Pallas kernels for 4%

profile of v1, /device:TPU:0, one launch (start us, length us, event | category | flops | bytes accessed | tf_op | source)
XLA Modules:
  0.0 697.2 jit_solution(10592727352283688246)
XLA Ops:
  12.1 47.9 %all-gather.6.cloned.1.call-done.refs_2_.proj_ref = bf16[640,2688]{1,0:T(8,128)(2,1)} async-done(((bf16[40,2688]{1,0:T(8,128)(2,1)}), bf16[640,2688]{1,0:T(8,128)(2,1)}) %all-gather.6.cloned.1.call-update) | async-done | bytes 3440656 | tf_op jit(solution)/shard_map/all_gather | solution.py:365
  62.6 28.5 %attention_forward.2 = (f32[4,256,640]{2,1,0:T(8,128)}, bf16[4,256,640]{2,1,0:T(8,128)(2,1)}) custom-call(s32[4]{0:T(128)} %refs_0_.3, bf16[4,256,640]{2,1,0:T(8,128)(2,1)} %refs_1_.1, bf16[640,2688]{1,0:T(8,128)(2,1)} %all-gather.6.cloned.1.call-done.refs_2_.proj_ref, f32[8,640]{1,0:T(8,128)} %convert_bitcast_fusion.refs_3_.refs_5_.vec_ref), custom_call_target="tpu_custom_call" | custom-call | tf_op jit(solution)/shard_map/attention_forward/pallas_call | solution.py:103
  91.1 33.5 %all-gather.8.cloned.1.call-done = bf16[1,640,5120]{2,1,0:T(8,128)(2,1)} async-done(((bf16[1,40,5120]{2,1,0:T(8,128)(2,1)}), bf16[1,640,5120]{2,1,0:T(8,128)(2,1)}) %all-gather.8.cloned.1.call-update) | async-done | bytes 6553616 | tf_op jit(solution)/shard_map/all_gather | solution.py:366
  124.7 64.3 %all-gather.10.cloned.1.call-done = bf16[1,5120,640]{2,1,0:T(8,128)(2,1)} async-done(((bf16[1,320,640]{2,1,0:T(8,128)(2,1)}), bf16[1,5120,640]{2,1,0:T(8,128)(2,1)}) %all-gather.10.cloned.1.call-update) | async-done | bytes 6553616 | tf_op jit(solution)/shard_map/all_gather | solution.py:367
  188.9 36.9 %feed_forward.2 = bf16[1024,640]{1,0:T(8,128)(2,1)} custom-call(bf16[1024,640]{1,0:T(8,128)(2,1)} %bitcast.131, f32[1024,640]{1,0:T(8,128)} %bitcast.129, bf16[640,5120]{1,0:T(8,128)(2,1)} %bitcast.110, bf16[5120,640]{1,0:T(8,128)(2,1)} %bitcast.114, f32[1,5120]{1,0:T(1,128)} %reshape.129.refs_4_, f32[8,640]{1,0:T(8,128)} %convert_bitcast_fusion.refs_3_.refs_5_.vec_ref), custom_call_target="tpu_custom_call" | custom-call | tf_op jit(solution)/shard_map/feed_forward/pallas_call | solution.py:151
  225.8 3.7 collective-permute-start
  229.6 28.4 %collective-permute-done = bf16[4,256,640]{2,1,0:T(8,128)(2,1)S(1)} collective-permute-done((bf16[4,256,640]{2,1,0:T(8,128)(2,1)}, bf16[4,256,640]{2,1,0:T(8,128)(2,1)S(1)}, u32[]{:S(2)}, u32[]{:S(2)}) %collective-permute-start) | collective-permute-done | bytes 1310752 | tf_op jit(solution)/shard_map/ppermute | solution.py:374
  259.1 29.6 %attention_forward.3 = (f32[4,256,640]{2,1,0:T(8,128)}, bf16[4,256,640]{2,1,0:T(8,128)(2,1)}, bf16[4,256,1920]{2,1,0:T(8,128)(2,1)}, bf16[4,20,256,256]{3,2,1,0:...) custom-call(s32[4]{0:T(128)} %refs_0_.3, ...), custom_call_target="tpu_custom_call" | custom-call | tf_op jit(solution)/shard_map/attention_forward/pallas_call | solution.py:103
  288.7 39.6 %feed_forward.3 = (bf16[1024,640]{1,0:T(8,128)(2,1)}, bf16[1024,5120]{1,0:T(8,128)(2,1)}, bf16[1024,5120]{1,0:T(8,128)(2,1)}) custom-call(bf16[1024,640]{1,0:T(8,128)(2,1)} %bitcast.125, f32[1024,640]{1,0:T(8,128)} %bitcast.118, bf16[640,5120]{1,0:T(8,128)(2,1)} %bitcast.111, bf16[5120,640]{1,0:T(8,128)(2,1)} %bitcast.115, f32[1,5120]{1,0:T(1,128)} %reshape.129.refs_4_, ...), custom_call_target="tpu_custom_call" | custom-call | tf_op jit(solution)/shard_map/feed_forward/pallas_call | solution.py:151
  328.3 25.7 %feed_forward_back.2 = f32[1024,640]{1,0:T(8,128)} custom-call(bf16[1024,640]{1,0:T(8,128)(2,1)} %bitcast.121, bf16[1024,5120]{1,0:T(8,128)(2,1)} %get-tuple-element.35.refs_1_, bf16[640,5120]{1,0:T(8,128)(2,1)} %bitcast.112, bf16[5120,640]{1,0:T(8,128)(2,1)} %bitcast.116), custom_call_target="tpu_custom_call" | custom-call | tf_op jit(solution)/shard_map/feed_forward_back/pallas_call | solution.py:210
  354.0 35.6 %attention_back.2 = (f32[4,256,640]{2,1,0:T(8,128)}, bf16[4,256,640]{2,1,0:T(8,128)(2,1)}, bf16[4,256,1920]{2,1,0:T(8,128)(2,1)}, f32[8,640]{1,0:T(8,128)}) custom-call(f32[4,256,640]{2,1,0:T(8,128)} %bitcast.122, bf16[4,256,640]{2,1,0:T(8,128)(2,1)} %dz_ref.1, f32[4,256,640]{2,1,0:T(8,128)} %get-tuple-element.33.m_ref, ...), custom_call_target="tpu_custom_call" | custom-call | tf_op jit(solution)/shard_map/attention_back/pallas_call | solution.py:277
  389.6 3.0 convert_element_type.138
  394.0 30.9 %collective-permute-done.1 = bf16[4,256,640]{2,1,0:T(8,128)(2,1)S(1)} collective-permute-done((bf16[4,256,640]{2,1,0:T(8,128)(2,1)}, bf16[4,256,640]{2,1,0:T(8,128)(2,1)S(1)}, u32[]{:S(2)}, u32[]{:S(2)}) %collective-permute-start.1) | collective-permute-done | bytes 1310752 | tf_op jit(solution)/shard_map/ppermute | solution.py:383
  426.1 41.6 %feed_forward_back.3 = (f32[1024,640]{1,0:T(8,128)}, bf16[640,5120]{1,0:T(8,128)(2,1)}, bf16[5120,640]{1,0:T(8,128)(2,1)}, f32[8,5120]{1,0:T(8,128)}) custom-call(bf16[1024,640]{1,0:T(8,128)(2,1)} %bitcast.120, bf16[1024,5120]{1,0:T(8,128)(2,1)} %get-tuple-element.35.refs_1_, bf16[640,5120]{1,0:T(8,128)(2,1)} %bitcast.113, bf16[5120,640]{1,0:T(8,128)(2,1)} %bitcast.117, ...), custom_call_target="tpu_custom_call" | custom-call | tf_op jit(solution)/shard_map/feed_forward_back/pallas_call | solution.py:210
  468.8 35.1 %attention_back.3 = (f32[4,256,640]{2,1,0:T(8,128)}, bf16[4,256,640]{2,1,0:T(8,128)(2,1)}, bf16[4,256,1920]{2,1,0:T(8,128)(2,1)}, f32[8,640]{1,0:T(8,128)}) custom-call(f32[4,256,640]{2,1,0:T(8,128)} %bitcast.128, bf16[4,256,640]{2,1,0:T(8,128)(2,1)} %broadcast_select_fusion.dz_ref, f32[4,256,640]{2,1,0:T(8,128)} %get-tuple-element.33.m_ref, ...), custom_call_target="tpu_custom_call" | custom-call | tf_op jit(solution)/shard_map/attention_back/pallas_call | solution.py:277
  505.7 9.5 %projection_gradients.1 = bf16[640,2688]{1,0:T(8,128)(2,1)} custom-call(bf16[1024,640]{1,0:T(8,128)(2,1)} %bitcast.134, bf16[1024,1920]{1,0:T(8,128)(2,1)} %bitcast.127, bf16[1024,640]{1,0:T(8,128)(2,1)} %bitcast.133, bf16[1024,640]{1,0:T(8,128)(2,1)} %bitcast.135, f32[640,128]{1,0:T(8,128)} %select_maximum_fusion.table_ref), custom_call_target="tpu_custom_call" | custom-call | tf_op jit(solution)/shard_map/projection_gradients/pallas_call | solution.py:305
  515.2 2.2 constant_dynamic-slice_fusion.5
  518.8 5.2 constant_dynamic-slice_fusion.3
  524.0 2.0 copy.113
  530.4 20.5 %collective-permute-done.3 = bf16[4,40,2688]{2,1,0:T(8,128)(2,1)S(1)} collective-permute-done((bf16[4,40,2688]{2,1,0:T(8,128)(2,1)S(1)}, bf16[4,40,2688]{2,1,0:T(8,128)(2,1)S(1)}, u32[]{:S(2)}, u32[]{:S(2)}) %collective-permute-start.3) | collective-permute-done | bytes 860192 | tf_op jit(solution)/shard_map/ppermute | solution.py:329
  555.2 5.3 constant_dynamic-slice_fusion.1
  560.5 2.0 copy.112
  562.5 9.8 %collective-permute-done.5 = bf16[40,2688]{1,0:T(8,128)(2,1)S(1)} collective-permute-done((bf16[40,2688]{1,0:T(8,128)(2,1)S(1)}, bf16[40,2688]{1,0:T(8,128)(2,1)S(1)}, u32[]{:S(2)}, u32[]{:S(2)}) %collective-permute-start.5) | collective-permute-done | bytes 215072 | tf_op jit(solution)/shard_map/ppermute | solution.py:329
  572.5 3.2 fusion.1
  583.4 3.7 fusion
  588.9 27.1 %collective-permute-done.8 = bf16[4,40,5120]{2,1,0:T(8,128)(2,1)} collective-permute-done((bf16[4,40,5120]{2,1,0:T(8,128)(2,1)}, bf16[4,40,5120]{2,1,0:T(8,128)(2,1)}, u32[]{:S(2)}, u32[]{:S(2)}) %collective-permute-start.8) | collective-permute-done | bytes 1638432 | tf_op jit(solution)/shard_map/ppermute | solution.py:329
  616.0 1.9 fusion.4
  618.1 2.0 collective-permute-start.10
  622.0 26.2 %collective-permute-done.13 = bf16[4,320,640]{2,1,0:T(8,128)(2,1)S(1)} collective-permute-done((bf16[4,320,640]{2,1,0:T(8,128)(2,1)S(1)}, bf16[4,320,640]{2,1,0:T(8,128)(2,1)S(1)}, u32[]{:S(2)}, u32[]{:S(2)}) %collective-permute-start.13) | collective-permute-done | bytes 1638432 | tf_op jit(solution)/shard_map/ppermute | solution.py:329
  648.9 3.8 collective-permute-start.15
  656.9 6.3 collective-permute-done.16
  663.2 26.1 %collective-permute-done.15 = bf16[320,640]{1,0:T(8,128)(2,1)S(1)} collective-permute-done((bf16[320,640]{1,0:T(8,128)(2,1)S(1)}, bf16[320,640]{1,0:T(8,128)(2,1)S(1)}, u32[]{:S(2)}, u32[]{:S(2)}) %collective-permute-start.15) | collective-permute-done | bytes 409632 | tf_op jit(solution)/shard_map/ppermute | solution.py:329
  (78 shorter events, 42.0 us)
Async XLA Ops:
  7.2 52.8 %all-gather.6.cloned.1.call-start = ((), (), s32[]{:S(2)}) async-start(), calls=%async_computation | async-start | bytes 3655680 | tf_op jit(solution)/shard_map/all_gather | solution.py:365
  10.6 114.1 %all-gather.8.cloned.1.call-start = ((), (), s32[]{:S(2)}) async-start(), calls=%async_computation.1 | async-start | bytes 6963200 | tf_op jit(solution)/shard_map/all_gather | solution.py:366
  11.3 177.6 %all-gather.10.cloned.1.call-start = ((), (), s32[]{:S(2)}) async-start(), calls=%async_computation.2 | async-start | bytes 6963200 | tf_op jit(solution)/shard_map/all_gather | solution.py:367
  188.9 69.0 %copy-start.2 = (bf16[4,256,640]{2,1,0:T(8,128)(2,1)S(1)}, bf16[4,256,640]{2,1,0:T(8,128)(2,1)}, u32[]{:S(2)}) copy-start(bf16[4,256,640]{2,1,0:T(8,128)(2,1)} %refs_1_.1) | copy-start | bytes 3932164
  225.8 32.1 %collective-permute-start = (bf16[4,256,640]{2,1,0:T(8,128)(2,1)}, bf16[4,256,640]{2,1,0:T(8,128)(2,1)S(1)}, u32[]{:S(2)}, u32[]{:S(2)}) collective-permute-start(bf16[4,256,640]{2,1,0:T(8,128)(2,1)} %bitcast.130), channel_id=1, source_target_pairs={{0,16},{1,17},{2,18},{3,19},{4,20},{5,21},{6,22},{7,23},{8,24},{9,... | collective-permute-start | bytes 3932168 | tf_op jit(solution)/shard_map/ppermute | solution.py:374
  389.6 35.3 %copy-start.1 = (bf16[4,256,640]{2,1,0:T(8,128)(2,1)S(1)}, bf16[4,256,640]{2,1,0:T(8,128)(2,1)}, u32[]{:S(2)}) copy-start(bf16[4,256,640]{2,1,0:T(8,128)(2,1)} %dz_ref.1) | copy-start | bytes 3932164
  392.7 32.2 %collective-permute-start.1 = (bf16[4,256,640]{2,1,0:T(8,128)(2,1)}, bf16[4,256,640]{2,1,0:T(8,128)(2,1)S(1)}, u32[]{:S(2)}, u32[]{:S(2)}) collective-permute-start(bf16[4,256,640]{2,1,0:T(8,128)(2,1)} %convert_element_type.138), channel_id=1, source_target_pairs={{16,0},{17,1},{18,2},{19,3},{20,4},{21,5},{22,6},{23,7},{24,8},{25... | collective-permute-start | bytes 3932168 | tf_op jit(solution)/shard_map/ppermute | solution.py:383
  518.8 7.7 %collective-permute-start.2 = (bf16[4,2,40,2688]{3,2,0,1:T(8,128)(2,1)}, bf16[4,2,40,2688]{3,2,0,1:T(8,128)(2,1)S(1)}, u32[]{:S(2)}, u32[]{:S(2)}) collective-permute-start(bf16[4,2,40,2688]{3,2,0,1:T(8,128)(2,1)} %bitcast.109), channel_id=1, source_target_pairs={{0,1},{1,0},{2,3},{3,2},{4,5},{5,4},{6,7},{7,6},{8,9},{9,8},{10,11... | collective-permute-start | bytes 5160968 | tf_op jit(solution)/shard_map/ppermute | solution.py:329
  526.1 46.4 %collective-permute-start.7 = (bf16[4,2,40,5120]{3,2,0,1:T(8,128)(2,1)}, bf16[4,2,40,5120]{3,2,0,1:T(8,128)(2,1)}, u32[]{:S(2)}, u32[]{:S(2)}) collective-permute-start(bf16[4,2,40,5120]{3,2,0,1:T(8,128)(2,1)} %bitcast.108), channel_id=1, source_target_pairs={{0,1},{1,0},{2,3},{3,2},{4,5},{5,4},{6,7},{7,6},{8,9},{9,8},{10,11... | collective-permute-start | bytes 9830408 | tf_op jit(solution)/shard_map/ppermute | solution.py:329
  526.6 1.3 copy-start.4
  529.8 21.1 %collective-permute-start.3 = (bf16[4,40,2688]{2,1,0:T(8,128)(2,1)S(1)}, bf16[4,40,2688]{2,1,0:T(8,128)(2,1)S(1)}, u32[]{:S(2)}, u32[]{:S(2)}) collective-permute-start(bf16[4,40,2688]{2,1,0:T(8,128)(2,1)S(1)} %dynamic-slice_bitcast_fusion.2), channel_id=1, source_target_pairs={{0,2},{1,3},{2,0},{3,1},{4,6},{5,7},{6,4},{7,5},{8,10},{9,11},{10,... | collective-permute-start | bytes 2580488 | tf_op jit(solution)/shard_map/ppermute | solution.py:329
  551.2 11.3 %collective-permute-start.6 = (bf16[40,2688]{1,0:T(8,128)(2,1)S(1)}, bf16[40,2688]{1,0:T(8,128)(2,1)S(1)}, u32[]{:S(2)}, u32[]{:S(2)}) collective-permute-start(bf16[40,2688]{1,0:T(8,128)(2,1)S(1)} %get-tuple-element.105), channel_id=1, source_target_pairs={{0,12},{1,13},{2,14},{3,15},{4,0},{5,1},{6,2},{7,3},{8,4},{9,5},{1... | collective-permute-start | bytes 645128 | tf_op jit(solution)/shard_map/ppermute | solution.py:329
  553.1 19.1 %collective-permute-start.5 = (bf16[40,2688]{1,0:T(8,128)(2,1)S(1)}, bf16[40,2688]{1,0:T(8,128)(2,1)S(1)}, u32[]{:S(2)}, u32[]{:S(2)}) collective-permute-start(bf16[40,2688]{1,0:T(8,128)(2,1)S(1)} %get-tuple-element.106), channel_id=1, source_target_pairs={{0,8},{1,9},{2,10},{3,11},{4,12},{5,13},{6,14},{7,15},{8,0},{9,1},... | collective-permute-start | bytes 645128 | tf_op jit(solution)/shard_map/ppermute | solution.py:329
  554.1 18.2 %collective-permute-start.4 = (bf16[40,2688]{1,0:T(8,128)(2,1)S(1)}, bf16[40,2688]{1,0:T(8,128)(2,1)S(1)}, u32[]{:S(2)}, u32[]{:S(2)}) collective-permute-start(bf16[40,2688]{1,0:T(8,128)(2,1)S(1)} %get-tuple-element.104), channel_id=1, source_target_pairs={{0,4},{1,5},{2,6},{3,7},{4,8},{5,9},{6,10},{7,11},{8,12},{9,13},{1... | collective-permute-start | bytes 645128 | tf_op jit(solution)/shard_map/ppermute | solution.py:329
  560.5 12.0 %copy-start = (bf16[4,2,1,40,5120]{4,3,2,1,0:T(8,128)(2,1)S(1)}, bf16[4,2,1,40,5120]{4,3,2,1,0:T(8,128)(2,1)}, u32[]{:S(2)}) copy-start(bf16[4,2,1,40,5120]{4,3,2,1,0:T(8,128)(2,1)} %get-tuple-element.92) | copy-start | bytes 9830404
  562.5 21.0 %collective-permute-start.12 = (bf16[4,2,320,640]{3,2,0,1:T(8,128)(2,1)}, bf16[4,2,320,640]{3,2,0,1:T(8,128)(2,1)}, u32[]{:S(2)}, u32[]{:S(2)}) collective-permute-start(bf16[4,2,320,640]{3,2,0,1:T(8,128)(2,1)} %bitcast.107), channel_id=1, source_target_pairs={{0,1},{1,0},{2,3},{3,2},{4,5},{5,4},{6,7},{7,6},{8,9},{9,8},{10,11... | collective-permute-start | bytes 9830408 | tf_op jit(solution)/shard_map/ppermute | solution.py:329
  572.4 3.3 copy-start.3
  576.9 39.1 %collective-permute-start.8 = (bf16[4,40,5120]{2,1,0:T(8,128)(2,1)}, bf16[4,40,5120]{2,1,0:T(8,128)(2,1)}, u32[]{:S(2)}, u32[]{:S(2)}) collective-permute-start(bf16[4,40,5120]{2,1,0:T(8,128)(2,1)} %dynamic-slice_bitcast_fusion.1), channel_id=1, source_target_pairs={{0,2},{1,3},{2,0},{3,1},{4,6},{5,7},{6,4},{7,5},{8,10},{9,11},{10,... | collective-permute-start | bytes 4915208 | tf_op jit(solution)/shard_map/ppermute | solution.py:329
  587.3 60.9 %collective-permute-start.13 = (bf16[4,320,640]{2,1,0:T(8,128)(2,1)S(1)}, bf16[4,320,640]{2,1,0:T(8,128)(2,1)S(1)}, u32[]{:S(2)}, u32[]{:S(2)}) collective-permute-start(bf16[4,320,640]{2,1,0:T(8,128)(2,1)S(1)} %dynamic-slice_bitcast_fusion), channel_id=1, source_target_pairs={{0,2},{1,3},{2,0},{3,1},{4,6},{5,7},{6,4},{7,5},{8,10},{9,11},{10,... | collective-permute-start | bytes 4915208 | tf_op jit(solution)/shard_map/ppermute | solution.py:329
  618.0 34.6 %collective-permute-start.11 = (bf16[40,5120]{1,0:T(8,128)(2,1)S(1)}, bf16[40,5120]{1,0:T(8,128)(2,1)S(1)}, u32[]{:S(2)}, u32[]{:S(2)}) collective-permute-start(bf16[40,5120]{1,0:T(8,128)(2,1)S(1)} %get-tuple-element.102), channel_id=1, source_target_pairs={{0,12},{1,13},{2,14},{3,15},{4,0},{5,1},{6,2},{7,3},{8,4},{9,5},{1... | collective-permute-start | bytes 1228808 | tf_op jit(solution)/shard_map/ppermute | solution.py:329
  618.1 37.7 %collective-permute-start.10 = (bf16[40,5120]{1,0:T(8,128)(2,1)S(1)}, bf16[40,5120]{1,0:T(8,128)(2,1)S(1)}, u32[]{:S(2)}, u32[]{:S(2)}) collective-permute-start(bf16[40,5120]{1,0:T(8,128)(2,1)S(1)} %get-tuple-element.103), channel_id=1, source_target_pairs={{0,8},{1,9},{2,10},{3,11},{4,12},{5,13},{6,14},{7,15},{8,0},{9,1},... | collective-permute-start | bytes 1228808 | tf_op jit(solution)/shard_map/ppermute | solution.py:329
  620.1 35.7 %collective-permute-start.9 = (bf16[40,5120]{1,0:T(8,128)(2,1)S(1)}, bf16[40,5120]{1,0:T(8,128)(2,1)S(1)}, u32[]{:S(2)}, u32[]{:S(2)}) collective-permute-start(bf16[40,5120]{1,0:T(8,128)(2,1)S(1)} %get-tuple-element.101), channel_id=1, source_target_pairs={{0,4},{1,5},{2,6},{3,7},{4,8},{5,9},{6,10},{7,11},{8,12},{9,13},{1... | collective-permute-start | bytes 1228808 | tf_op jit(solution)/shard_map/ppermute | solution.py:329
  648.8 14.5 %collective-permute-start.16 = (bf16[320,640]{1,0:T(8,128)(2,1)S(1)}, bf16[320,640]{1,0:T(8,128)(2,1)S(1)}, u32[]{:S(2)}, u32[]{:S(2)}) collective-permute-start(bf16[320,640]{1,0:T(8,128)(2,1)S(1)} %get-tuple-element.99), channel_id=1, source_target_pairs={{0,12},{1,13},{2,14},{3,15},{4,0},{5,1},{6,2},{7,3},{8,4},{9,5},{1... | collective-permute-start | bytes 1228808 | tf_op jit(solution)/shard_map/ppermute | solution.py:329
  648.9 40.5 %collective-permute-start.15 = (bf16[320,640]{1,0:T(8,128)(2,1)S(1)}, bf16[320,640]{1,0:T(8,128)(2,1)S(1)}, u32[]{:S(2)}, u32[]{:S(2)}) collective-permute-start(bf16[320,640]{1,0:T(8,128)(2,1)S(1)} %get-tuple-element.100), channel_id=1, source_target_pairs={{0,8},{1,9},{2,10},{3,11},{4,12},{5,13},{6,14},{7,15},{8,0},{9,1},... | collective-permute-start | bytes 1228808 | tf_op jit(solution)/shard_map/ppermute | solution.py:329
  652.7 36.7 %collective-permute-start.14 = (bf16[320,640]{1,0:T(8,128)(2,1)S(1)}, bf16[320,640]{1,0:T(8,128)(2,1)S(1)}, u32[]{:S(2)}, u32[]{:S(2)}) collective-permute-start(bf16[320,640]{1,0:T(8,128)(2,1)S(1)} %get-tuple-element.98), channel_id=1, source_target_pairs={{0,4},{1,5},{2,6},{3,7},{4,8},{5,9},{6,10},{7,11},{8,12},{9,13},{1... | collective-permute-start | bytes 1228808 | tf_op jit(solution)/shard_map/ppermute | solution.py:329
Sparse Core Ops, SparseCore 0:
  10.7 49.1 all-gather.5
  62.3 62.3 all-gather.7
  126.9 61.9 all-gather.9

commit v2 on v1

v2 whole, which is shorter than its diff:
```python
import jax
import jax.numpy as jnp
from jax import lax
from jax.experimental import pallas as pl
from jax.experimental.pallas import tpu as pltpu
from jax.sharding import PartitionSpec as P

HEADS = 20
HEAD_DIM = 32
GROUP = 128 // HEAD_DIM
SCALE = HEAD_DIM ** -0.5
LOG2E = 1.4426950408889634
VMEM_LIMIT = 56 * 1024 * 1024
F32 = jnp.float32
BF16 = jnp.bfloat16


def cost(us):
    return pl.CostEstimate(flops=int(us * 1.1e9), bytes_accessed=1024, transcendentals=0)


def tied(count):
    return [pl.BlockSpec(memory_space=pl.ANY)] * count


def dot(a, b, dims=((1,), (0,))):
    return lax.dot_general(a, b, (dims, ((), ())), preferred_element_type=F32)


def gelu_pair(u):
    below = 0.5 + 0.5 * lax.erf(u * 0.7071067811865476)
    return u * below, below + (0.3989422804014327 * u) * jnp.exp(-0.5 * (u * u))


def normed(v, gain, shift):
    centered = v - jnp.mean(v, axis=-1, keepdims=True)
    spread = jnp.mean(centered * centered, axis=-1, keepdims=True)
    hat = centered * lax.rsqrt(spread + 1e-05)
    return hat * gain + shift


def norm_back(v, gain, grad):
    centered = v - jnp.mean(v, axis=-1, keepdims=True)
    spread = jnp.mean(centered * centered, axis=-1, keepdims=True)
    inv = lax.rsqrt(spread + 1e-05)
    hat = centered * inv
    g = grad * gain
    back = inv * (g - jnp.mean(g, axis=-1, keepdims=True) - hat * jnp.mean(g * hat, axis=-1, keepdims=True))
    return back, jnp.sum(grad * hat, axis=0, keepdims=True), jnp.sum(grad, axis=0, keepdims=True)


def attn_fwd_body(save, len_ref, h_ref, wqkv_ref, vec_ref, *outs):
    if save:
        m_ref, c_ref, qkv_ref, e_ref, o_ref, a_ref, inv_ref = outs
    else:
        m_ref, c_ref = outs
    width = h_ref.shape[2]
    seq = h_ref.shape[1]
    length = len_ref[pl.program_id(0)]
    h = h_ref[0].astype(F32)
    vec = vec_ref[...]
    a = normed(h, vec[0:1], vec[2:3]).astype(BF16)
    q_all = (dot(a, wqkv_ref[:, :width]) + vec[4:5]).astype(BF16)
    k_all = dot(a, wqkv_ref[:, width:2 * width]).astype(BF16)
    v_all = (dot(a, wqkv_ref[:, 2 * width:3 * width]) + vec[5:6]).astype(BF16)
    if save:
        a_ref[0] = a
        qkv_ref[0, :, :width] = q_all
        qkv_ref[0, :, width:2 * width] = k_all
        qkv_ref[0, :, 2 * width:] = v_all
    head_of = lax.broadcasted_iota(jnp.int32, (1, 128), 1) // HEAD_DIM
    key_at = lax.broadcasted_iota(jnp.int32, (seq, 128), 0)
    lane = lax.broadcasted_iota(jnp.int32, (seq, 128), 1)
    past = jnp.where((lane == 0) & (key_at >= length), -1e30, 0.0).astype(BF16)
    first = jnp.where(lane == 0, 1.0, 0.0).astype(BF16)
    ones = jnp.ones((seq, 128), BF16)
    zero = jnp.zeros((seq, 128), BF16)
    mixed = []
    for g in range(width // 128):
        at = slice(128 * g, 128 * g + 128)
        q, v = q_all[:, at], v_all[:, at]
        k = jnp.concatenate([k_all[:, at], past], axis=1)
        acc, inv = None, None
        for j in range(GROUP):
            mine = head_of == j
            s = dot(jnp.concatenate([jnp.where(mine, q, zero), first], axis=1), k, ((1,), (1,)))
            e = jnp.exp2((s - jnp.max(s, axis=1, keepdims=True)) * (SCALE * LOG2E)).astype(BF16)
            if save:
                e_ref[0, GROUP * g + j] = e
            both_parts = dot(e, jnp.concatenate([jnp.where(mine, v, zero), ones], axis=1))
            one_over = 1.0 / both_parts[:, 128:]
            part = both_parts[:, :128] * one_over
            acc = part if acc is None else acc + part
            inv = one_over if inv is None else jnp.where(mine, one_over, inv)
        mixed.append(acc.astype(BF16))
        if save:
            inv_ref[0, :, at] = inv
    o = jnp.concatenate(mixed, axis=1)
    if save:
        o_ref[0] = o
    m = h + dot(o, wqkv_ref[:, 3 * width:4 * width]) + vec[6:7]
    m_ref[0] = m
    c_ref[0] = normed(m, vec[1:2], vec[3:4]).astype(BF16)


def whole(shape):
    return pl.BlockSpec(shape, lambda *_: (0,) * len(shape))


def attn_fwd(h, lengths, proj, vec, save, after=()):
    n, seq, width = h.shape
    row = lambda *tail: pl.BlockSpec((1,) + tail, lambda i, *_: (i,) + (0,) * len(tail))
    shapes = [((seq, width), F32), ((seq, width), BF16)]
    if save:
        shapes += [((seq, 3 * width), BF16), ((HEADS, seq, seq), BF16), ((seq, width), BF16), ((seq, width), BF16), ((seq, width), F32)]
    waits = len(after)
    return pl.pallas_call(
        lambda *refs: attn_fwd_body(save, *refs[:4], *refs[4 + waits:]),
        grid_spec=pltpu.PrefetchScalarGridSpec(
            num_scalar_prefetch=1,
            grid=(n,),
            in_specs=[row(seq, width), whole(proj.shape), whole(vec.shape)] + tied(waits),
            out_specs=[row(*s) for s, _ in shapes],
        ),
        out_shape=[jax.ShapeDtypeStruct((n,) + s, d) for s, d in shapes],
        compiler_params=pltpu.CompilerParams(vmem_limit_bytes=VMEM_LIMIT),
        cost_estimate=cost(7 * n),
        name="attention_forward",
    )(lengths, h, proj, vec, *after)


def mlp_fwd_body(save, rows, c_ref, m_ref, wup_ref, wdown_ref, bup_ref, vec_ref, *outs):
    if save:
        y_ref, g_ref, gp_ref, acc_ref = outs
    else:
        y_ref, acc_ref = outs
    step = pl.program_id(0)

    @pl.when(step == 0)
    def _():
        acc_ref[...] = m_ref[...] + vec_ref[7:8]

    for r in range(c_ref.shape[0] // rows):
        at = slice(r * rows, r * rows + rows)
        u = dot(c_ref[at], wup_ref[...]) + bup_ref[...]
        act, slope = gelu_pair(u)
        act = act.astype(BF16)
        if save:
            g_ref[at] = act
            gp_ref[at] = slope.astype(BF16)
        acc_ref[at] += dot(act, wdown_ref[...])

    @pl.when(step == pl.num_programs(0) - 1)
    def _():
        y_ref[...] = acc_ref[...].astype(BF16)


def mlp_fwd(c, m, wup, wdown, bup, vec, save, chunk=1280, rows=256):
    n, width = c.shape
    ff = wup.shape[1]
    outs = [jax.ShapeDtypeStruct((n, width), BF16)]
    specs = [whole((n, width))]
    if save:
        outs += [jax.ShapeDtypeStruct((n, ff), BF16)] * 2
        specs += [pl.BlockSpec((n, chunk), lambda i: (0, i))] * 2
    return pl.pallas_call(
        lambda *refs: mlp_fwd_body(save, rows, *refs),
        grid=(ff // chunk,),
        in_specs=[whole(c.shape), whole(m.shape), pl.BlockSpec((width, chunk), lambda i: (0, i)),
                  pl.BlockSpec((chunk, width), lambda i: (i, 0)), pl.BlockSpec((1, chunk), lambda i: (0, i)), whole(vec.shape)],
        out_specs=specs,
        out_shape=outs,
        scratch_shapes=[pltpu.VMEM((n, width), F32)],
        compiler_params=pltpu.CompilerParams(vmem_limit_bytes=VMEM_LIMIT),
        cost_estimate=cost(38),
        name="feed_forward",
    )(c, m, wup, wdown, bup, vec)


def mlp_up_body(rows, c_ref, wup_ref, bup_ref, g_ref):
    for r in range(c_ref.shape[0] // rows):
        at = slice(r * rows, r * rows + rows)
        g_ref[at] = gelu_pair(dot(c_ref[at], wup_ref[...]) + bup_ref[...])[0].astype(BF16)


def mlp_up(c, wup, bup, after=(), chunk=1280, rows=256):
    n, width = c.shape
    ff = wup.shape[1]
    waits = len(after)
    return pl.pallas_call(
        lambda *refs: mlp_up_body(rows, *refs[:3], *refs[3 + waits:]),
        grid=(ff // chunk,),
        in_specs=[whole(c.shape), pl.BlockSpec((width, chunk), lambda i: (0, i)), pl.BlockSpec((1, chunk), lambda i: (0, i))] + tied(waits),
        out_specs=pl.BlockSpec((n, chunk), lambda i: (0, i)),
        out_shape=jax.ShapeDtypeStruct((n, ff), BF16),
        compiler_params=pltpu.CompilerParams(vmem_limit_bytes=VMEM_LIMIT),
        cost_estimate=cost(0.027 * n),
        name="feed_forward_up",
    )(c, wup, bup, *after)


def mlp_down_body(g_ref, m_ref, wdown_ref, vec_ref, y_ref, acc_ref):
    step = pl.program_id(0)

    @pl.when(step == 0)
    def _():
        acc_ref[...] = m_ref[...] + vec_ref[7:8]

    acc_ref[...] += dot(g_ref[...], wdown_ref[...])

    @pl.when(step == pl.num_programs(0) - 1)
    def _():
        y_ref[...] = acc_ref[...].astype(BF16)


def mlp_down(g, m, wdown, vec, at, parts, after=(), chunk=1280):
    ff, width = wdown.shape
    rows = g.shape[0] // parts
    waits = len(after)
    return pl.pallas_call(
        lambda *refs: mlp_down_body(*refs[:4], *refs[4 + waits:]),
        grid=(ff // chunk,),
        in_specs=[pl.BlockSpec((rows, chunk), lambda i: (at, i)), pl.BlockSpec((rows, width), lambda i: (at, 0)),
                  pl.BlockSpec((chunk, width), lambda i: (i, 0)), whole(vec.shape)] + tied(waits),
        out_specs=whole((rows, width)),
        out_shape=jax.ShapeDtypeStruct((rows, width), BF16),
        scratch_shapes=[pltpu.VMEM((rows, width), F32)],
        compiler_params=pltpu.CompilerParams(vmem_limit_bytes=VMEM_LIMIT),
        cost_estimate=cost(6),
        name="feed_forward_down",
    )(g, m, wdown, vec, *after)


def mlp_bwd_body(grads, rows, base_ref, dz_ref, gp_ref, wup_ref, wdown_ref, *rest):
    if grads:
        c_ref, dc_ref, gup_ref, gbu_ref, du_ref, ct_ref = rest
    else:
        dc_ref, = rest
    step = pl.program_id(0)
    n, width = dz_ref.shape

    @pl.when(step == 0)
    def _():
        dc_ref[...] = jnp.zeros_like(dc_ref) if base_ref is None else base_ref[...]
        if grads:
            ct_ref[:width] = c_ref[...].T
            ct_ref[width:] = jnp.ones_like(ct_ref[width:])

    for r in range(n // rows):
        at = slice(r * rows, r * rows + rows)
        dg = dot(dz_ref[at], wdown_ref[...], ((1,), (1,)))
        du = (dg * gp_ref[at].astype(F32)).astype(BF16)
        if grads:
            du_ref[at] = du
        dc_ref[at] += dot(du, wup_ref[...], ((1,), (1,)))
    if grads:
        gup = dot(ct_ref[...], du_ref[...])
        gup_ref[...] = gup[:width].astype(BF16)
        gbu_ref[...] = gup[width:width + 8]


def mlp_bwd(dz, gp, wup, wdown, c=None, at=0, parts=1, carry=None, after=(), chunk=1280, rows=256):
    n, width = dz.shape
    ff = wup.shape[1] // parts
    first = at * ff // chunk
    grads = c is not None
    args = [dz, gp, wup, wdown]
    in_specs = [whole(dz.shape), pl.BlockSpec((n, chunk), lambda i: (0, i + first)), pl.BlockSpec((width, chunk), lambda i: (0, i + first)),
                pl.BlockSpec((chunk, width), lambda i: (i + first, 0))]
    outs = [jax.ShapeDtypeStruct((n, width), F32)]
    specs = [whole((n, width))]
    scratch = []
    if grads:
        args += [c]
        in_specs += [whole(c.shape)]
        outs += [jax.ShapeDtypeStruct((width, ff), BF16), jax.ShapeDtypeStruct((8, ff), F32)]
        specs += [pl.BlockSpec((width, chunk), lambda i: (0, i)), pl.BlockSpec((8, chunk), lambda i: (0, i))]
        scratch = [pltpu.VMEM((n, chunk), BF16), pltpu.VMEM((width + 16, n), BF16)]
    if carry is not None:
        args += [carry]
        in_specs += [whole(carry.shape)]
    used, waits = len(args), len(after)
    args += after
    in_specs += tied(waits)

    def body(*refs):
        base = refs[used - 1] if carry is not None else None
        mlp_bwd_body(grads, rows, base, *refs[:5 if grads else 4], *refs[used + waits:])

    return pl.pallas_call(
        body,
        grid=(ff // chunk,),
        in_specs=in_specs,
        out_specs=specs,
        out_shape=outs,
        scratch_shapes=scratch,
        compiler_params=pltpu.CompilerParams(vmem_limit_bytes=VMEM_LIMIT),
        cost_estimate=cost((34 if grads else 26) / parts),
        name="feed_forward_back",
    )(*args)


def down_grad_body(g_ref, dz_ref, out_ref):
    out_ref[...] = dot(g_ref[...], dz_ref[...], ((0,), (0,))).astype(BF16)


def down_grad(g, dz, chunk=1280):
    n, ff = g.shape
    width = dz.shape[1]
    return pl.pallas_call(
        down_grad_body,
        grid=(ff // chunk,),
        in_specs=[pl.BlockSpec((n, chunk), lambda i: (0, i)), whole(dz.shape)],
        out_specs=pl.BlockSpec((chunk, width), lambda i: (i, 0)),
        out_shape=jax.ShapeDtypeStruct((ff, width), BF16),
        compiler_params=pltpu.CompilerParams(vmem_limit_bytes=VMEM_LIMIT),
        cost_estimate=cost(10),
        name="down_gradient",
    )(g, dz)


def attn_bwd_body(grads, dc_ref, dz_ref, m_ref, h_ref, qkv_ref, e_ref, o_ref, inv_ref, proj_ref, vec_ref, dh_ref, *outs):
    if grads:
        dr_ref, dqkv_ref, small_ref = outs
    width = h_ref.shape[2]
    vec = vec_ref[...]

    if grads:
        @pl.when(pl.program_id(0) == 0)
        def _():
            small_ref[...] = jnp.zeros_like(small_ref)

    dz = dz_ref[0].astype(F32)
    back, g_gain1, g_shift1 = norm_back(m_ref[0], vec[1:2], dc_ref[0])
    dm = dz + back
    dr = dm.astype(BF16)
    if grads:
        dr_ref[0] = dr
    do_all = dot(dr, proj_ref[:, 3 * width:4 * width], ((1,), (1,))).astype(BF16)
    seq = h_ref.shape[1]
    head_of = lax.broadcasted_iota(jnp.int32, (1, 128), 1) // HEAD_DIM
    ones = jnp.ones((seq, 128), BF16)
    zero = jnp.zeros((seq, 128), BF16)
    dq_all, dk_all, dv_all = [], [], []
    for g in range(width // 128):
        at = slice(128 * g, 128 * g + 128)
        q = qkv_ref[0, :, 128 * g:128 * g + 128]
        k = qkv_ref[0, :, width + 128 * g:width + 128 * g + 128]
        v = jnp.concatenate([qkv_ref[0, :, 2 * width + 128 * g:2 * width + 128 * g + 128], ones], axis=1)
        scaled = do_all[:, at].astype(F32) * (inv_ref[0, :, at] * SCALE)
        do = scaled.astype(BF16)
        less = (-scaled * o_ref[0, :, at].astype(F32)).astype(BF16)
        do_t, q_t = do.T, q.T
        dq = None
        dk_t, dv_t = [], []
        for j in range(GROUP):
            mine = head_of == j
            e = e_ref[0, GROUP * g + j]
            rows = slice(HEAD_DIM * j, HEAD_DIM * j + HEAD_DIM)
            dv_t.append(dot(do_t[rows], e))
            dp = dot(jnp.concatenate([jnp.where(mine, do, zero), jnp.where(mine, less, zero)], axis=1), v, ((1,), (1,)))
            ds = (e.astype(F32) * dp).astype(BF16)
            part = dot(ds, jnp.where(mine, k, zero))
            dq = part if dq is None else dq + part
            dk_t.append(dot(q_t[rows], ds))
        dq_all.append(dq.astype(BF16))
        dk_all.append(jnp.concatenate(dk_t, axis=0).astype(BF16).T)
        dv_all.append((jnp.concatenate(dv_t, axis=0) * (1.0 / SCALE)).astype(BF16).T)
    dqkv = jnp.concatenate(dq_all + dk_all + dv_all, axis=1)
    if grads:
        dqkv_ref[0] = dqkv
    da = dot(dqkv, proj_ref[:, :3 * width], ((1,), (1,)))
    back, g_gain0, g_shift0 = norm_back(h_ref[0].astype(F32), vec[0:1], da)
    dh_ref[0] = (dm + back).astype(dh_ref.dtype)
    if not grads:
        return
    total = lambda x: jnp.sum(x.astype(F32), axis=0, keepdims=True)
    small_ref[...] += jnp.concatenate(
        [g_gain0, g_gain1, g_shift0, g_shift1, total(dqkv[:, :width]), total(dqkv[:, 2 * width:]), total(dr), total(dz)], axis=0)


def attn_bwd(dc, dz, m, h, qkv, e, o, inv, proj, vec, at, parts, grads, after=()):
    n, seq, width = h.shape
    n //= parts
    row = lambda *tail: pl.BlockSpec((1,) + tail, lambda i: (i + at * n,) + (0,) * len(tail))
    out = lambda *tail: pl.BlockSpec((1,) + tail, lambda i: (i,) + (0,) * len(tail))
    shapes = [((seq, width), F32), ((seq, width), BF16), ((seq, 3 * width), BF16)]
    specs = [out(*s) for s, _ in shapes] + [whole((8, width))]
    results = [jax.ShapeDtypeStruct((n,) + s, d) for s, d in shapes] + [jax.ShapeDtypeStruct((8, width), F32)]
    if not grads:
        specs, results = specs[:1], [jax.ShapeDtypeStruct((n, seq, width), BF16)]
    waits = len(after)
    return pl.pallas_call(
        lambda *refs: attn_bwd_body(grads, *refs[:10], *refs[10 + waits:]),
        grid=(n,),
        in_specs=[row(seq, width), row(seq, width), row(seq, width), row(seq, width), row(seq, 3 * width), row(HEADS, seq, seq), row(seq, width), row(seq, width),
                  whole(proj.shape), whole(vec.shape)] + tied(waits),
        out_specs=specs,
        out_shape=results,
        compiler_params=pltpu.CompilerParams(vmem_limit_bytes=VMEM_LIMIT),
        cost_estimate=cost(9 * n),
        name="attention_back",
    )(dc, dz, m, h, qkv, e, o, inv, proj, vec, *after)


def proj_grad_body(a_ref, dqkv_ref, o_ref, dr_ref, table_ref, out_ref, at_ref):
    step = pl.program_id(0)
    width = a_ref.shape[1]

    @pl.when(step == 0)
    def _():
        at_ref[...] = a_ref[...].T
        out_ref[:, 3 * width:4 * width] = dot(o_ref[...], dr_ref[...], ((0,), (0,))).astype(BF16)
        out_ref[:, 4 * width:] = table_ref[...].astype(BF16)

    out_ref[:, pl.ds(pl.multiple_of(step * width, 128), width)] = dot(at_ref[...], dqkv_ref[...]).astype(BF16)


def proj_grad(a, dqkv, o, dr, table, after=()):
    n, width = a.shape
    waits = len(after)
    shape = (width, 4 * width + table.shape[1])
    return pl.pallas_call(
        lambda *refs: proj_grad_body(*refs[:5], *refs[5 + waits:]),
        grid=(3,),
        in_specs=[whole(a.shape), pl.BlockSpec((n, width), lambda i: (0, i)), whole(o.shape), whole(dr.shape), whole(table.shape)] + tied(waits),
        out_specs=whole(shape),
        out_shape=jax.ShapeDtypeStruct(shape, BF16),
        scratch_shapes=[pltpu.VMEM((width, n), BF16)],
        compiler_params=pltpu.CompilerParams(vmem_limit_bytes=VMEM_LIMIT),
        cost_estimate=cost(9),
        name="projection_gradients",
    )(a, dqkv, o, dr, table, *after)


def place_body(count, to_ref, *refs):
    pieces, out_ref, sems = refs[:count], refs[count], refs[count + 1]
    copies = [pltpu.make_async_copy(piece, out_ref.at[to_ref[i]], sems.at[i]) for i, piece in enumerate(pieces)]
    for copy in copies:
        copy.start()
    for copy in copies:
        copy.wait()


def place(pieces, to, after=()):
    rows, columns = pieces[0].shape
    count, waits = len(pieces), len(after)
    out = pl.pallas_call(
        lambda *refs: place_body(count, *refs[:count + 1], *refs[count + 1 + waits:]),
        in_specs=[pl.BlockSpec(memory_space=pltpu.SMEM)] + [pl.BlockSpec(memory_space=pl.ANY)] * count + tied(waits),
        out_specs=pl.BlockSpec(memory_space=pltpu.VMEM),
        out_shape=jax.ShapeDtypeStruct((count, rows, columns), BF16),
        scratch_shapes=[pltpu.SemaphoreType.DMA((count,))],
        compiler_params=pltpu.CompilerParams(vmem_limit_bytes=VMEM_LIMIT),
        cost_estimate=cost(4),
        name="place_pieces",
    )(to, *pieces, *after)
    return out.reshape(count * rows, columns)


def places(count):
    return count // 4, 2, 2


def hop(value, kind, step=1):
    zs, ys, cores = places(lax.axis_size("dp"))
    pairs = []
    for z in range(zs):
        for y in range(ys):
            for c in range(cores):
                to = {"core": (z, y, c ^ 1), "y": (z, y ^ 1, c), "z": ((z + step) % zs, y, c)}[kind]
                pairs.append(((z * ys + y) * cores + c, (to[0] * ys + to[1]) * cores + to[2]))
    return lax.ppermute(value, "dp", pairs)


def pick(value, index, axis):
    return lax.dynamic_index_in_dim(value, index, axis, keepdims=False)


def behind_me():
    zs, ys, cores = places(lax.axis_size("dp"))
    me = lax.axis_index("dp")
    return me // (cores * ys), (me // cores) % ys, me % cores


def along_line(shard):
    return [shard] + [hop(shard, "z", step) for step in range(1, places(lax.axis_size("dp"))[0])]


def both(mine, got):
    return (mine.astype(F32) + got.astype(F32)).astype(BF16)


def core_step(grad, rows):
    zs, ys, cores = places(lax.axis_size("dp"))
    _, _, c = behind_me()
    parts = grad.reshape(zs, ys, cores, rows, grad.shape[1])
    return hop(pick(parts, 1 - c, 2), "core"), pick(parts, c, 2)


def y_step(parts):
    _, y, _ = behind_me()
    return hop(pick(parts, 1 - y, 1), "y"), pick(parts, y, 1)


def z_step(parts):
    zs, _, _ = places(lax.axis_size("dp"))
    z, _, _ = behind_me()
    return [hop(pick(parts, (z + step) % zs, 0), "z", step) for step in range(1, zs)], pick(parts, z, 0)


def z_total(got, mine):
    total = mine.astype(F32)
    for piece in got:
        total = total + piece.astype(F32)
    return total


def held(value, *after):
    return lax.optimization_barrier((value, *after))[0]


def assemble(line, other, siblings):
    zs, ys, cores = places(lax.axis_size("dp"))
    z, y, c = behind_me()
    to = []
    for core in (c, 1 - c):
        for row in (y, 1 - y):
            to += [(((z + zs - step) % zs) * ys + row) * cores + core for step in range(zs)]
    return place(line + other + siblings, jnp.stack(to).astype(jnp.int32))


def on_device(tokens, lengths, cotangent, w_qkv, w_out, w_up, w_down, norm_gain, norm_bias, bias_vec, up_bias):
    section = lax.axis_index("section")
    windows, seq, width = tokens.shape
    n = windows * seq
    shard = w_qkv.shape[1]
    per_row = up_bias.shape[1] // shard
    ff = w_up.shape[2]
    parts = 2
    part = windows // parts
    by_hand = lax.axis_size("dp") == 16
    table = jnp.concatenate([norm_gain[0], norm_bias[0], bias_vec[0]], axis=0).T
    table = jnp.concatenate([table, up_bias.reshape(shard, per_row)], axis=1)
    used = table.shape[1]
    table = jnp.pad(table, ((0, 0), (0, 128 - used)))
    packed = jnp.concatenate([w_qkv[0], w_out[0], table], axis=1)
    proj = lax.all_gather(packed, "dp", axis=0, tiled=True)
    if by_hand:
        up_line = along_line(w_up[0])
        up_other = [hop(piece, "y") for piece in up_line]
        wup = assemble(up_line, up_other, [hop(piece, "core") for piece in up_line + up_other])
        own = w_down[0]
        near = held(own, *up_line[1:])
        near = [hop(near, "z", step) for step in (1, 3)]
        far = hop(held(own, near[0]), "z", 2)
        down_line = [own, near[0], far, near[1]]
        down_other = [hop(piece, "y") for piece in down_line]
    else:
        up_line, up_other, down_line, down_other = (), (), (), ()
        wup = lax.all_gather(w_up[0], "dp", axis=0, tiled=True)
        wdown = lax.all_gather(w_down[0], "dp", axis=0, tiled=True)
    small = proj[:, 4 * width:4 * width + used]
    vec = small[:, :8].T.astype(F32)
    bup = small[:, 8:].reshape(1, ff).astype(F32)

    mid, c = attn_fwd(tokens, lengths, proj, vec, False, (*up_line, *down_other[:1]))
    act = mlp_up(c.reshape(n, width), wup, bup, (*down_line, *down_other[1::2]))
    if by_hand:
        wdown = assemble(down_line, down_other, [hop(piece, "core") for piece in down_line + down_other])
    mid = mid.reshape(n, width)
    arrived = []
    for at in range(parts):
        y = mlp_down(act, mid, wdown, vec, at, parts)
        arrived.append(lax.ppermute(y.reshape(part, seq, width), "section", [(0, 1)]))
    h = jnp.where(section == 0, tokens, jnp.concatenate(arrived))

    m, c, qkv, e, o, a, inv = attn_fwd(h, lengths, proj, vec, True)
    c = c.reshape(n, width)
    y, g, gp = mlp_fwd(c, m.reshape(n, width), wup, wdown, bup, vec, True)

    dc, = mlp_bwd(cotangent.reshape(n, width), gp, wup, wdown)
    dc = dc.reshape(tokens.shape)
    arrived = []
    for at in range(parts):
        back, = attn_bwd(dc, cotangent, m, h, qkv, e, o, inv, proj, vec, at, parts, False)
        arrived.append(lax.ppermute(back, "section", [(1, 0)]))
    dz = jnp.where(section == 1, cotangent, jnp.concatenate(arrived))

    g_down = down_grad(g, dz.reshape(n, width))
    sum_down = lax.psum_scatter(g_down, "dp", scatter_dimension=0, tiled=True).astype(F32)
    flat = dz.reshape(n, width)
    dc, g_up_a, g_bup_a = mlp_bwd(flat, gp, wup, wdown, c, 0, 2, None, (g_down,))
    got_a, mine_a = core_step(g_up_a, shard)
    dc, g_up_b, g_bup_b = mlp_bwd(flat, gp, wup, wdown, c, 1, 2, dc)
    dc = dc.reshape(tokens.shape)
    got_b, mine_b = core_step(g_up_b, shard)
    ya = y_step(both(mine_a, got_a))
    back_a = attn_bwd(dc, dz, m, h, qkv, e, o, inv, proj, vec, 0, 2, True, (got_a,))
    yb = y_step(both(mine_b, got_b))
    za = z_step(both(ya[1], ya[0]))
    back_b = attn_bwd(dc, dz, m, h, qkv, e, o, inv, proj, vec, 1, 2, True, (back_a[0], got_b, ya[0]))
    dh, dr, dqkv = [jnp.concatenate([back_a[i], back_b[i]]) for i in range(3)]
    smalls = back_a[3] + back_b[3]
    g_bup = jnp.concatenate([g_bup_a[0], g_bup_b[0]])
    g_table = jnp.concatenate([smalls.T, g_bup.reshape(width, per_row)], axis=1)
    g_table = jnp.pad(g_table, ((0, 0), (0, 128 - used)))
    zb = z_step(both(yb[1], yb[0]))
    g_proj = proj_grad(a.reshape(n, width), dqkv.reshape(n, 3 * width), o.reshape(n, width), dr.reshape(n, width), g_table, (yb[0],))
    got_p, mine_p = core_step(g_proj, shard)
    yp = y_step(both(mine_p, got_p))
    sum_up = jnp.concatenate([z_total(*za), z_total(*zb)], axis=1)
    sum_proj = z_total(*z_step(held(both(yp[1], yp[0]), *zb[0])))
    vectors = sum_proj[:, 4 * width:4 * width + 8].T
    return (
        y.reshape((1,) + tokens.shape),
        dh[None],
        sum_proj[None, :, :3 * width],
        sum_proj[None, :, 3 * width:4 * width],
        sum_up[None],
        sum_down[None],
        vectors[None, 0:2],
        vectors[None, 2:4],
        vectors[None, 4:8],
        sum_proj[:, 4 * width + 8:4 * width + used].reshape(1, -1),
    )


def solution(mesh):
    sharded = [P("section", "dp", None)] * 4 + [P("section", None, "dp")] * 3 + [P("section", "dp")]
    windows = P("dp", None, None)
    out = P("section", "dp", None, None)
    return jax.shard_map(
        on_device, mesh=mesh, in_specs=(windows, P("dp"), windows, *sharded), out_specs=(out, out, *sharded), check_vma=False
    )
```

time: 704 us -> 572 us (0.81)
  waiting for transfers between devices: 324 us -> 201 us
  Pallas kernels: 282 us -> 250 us
  starting transfers between devices: 22.2 us -> 44.4 us
    all_gather x2 -> x0, waiting for transfers between devices: 97.8 us -> none  [the longest x1 64.3 us: on_device(): wdown = lax.all_gather(w_down[0], 'dp', axis=0, tiled=True)]
    pallas_call x2 -> x1, Pallas kernels: 76.5 us -> 26.5 us  [mlp_fwd(): pl.pallas_call(lambda *refs: mlp_fwd_body(save, rows, *refs), grid=(ff //...]
    all_gather x1, waiting for transfers between devices: 47.9 us -> 0.02 us  [on_device(): proj = lax.all_gather(packed, 'dp', axis=0, tiled=True)]
    ppermute x15 -> x45, waiting for transfers between devices: 117 us -> 157 us  [hop(): return lax.ppermute(value, 'dp', pairs)]
    ppermute x15 -> x45, starting transfers between devices: 17 us -> 36.7 us  [hop(): return lax.ppermute(value, 'dp', pairs)]
    pallas_call x7 -> x16, Pallas kernels: 206 us -> 224 us  [the longest x4 64.3 us: attn_bwd(): pl.pallas_call(lambda *refs: attn_bwd_body(grads, *refs[:10], *refs[10 +...]
    ppermute x2 -> x4, waiting for transfers between devices: 59.3 us -> 44.4 us  [the longest x2 27.2 us: on_device(): lax.ppermute(y.reshape(part, seq, width), 'section', [(0, 1)])]
    convert_element_type x7 -> x6, other arithmetic: 14.4 us -> 5.11 us  [both(): return (mine.astype(F32) + got.astype(F32)).astype(BF16)]
  transfers between devices with their start and end apart: 20 -> 51, of which waited for: 12 -> 21; matrix products, arithmetic and copies ran while one was open for 5% -> 5% of each run, Pallas kernels for 4% -> 13%
where the time goes in v2:
time: 572 us; the launch traced here: 563 us
  Pallas kernels  250 us (44%)
  waiting for transfers between devices  201 us (35%)
  starting transfers between devices  44.4 us (8%)
  local copies, waits for them, and re-layouts  27.7 us (5%)
  other arithmetic  24.3 us (4%)
  between operations  15.2 us (3%)
    ppermute x45, waiting for transfers between devices, hop(): return lax.ppermute(value, 'dp', pairs)  157 us
    pallas_call x4, Pallas kernels, attn_bwd(): pl.pallas_call(lambda *refs: attn_bwd_body(grads, *refs[:10], *refs[10 +...  64.3 us
    pallas_call x3, Pallas kernels, mlp_bwd(): pl.pallas_call(body, grid=(ff // chunk,), in_specs=in_specs, out_specs=sp...  59.5 us
    ppermute x45, starting transfers between devices, hop(): return lax.ppermute(value, 'dp', pairs)  36.7 us
    pallas_call x2, Pallas kernels, attn_fwd(): pl.pallas_call(lambda *refs: attn_fwd_body(save, *refs[:4], *refs[4 + wai...  34.8 us
    ppermute x2, waiting for transfers between devices, on_device(): lax.ppermute(y.reshape(part, seq, width), 'section', [(0, 1)])  27.2 us
    pallas_call x1, Pallas kernels, mlp_fwd(): pl.pallas_call(lambda *refs: mlp_fwd_body(save, rows, *refs), grid=(ff //...  26.5 us
    pallas_call x2, Pallas kernels, mlp_down(): pl.pallas_call(lambda *refs: mlp_down_body(*refs[:4], *refs[4 + waits:]),...  17.7 us
  transfers between devices with their start and end apart: 51, of which 21 were waited for; matrix products, arithmetic and copies ran while one was open for 5% of the time, Pallas kernels for 13%

profile of v2, /device:TPU:0, one launch (start us, length us, event | category | flops | bytes accessed | tf_op | source)
XLA Modules:
  0.0 563.3 jit_solution(15505859997888372300)
XLA Ops:
  18.3 10.9 %collective-permute-done.2.refs_7_.refs_4_ = bf16[40,5120]{1,0:T(8,128)(2,1)S(1)} collective-permute-done((bf16[40,5120]{1,0:T(8,128)(2,1)}, bf16[40,5120]{1,0:T(8,128)(2,1)S(1)}, u32[]{:S(2)}, u32[]{:S(2)}) %collective-permute-start.2) | collective-permute-done | bytes 409632 | tf_op jit(solution)/shard_map/ppermute | solution.py:473
  29.2 28.7 %collective-permute-done.1.refs_6_.refs_3_ = bf16[40,5120]{1,0:T(8,128)(2,1)S(1)} collective-permute-done((bf16[40,5120]{1,0:T(8,128)(2,1)}, bf16[40,5120]{1,0:T(8,128)(2,1)S(1)}, u32[]{:S(2)}, u32[]{:S(2)}) %collective-permute-start.1) | collective-permute-done | bytes 409632 | tf_op jit(solution)/shard_map/ppermute | solution.py:473
  60.9 17.5 %collective-permute-done.3.refs_8_.refs_5_ = bf16[320,640]{1,0:T(8,128)(2,1)S(1)} collective-permute-done((bf16[320,640]{1,0:T(8,128)(2,1)}, bf16[320,640]{1,0:T(8,128)(2,1)S(1)}, u32[]{:S(2)}, u32[]{:S(2)}) %collective-permute-start.3) | collective-permute-done | bytes 409632 | tf_op jit(solution)/shard_map/ppermute | solution.py:473
  80.1 7.1 %collective-permute-done.7.refs_8_ = bf16[40,5120]{1,0:T(8,128)(2,1)S(1)} collective-permute-done((bf16[40,5120]{1,0:T(8,128)(2,1)S(1)}, bf16[40,5120]{1,0:T(8,128)(2,1)S(1)}, u32[]{:S(2)}, u32[]{:S(2)}) %collective-permute-start.7) | collective-permute-done | bytes 409632 | tf_op jit(solution)/shard_map/ppermute | solution.py:473
  87.9 8.1 %collective-permute-done.6.refs_7_ = bf16[40,5120]{1,0:T(8,128)(2,1)S(1)} collective-permute-done((bf16[40,5120]{1,0:T(8,128)(2,1)S(1)}, bf16[40,5120]{1,0:T(8,128)(2,1)S(1)}, u32[]{:S(2)}, u32[]{:S(2)}) %collective-permute-start.6) | collective-permute-done | bytes 409632 | tf_op jit(solution)/shard_map/ppermute | solution.py:473
  97.4 6.6 %collective-permute-done.5.refs_6_ = bf16[40,5120]{1,0:T(8,128)(2,1)} collective-permute-done((bf16[40,5120]{1,0:T(8,128)(2,1)S(1)}, bf16[40,5120]{1,0:T(8,128)(2,1)}, u32[]{:S(2)}, u32[]{:S(2)}) %collective-permute-start.5) | collective-permute-done | bytes 409632 | tf_op jit(solution)/shard_map/ppermute | solution.py:473
  106.3 9.6 %collective-permute-done.17.refs_5_.refs_3_ = bf16[320,640]{1,0:T(8,128)(2,1)} collective-permute-done((bf16[320,640]{1,0:T(8,128)(2,1)}, bf16[320,640]{1,0:T(8,128)(2,1)}, u32[]{:S(2)}, u32[]{:S(2)}) %collective-permute-start.17) | collective-permute-done | bytes 409632 | tf_op jit(solution)/shard_map/ppermute | solution.py:473
  118.5 7.0 %collective-permute-done.19.refs_7_.refs_6_ = bf16[320,640]{1,0:T(8,128)(2,1)} collective-permute-done((bf16[320,640]{1,0:T(8,128)(2,1)S(1)}, bf16[320,640]{1,0:T(8,128)(2,1)}, u32[]{:S(2)}, u32[]{:S(2)}) %collective-permute-start.19) | collective-permute-done | bytes 409632 | tf_op jit(solution)/shard_map/ppermute | solution.py:473
  126.0 7.8 %collective-permute-done.21.refs_7_ = bf16[320,640]{1,0:T(8,128)(2,1)} collective-permute-done((bf16[320,640]{1,0:T(8,128)(2,1)}, bf16[320,640]{1,0:T(8,128)(2,1)}, u32[]{:S(2)}, u32[]{:S(2)}) %collective-permute-start.21) | collective-permute-done | bytes 409632 | tf_op jit(solution)/shard_map/ppermute | solution.py:473
  133.8 6.4 %place_pieces.2 = bf16[16,40,5120]{2,1,0:T(8,128)(2,1)} custom-call(s32[16]{0:T(128)} %stack.84.refs_0_, bf16[40,5120]{1,0:T(8,128)(2,1)} %bitcast.156, bf16[40,5120]{1,0:T(8,128)(2,1)} %copy-done.18, bf16[40,5120]{1,0:T(8,128)(2,1)} %copy-done.17, bf16[40,5120]{1,0:T(8,128)(2,1)} %copy-done.16, bf16[40,5120]{1,0:T(8,128)(2,1)} %copy-done.22, ...), custom_call_target="tpu_custom_call" | custom-call | flops 4400000000 | bytes 1024 | tf_op jit(solution)/shard_map/place_pieces/pallas_call | solution.py:448
  142.2 6.3 %place_pieces.3 = bf16[16,320,640]{2,1,0:T(8,128)(2,1)} custom-call(s32[16]{0:T(128)} %stack.84.refs_0_, bf16[320,640]{1,0:T(8,128)(2,1)} %bitcast.163, bf16[320,640]{1,0:T(8,128)(2,1)} %copy-done.20, bf16[320,640]{1,0:T(8,128)(2,1)} %collective-permute-done.17.refs_5_.refs_3_, bf16[320,640]{1,0:T(8,128)(2,1)} %collective-permute-done.18.refs_6_.refs_4_, ...), custom_call_target="tpu_custom_call" | custom-call | flops 4400000000 | bytes 1024 | tf_op jit(solution)/shard_map/place_pieces/pallas_call | solution.py:448
  151.2 16.7 %attention_forward.2 = (f32[4,256,640]{2,1,0:T(8,128)}, bf16[4,256,640]{2,1,0:T(8,128)(2,1)}) custom-call(s32[4]{0:T(128)} %refs_0_.3, bf16[4,256,640]{2,1,0:T(8,128)(2,1)} %refs_1_.3, bf16[640,2688]{1,0:T(8,128)(2,1)} %all-gather.2.cloned.1.call-done.refs_2_.refs_8_, f32[8,640]{1,0:T(8,128)} %convert_bitcast_fusion.refs_3_.refs_5_.refs_9_, ...), custom_call_target="tpu_custom_call" | custom-call | flops 30799998976 | bytes 1024 | tf_op jit(solution)/shard_map/attention_forward/pallas_call | solution.py:117
  167.9 12.7 %feed_forward_up.1.refs_0_ = bf16[1024,5120]{1,0:T(8,128)(2,1)} custom-call(bf16[1024,640]{1,0:T(8,128)(2,1)} %bitcast.189, bf16[640,5120]{1,0:T(8,128)(2,1)} %bitcast.165, f32[1,5120]{1,0:T(1,128)} %reshape.147.refs_2_.refs_4_, bf16[320,640]{1,0:T(8,128)(2,1)} %bitcast.164, bf16[320,640]{1,0:T(8,128)(2,1)} %copy-done.20, ...), custom_call_target="tpu_custom_call" | custom-call | flops 30412800000 | bytes 1024 | tf_op jit(solution)/shard_map/feed_forward_up/pallas_call | solution.py:190
  180.6 8.8 %feed_forward_down.3 = bf16[512,640]{1,0:T(8,128)(2,1)} custom-call(bf16[1024,5120]{1,0:T(8,128)(2,1)} %feed_forward_up.1.refs_0_, f32[1024,640]{1,0:T(8,128)} %bitcast.179, bf16[5120,640]{1,0:T(8,128)(2,1)} %bitcast.170, f32[8,640]{1,0:T(8,128)} %convert_bitcast_fusion.refs_3_.refs_5_.refs_9_), custom_call_target="tpu_custom_call" | custom-call | flops 6600000000 | bytes 1024 | tf_op jit(solution)/shard_map/feed_forward_down/pallas_call | solution.py:220
  189.4 8.9 %feed_forward_down.2 = bf16[512,640]{1,0:T(8,128)(2,1)} custom-call(bf16[1024,5120]{1,0:T(8,128)(2,1)} %feed_forward_up.1.refs_0_, f32[1024,640]{1,0:T(8,128)} %bitcast.180, bf16[5120,640]{1,0:T(8,128)(2,1)} %bitcast.171, f32[8,640]{1,0:T(8,128)} %convert_bitcast_fusion.refs_3_.refs_5_.refs_9_), custom_call_target="tpu_custom_call" | custom-call | flops 6600000000 | bytes 1024 | tf_op jit(solution)/shard_map/feed_forward_down/pallas_call | solution.py:220
  203.3 13.4 %collective-permute-done.31 = bf16[2,256,640]{2,1,0:T(8,128)(2,1)S(1)} collective-permute-done((bf16[2,256,640]{2,1,0:T(8,128)(2,1)S(1)}, bf16[2,256,640]{2,1,0:T(8,128)(2,1)S(1)}, u32[]{:S(2)}, u32[]{:S(2)}) %collective-permute-start.31) | collective-permute-done | bytes 655392 | tf_op jit(solution)/shard_map/ppermute | solution.py:575
  216.8 13.8 %collective-permute-done.30 = bf16[2,256,640]{2,1,0:T(8,128)(2,1)S(1)} collective-permute-done((bf16[2,256,640]{2,1,0:T(8,128)(2,1)}, bf16[2,256,640]{2,1,0:T(8,128)(2,1)S(1)}, u32[]{:S(2)}, u32[]{:S(2)}) %collective-permute-start.30) | collective-permute-done | bytes 655392 | tf_op jit(solution)/shard_map/ppermute | solution.py:575
  231.8 18.1 %attention_forward.3 = (f32[4,256,640]{2,1,0:T(8,128)}, bf16[4,256,640]{2,1,0:T(8,128)(2,1)}, bf16[4,256,1920]{2,1,0:T(8,128)(2,1)}, bf16[4,20,256,256]{3,2,1,0:...) custom-call(s32[4]{0:T(128)} %refs_0_.3, ...), custom_call_target="tpu_custom_call" | custom-call | flops 30799998976 | bytes 1024 | tf_op jit(solution)/shard_map/attention_forward/pallas_call | solution.py:117
  249.9 26.5 %feed_forward.1 = (bf16[1024,640]{1,0:T(8,128)(2,1)}, bf16[1024,5120]{1,0:T(8,128)(2,1)}, bf16[1024,5120]{1,0:T(8,128)(2,1)}) custom-call(bf16[1024,640]{1,0:T(8,128)(2,1)} %bitcast.186, f32[1024,640]{1,0:T(8,128)} %bitcast.176, bf16[640,5120]{1,0:T(8,128)(2,1)} %bitcast.166, bf16[5120,640]{1,0:T(8,128)(2,1)} %bitcast.172, ...), custom_call_target="tpu_custom_call" | custom-call | flops 41799999488 | bytes 1024 | tf_op jit(solution)/shard_map/feed_forward/pallas_call | solution.py:166
  276.4 22.8 %feed_forward_back.3 = f32[1024,640]{1,0:T(8,128)} custom-call(bf16[1024,640]{1,0:T(8,128)(2,1)} %bitcast.137, bf16[1024,5120]{1,0:T(8,128)(2,1)} %get-tuple-element.46.refs_1_, bf16[640,5120]{1,0:T(8,128)(2,1)} %bitcast.167, bf16[5120,640]{1,0:T(8,128)(2,1)} %bitcast.173), custom_call_target="tpu_custom_call" | custom-call | flops 28600000512 | bytes 1024 | tf_op jit(solution)/shard_map/feed_forward_back/pallas_call | solution.py:290
  299.3 15.6 %attention_back.4 = bf16[2,256,640]{2,1,0:T(8,128)(2,1)} custom-call(f32[4,256,640]{2,1,0:T(8,128)} %bitcast.181, bf16[4,256,640]{2,1,0:T(8,128)(2,1)} %refs_1_.5, f32[4,256,640]{2,1,0:T(8,128)} %get-tuple-element.44.refs_2_, bf16[4,256,640]{2,1,0:T(8,128)(2,1)} %maximum_select_fusion.refs_1_.refs_3_, bf16[4,256,1920]{2,1,0:T(8,128)(2,1)} %get-tuple-element.47.refs_4_, ...), custom_call_target="tpu_custom_call" | custom-call | flops 19800000512 | bytes 1024 | tf_op jit(solution)/shard_map/attention_back/pallas_call | solution.py:393
  316.3 15.7 %attention_back.5 = bf16[2,256,640]{2,1,0:T(8,128)(2,1)} custom-call(f32[4,256,640]{2,1,0:T(8,128)} %bitcast.182, bf16[4,256,640]{2,1,0:T(8,128)(2,1)} %refs_1_.5, f32[4,256,640]{2,1,0:T(8,128)} %get-tuple-element.44.refs_2_, bf16[4,256,640]{2,1,0:T(8,128)(2,1)} %maximum_select_fusion.refs_1_.refs_3_, bf16[4,256,1920]{2,1,0:T(8,128)(2,1)} %get-tuple-element.47.refs_4_, ...), custom_call_target="tpu_custom_call" | custom-call | flops 19800000512 | bytes 1024 | tf_op jit(solution)/shard_map/attention_back/pallas_call | solution.py:393
  333.4 17.1 %collective-permute-done.33 = bf16[2,256,640]{2,1,0:T(8,128)(2,1)S(1)} collective-permute-done((bf16[2,256,640]{2,1,0:T(8,128)(2,1)}, bf16[2,256,640]{2,1,0:T(8,128)(2,1)S(1)}, u32[]{:S(2)}, u32[]{:S(2)}) %collective-permute-start.33) | collective-permute-done | bytes 655392 | tf_op jit(solution)/shard_map/ppermute | solution.py:587
  351.7 12.4 %down_gradient.1.refs_5_ = bf16[5120,640]{1,0:T(8,128)(2,1)} custom-call(bf16[1024,5120]{1,0:T(8,128)(2,1)} %get-tuple-element.51.g_ref, bf16[1024,640]{1,0:T(8,128)(2,1)} %bitcast.138), custom_call_target="tpu_custom_call" | custom-call | flops 11000000512 | bytes 1024 | tf_op jit(solution)/shard_map/down_gradient/pallas_call | solution.py:310
  364.1 17.7 %feed_forward_back.4 = (f32[1024,640]{1,0:T(8,128)}, bf16[640,2560]{1,0:T(8,128)(2,1)}, f32[8,2560]{1,0:T(8,128)}) custom-call(bf16[1024,640]{1,0:T(8,128)(2,1)} %bitcast.139, bf16[1024,5120]{1,0:T(8,128)(2,1)} %get-tuple-element.46.refs_1_, bf16[640,5120]{1,0:T(8,128)(2,1)} %bitcast.168, bf16[5120,640]{1,0:T(8,128)(2,1)} %bitcast.174, ...), custom_call_target="tpu_custom_call" | custom-call | flops 18699999232 | bytes 1024 | tf_op jit(solution)/shard_map/feed_forward_back/pallas_call | solution.py:290
  381.9 18.9 %feed_forward_back.5 = (f32[1024,640]{1,0:T(8,128)}, bf16[640,2560]{1,0:T(8,128)(2,1)}, f32[8,2560]{1,0:T(8,128)}) custom-call(bf16[1024,640]{1,0:T(8,128)(2,1)} %bitcast.140, bf16[1024,5120]{1,0:T(8,128)(2,1)} %get-tuple-element.46.refs_1_, bf16[640,5120]{1,0:T(8,128)(2,1)} %bitcast.169, bf16[5120,640]{1,0:T(8,128)(2,1)} %bitcast.175, ...), custom_call_target="tpu_custom_call" | custom-call | flops 18699999232 | bytes 1024 | tf_op jit(solution)/shard_map/feed_forward_back/pallas_call | solution.py:290
  418.9 17.1 %attention_back.6 = (f32[2,256,640]{2,1,0:T(8,128)}, bf16[2,256,640]{2,1,0:T(8,128)(2,1)}, bf16[2,256,1920]{2,1,0:T(8,128)(2,1)}, f32[8,640]{1,0:T(8,128)}) custom-call(f32[4,256,640]{2,1,0:T(8,128)} %bitcast.177, bf16[4,256,640]{2,1,0:T(8,128)(2,1)} %maximum_select_fusion.1.refs_1_, f32[4,256,640]{2,1,0:T(8,128)} %get-tuple-element.44.refs_2_, ...), custom_call_target="tpu_custom_call" | custom-call | flops 19800000512 | bytes 1024 | tf_op jit(solution)/shard_map/attention_back/pallas_call | solution.py:393
  438.2 15.9 %attention_back.7 = (f32[2,256,640]{2,1,0:T(8,128)}, bf16[2,256,640]{2,1,0:T(8,128)(2,1)}, bf16[2,256,1920]{2,1,0:T(8,128)(2,1)}, f32[8,640]{1,0:T(8,128)}) custom-call(f32[4,256,640]{2,1,0:T(8,128)} %bitcast.178, bf16[4,256,640]{2,1,0:T(8,128)(2,1)} %maximum_select_fusion.1.refs_1_, f32[4,256,640]{2,1,0:T(8,128)} %get-tuple-element.44.refs_2_, ...), custom_call_target="tpu_custom_call" | custom-call | flops 19800000512 | bytes 1024 | tf_op jit(solution)/shard_map/attention_back/pallas_call | solution.py:393
  464.8 9.7 %projection_gradients.1 = bf16[640,2688]{1,0:T(8,128)(2,1)} custom-call(bf16[1024,640]{1,0:T(8,128)(2,1)} %bitcast.185, bf16[1024,1920]{1,0:T(8,128)(2,1)} %bitcast.132, bf16[1024,640]{1,0:T(8,128)(2,1)} %bitcast.184, bf16[1024,640]{1,0:T(8,128)(2,1)} %bitcast.141, f32[640,128]{1,0:T(8,128)} %pad.9.refs_4_, bf16[4,40,2560]{2,1,0:T(8,128)(2,1)} %collective-permute-done.37.refs_5_), custom_call_target="tpu_custom_call" | custom-call | flops 9900000256 | bytes 1024 | tf_op jit(solution)/shard_map/projection_gradients/pallas_call | solution.py:423
  491.2 9.6 %collective-permute-done.48 = bf16[40,2560]{1,0:T(8,128)(2,1)S(1)} collective-permute-done((bf16[40,2560]{1,0:T(8,128)(2,1)S(1)}, bf16[40,2560]{1,0:T(8,128)(2,1)S(1)}, u32[]{:S(2)}, u32[]{:S(2)}) %collective-permute-start.48) | collective-permute-done | bytes 204832 | tf_op jit(solution)/shard_map/ppermute | solution.py:473
  508.9 18.0 %collective-permute-done.41 = bf16[40,2560]{1,0:T(8,128)(2,1)S(1)} collective-permute-done((bf16[40,2560]{1,0:T(8,128)(2,1)S(1)}, bf16[40,2560]{1,0:T(8,128)(2,1)S(1)}, u32[]{:S(2)}, u32[]{:S(2)}) %collective-permute-start.41) | collective-permute-done | bytes 204832 | tf_op jit(solution)/shard_map/ppermute | solution.py:473
  539.9 9.8 %collective-permute-done.44 = bf16[40,2688]{1,0:T(8,128)(2,1)S(1)} collective-permute-done((bf16[40,2688]{1,0:T(8,128)(2,1)S(1)}, bf16[40,2688]{1,0:T(8,128)(2,1)S(1)}, u32[]{:S(2)}, u32[]{:S(2)}) %collective-permute-start.44) | collective-permute-done | bytes 215072 | tf_op jit(solution)/shard_map/ppermute | solution.py:473
  (225 shorter events, 112.7 us)
Async XLA Ops:
  7.2 141.3 %all-gather.2.cloned.1.call-start = ((), (), s32[]{:S(2)}) async-start(), calls=%async_computation.1 | async-start | bytes 3655680 | tf_op jit(solution)/shard_map/all_gather | solution.py:548
  10.6 543.4 %reduce-scatter.2.cloned.1.call-start = ((), (), s32[]{:S(2)}) async-start(), calls=%async_computation.2 | async-start | bytes 6963200 | tf_op jit(solution)/shard_map/reduce_scatter | solution.py:591
  10.6 18.5 %collective-permute-start.2 = (bf16[40,5120]{1,0:T(8,128)(2,1)}, bf16[40,5120]{1,0:T(8,128)(2,1)S(1)}, u32[]{:S(2)}, u32[]{:S(2)}) collective-permute-start(bf16[40,5120]{1,0:T(8,128)(2,1)} %bitcast.151), channel_id=1, source_target_pairs={{0,12},{1,13},{2,14},{3,15},{4,0},{5,1},{6,2},{7,3},{8,4},{9,5},{1... | collective-permute-start | bytes 1228808 | tf_op jit(solution)/shard_map/ppermute | solution.py:473
  15.7 42.1 %collective-permute-start.1 = (bf16[40,5120]{1,0:T(8,128)(2,1)}, bf16[40,5120]{1,0:T(8,128)(2,1)S(1)}, u32[]{:S(2)}, u32[]{:S(2)}) collective-permute-start(bf16[40,5120]{1,0:T(8,128)(2,1)} %bitcast.152), channel_id=1, source_target_pairs={{0,8},{1,9},{2,10},{3,11},{4,12},{5,13},{6,14},{7,15},{8,0},{9,1},... | collective-permute-start | bytes 1228808 | tf_op jit(solution)/shard_map/ppermute | solution.py:473
  15.8 43.6 %collective-permute-start = (bf16[40,5120]{1,0:T(8,128)(2,1)}, bf16[40,5120]{1,0:T(8,128)(2,1)S(1)}, u32[]{:S(2)}, u32[]{:S(2)}) collective-permute-start(bf16[40,5120]{1,0:T(8,128)(2,1)} %bitcast.153), channel_id=1, source_target_pairs={{0,4},{1,5},{2,6},{3,7},{4,8},{5,9},{6,10},{7,11},{8,12},{9,13},{1... | collective-permute-start | bytes 1228808 | tf_op jit(solution)/shard_map/ppermute | solution.py:473
  16.8 42.6 %collective-permute-start.4 = (bf16[40,5120]{1,0:T(8,128)(2,1)}, bf16[40,5120]{1,0:T(8,128)(2,1)S(1)}, u32[]{:S(2)}, u32[]{:S(2)}) collective-permute-start(bf16[40,5120]{1,0:T(8,128)(2,1)} %bitcast.154), channel_id=1, source_target_pairs={{0,2},{1,3},{2,0},{3,1},{4,6},{5,7},{6,4},{7,5},{8,10},{9,11},{10,... | collective-permute-start | bytes 1228808 | tf_op jit(solution)/shard_map/ppermute | solution.py:473
  18.3 41.7 %collective-permute-start.8 = (bf16[40,5120]{1,0:T(8,128)(2,1)}, bf16[40,5120]{1,0:T(8,128)(2,1)S(1)}, u32[]{:S(2)}, u32[]{:S(2)}) collective-permute-start(bf16[40,5120]{1,0:T(8,128)(2,1)} %bitcast.155), channel_id=1, source_target_pairs={{0,1},{1,0},{2,3},{3,2},{4,5},{5,4},{6,7},{7,6},{8,9},{9,8},{10,11... | collective-permute-start | bytes 1228808 | tf_op jit(solution)/shard_map/ppermute | solution.py:473
  29.2 30.8 %collective-permute-start.22 = (bf16[320,640]{1,0:T(8,128)(2,1)}, bf16[320,640]{1,0:T(8,128)(2,1)S(1)}, u32[]{:S(2)}, u32[]{:S(2)}) collective-permute-start(bf16[320,640]{1,0:T(8,128)(2,1)} %bitcast.158), channel_id=1, source_target_pairs={{0,1},{1,0},{2,3},{3,2},{4,5},{5,4},{6,7},{7,6},{8,9},{9,8},{10,11... | collective-permute-start | bytes 1228808 | tf_op jit(solution)/shard_map/ppermute | solution.py:473
  57.8 20.6 %collective-permute-start.3 = (bf16[320,640]{1,0:T(8,128)(2,1)}, bf16[320,640]{1,0:T(8,128)(2,1)S(1)}, u32[]{:S(2)}, u32[]{:S(2)}) collective-permute-start(bf16[320,640]{1,0:T(8,128)(2,1)} %bitcast.159), channel_id=1, source_target_pairs={{0,2},{1,3},{2,0},{3,1},{4,6},{5,7},{6,4},{7,5},{8,10},{9,11},{10,... | collective-permute-start | bytes 1228808 | tf_op jit(solution)/shard_map/ppermute | solution.py:473
  59.4 19.1 %collective-permute-start.12 = (bf16[40,5120]{1,0:T(8,128)(2,1)S(1)}, bf16[40,5120]{1,0:T(8,128)(2,1)S(1)}, u32[]{:S(2)}, u32[]{:S(2)}) collective-permute-start(bf16[40,5120]{1,0:T(8,128)(2,1)S(1)} %collective-permute-done.4.refs_5_), channel_id=1, source_target_pairs={{0,1},{1,0},{2,3},{3,2},{4,5},{5,4},{6,7},{7,6},{8,9},{9,8},{10,11... | collective-permute-start | bytes 1228808 | tf_op jit(solution)/shard_map/ppermute | solution.py:473
  59.4 19.8 %collective-permute-start.11 = (bf16[40,5120]{1,0:T(8,128)(2,1)S(1)}, bf16[40,5120]{1,0:T(8,128)(2,1)S(1)}, u32[]{:S(2)}, u32[]{:S(2)}) collective-permute-start(bf16[40,5120]{1,0:T(8,128)(2,1)S(1)} %collective-permute-done.2.refs_7_.refs_4_), channel_id=1, source_target_pairs={{0,1},{1,0},{2,3},{3,2},{4,5},{5,4},{6,7},{7,6},{8,9},{9,8},{10,11... | collective-permute-start | bytes 1228808 | tf_op jit(solution)/shard_map/ppermute | solution.py:473
  59.9 20.2 %collective-permute-start.16 = (bf16[320,640]{1,0:T(8,128)(2,1)}, bf16[320,640]{1,0:T(8,128)(2,1)S(1)}, u32[]{:S(2)}, u32[]{:S(2)}) collective-permute-start(bf16[320,640]{1,0:T(8,128)(2,1)} %bitcast.160), channel_id=1, source_target_pairs={{0,4},{1,5},{2,6},{3,7},{4,8},{5,9},{6,10},{7,11},{8,12},{9,13},{1... | collective-permute-start | bytes 1228808 | tf_op jit(solution)/shard_map/ppermute | solution.py:473
  60.0 27.2 %collective-permute-start.7 = (bf16[40,5120]{1,0:T(8,128)(2,1)S(1)}, bf16[40,5120]{1,0:T(8,128)(2,1)S(1)}, u32[]{:S(2)}, u32[]{:S(2)}) collective-permute-start(bf16[40,5120]{1,0:T(8,128)(2,1)S(1)} %collective-permute-done.2.refs_7_.refs_4_), channel_id=1, source_target_pairs={{0,2},{1,3},{2,0},{3,1},{4,6},{5,7},{6,4},{7,5},{8,10},{9,11},{10,... | collective-permute-start | bytes 1228808 | tf_op jit(solution)/shard_map/ppermute | solution.py:473
  96.5 19.4 %collective-permute-start.17 = (bf16[320,640]{1,0:T(8,128)(2,1)}, bf16[320,640]{1,0:T(8,128)(2,1)}, u32[]{:S(2)}, u32[]{:S(2)}) collective-permute-start(bf16[320,640]{1,0:T(8,128)(2,1)} %bitcast.162), channel_id=1, source_target_pairs={{0,8},{1,9},{2,10},{3,11},{4,12},{5,13},{6,14},{7,15},{8,0},{9,1},... | collective-permute-start | bytes 1228808 | tf_op jit(solution)/shard_map/ppermute | solution.py:473
  104.9 20.6 %collective-permute-start.19 = (bf16[320,640]{1,0:T(8,128)(2,1)S(1)}, bf16[320,640]{1,0:T(8,128)(2,1)}, u32[]{:S(2)}, u32[]{:S(2)}) collective-permute-start(bf16[320,640]{1,0:T(8,128)(2,1)S(1)} %collective-permute-done.16.refs_4_.refs_2_), channel_id=1, source_target_pairs={{0,2},{1,3},{2,0},{3,1},{4,6},{5,7},{6,4},{7,5},{8,10},{9,11},{10,... | collective-permute-start | bytes 1228808 | tf_op jit(solution)/shard_map/ppermute | solution.py:473
  106.2 19.2 %collective-permute-start.13 = (bf16[40,5120]{1,0:T(8,128)(2,1)}, bf16[40,5120]{1,0:T(8,128)(2,1)}, u32[]{:S(2)}, u32[]{:S(2)}) collective-permute-start(bf16[40,5120]{1,0:T(8,128)(2,1)} %collective-permute-done.5.refs_6_), channel_id=1, source_target_pairs={{0,1},{1,0},{2,3},{3,2},{4,5},{5,4},{6,7},{7,6},{8,9},{9,8},{10,11... | collective-permute-start | bytes 1228808 | tf_op jit(solution)/shard_map/ppermute | solution.py:473
  115.9 17.9 %collective-permute-start.21 = (bf16[320,640]{1,0:T(8,128)(2,1)}, bf16[320,640]{1,0:T(8,128)(2,1)}, u32[]{:S(2)}, u32[]{:S(2)}) collective-permute-start(bf16[320,640]{1,0:T(8,128)(2,1)} %collective-permute-done.17.refs_5_.refs_3_), channel_id=1, source_target_pairs={{0,2},{1,3},{2,0},{3,1},{4,6},{5,7},{6,4},{7,5},{8,10},{9,11},{10,... | collective-permute-start | bytes 1228808 | tf_op jit(solution)/shard_map/ppermute | solution.py:473
  117.9 22.3 %collective-permute-start.23 = (bf16[320,640]{1,0:T(8,128)(2,1)S(1)}, bf16[320,640]{1,0:T(8,128)(2,1)S(1)}, u32[]{:S(2)}, u32[]{:S(2)}) collective-permute-start(bf16[320,640]{1,0:T(8,128)(2,1)S(1)} %collective-permute-done.16.refs_4_.refs_2_), channel_id=1, source_target_pairs={{0,1},{1,0},{2,3},{3,2},{4,5},{5,4},{6,7},{7,6},{8,9},{9,8},{10,11... | collective-permute-start | bytes 1228808 | tf_op jit(solution)/shard_map/ppermute | solution.py:473
  117.9 22.3 %collective-permute-start.24 = (bf16[320,640]{1,0:T(8,128)(2,1)}, bf16[320,640]{1,0:T(8,128)(2,1)S(1)}, u32[]{:S(2)}, u32[]{:S(2)}) collective-permute-start(bf16[320,640]{1,0:T(8,128)(2,1)} %collective-permute-done.17.refs_5_.refs_3_), channel_id=1, source_target_pairs={{0,1},{1,0},{2,3},{3,2},{4,5},{5,4},{6,7},{7,6},{8,9},{9,8},{10,11... | collective-permute-start | bytes 1228808 | tf_op jit(solution)/shard_map/ppermute | solution.py:473
  198.3 18.4 %collective-permute-start.31 = (bf16[2,256,640]{2,1,0:T(8,128)(2,1)S(1)}, bf16[2,256,640]{2,1,0:T(8,128)(2,1)S(1)}, u32[]{:S(2)}, u32[]{:S(2)}) collective-permute-start(bf16[2,256,640]{2,1,0:T(8,128)(2,1)S(1)} %bitcast.150), channel_id=1, source_target_pairs={{0,16},{1,17},{2,18},{3,19},{4,20},{5,21},{6,22},{7,23},{8,24},{9,... | collective-permute-start | bytes 1966088 | tf_op jit(solution)/shard_map/ppermute | solution.py:575
  201.8 28.7 %collective-permute-start.30 = (bf16[2,256,640]{2,1,0:T(8,128)(2,1)}, bf16[2,256,640]{2,1,0:T(8,128)(2,1)S(1)}, u32[]{:S(2)}, u32[]{:S(2)}) collective-permute-start(bf16[2,256,640]{2,1,0:T(8,128)(2,1)} %bitcast.149), channel_id=1, source_target_pairs={{0,16},{1,17},{2,18},{3,19},{4,20},{5,21},{6,22},{7,23},{8,24},{9,... | collective-permute-start | bytes 1966088 | tf_op jit(solution)/shard_map/ppermute | solution.py:575
  314.8 18.6 %collective-permute-start.32 = (bf16[2,256,640]{2,1,0:T(8,128)(2,1)}, bf16[2,256,640]{2,1,0:T(8,128)(2,1)S(1)}, u32[]{:S(2)}, u32[]{:S(2)}) collective-permute-start(bf16[2,256,640]{2,1,0:T(8,128)(2,1)} %attention_back.4), channel_id=1, source_target_pairs={{16,0},{17,1},{18,2},{19,3},{20,4},{21,5},{22,6},{23,7},{24,8},{25... | collective-permute-start | bytes 1966088 | tf_op jit(solution)/shard_map/ppermute | solution.py:587
  332.0 18.5 %collective-permute-start.33 = (bf16[2,256,640]{2,1,0:T(8,128)(2,1)}, bf16[2,256,640]{2,1,0:T(8,128)(2,1)S(1)}, u32[]{:S(2)}, u32[]{:S(2)}) collective-permute-start(bf16[2,256,640]{2,1,0:T(8,128)(2,1)} %attention_back.5), channel_id=1, source_target_pairs={{16,0},{17,1},{18,2},{19,3},{20,4},{21,5},{22,6},{23,7},{24,8},{25... | collective-permute-start | bytes 1966088 | tf_op jit(solution)/shard_map/ppermute | solution.py:587
  413.1 24.3 %collective-permute-start.36 = (bf16[4,40,2560]{2,1,0:T(8,128)(2,1)S(1)}, bf16[4,40,2560]{2,1,0:T(8,128)(2,1)S(1)}, u32[]{:S(2)}, u32[]{:S(2)}) collective-permute-start(bf16[4,40,2560]{2,1,0:T(8,128)(2,1)S(1)} %dynamic-slice_bitcast_fusion.2), channel_id=1, source_target_pairs={{0,2},{1,3},{2,0},{3,1},{4,6},{5,7},{6,4},{7,5},{8,10},{9,11},{10,... | collective-permute-start | bytes 2457608 | tf_op jit(solution)/shard_map/ppermute | solution.py:473
  416.5 48.3 %collective-permute-start.37 = (bf16[4,40,2560]{2,1,0:T(8,128)(2,1)}, bf16[4,40,2560]{2,1,0:T(8,128)(2,1)}, u32[]{:S(2)}, u32[]{:S(2)}) collective-permute-start(bf16[4,40,2560]{2,1,0:T(8,128)(2,1)} %dynamic-slice_bitcast_fusion.1), channel_id=1, source_target_pairs={{0,2},{1,3},{2,0},{3,1},{4,6},{5,7},{6,4},{7,5},{8,10},{9,11},{10,... | collective-permute-start | bytes 2457608 | tf_op jit(solution)/shard_map/ppermute | solution.py:473
  478.8 22.1 %collective-permute-start.48 = (bf16[40,2560]{1,0:T(8,128)(2,1)S(1)}, bf16[40,2560]{1,0:T(8,128)(2,1)S(1)}, u32[]{:S(2)}, u32[]{:S(2)}) collective-permute-start(bf16[40,2560]{1,0:T(8,128)(2,1)S(1)} %get-tuple-element.110), channel_id=1, source_target_pairs={{0,12},{1,13},{2,14},{3,15},{4,0},{5,1},{6,2},{7,3},{8,4},{9,5},{1... | collective-permute-start | bytes 614408 | tf_op jit(solution)/shard_map/ppermute | solution.py:473
  482.6 20.7 %collective-permute-start.47 = (bf16[40,2560]{1,0:T(8,128)(2,1)S(1)}, bf16[40,2560]{1,0:T(8,128)(2,1)S(1)}, u32[]{:S(2)}, u32[]{:S(2)}) collective-permute-start(bf16[40,2560]{1,0:T(8,128)(2,1)S(1)} %get-tuple-element.111), channel_id=1, source_target_pairs={{0,8},{1,9},{2,10},{3,11},{4,12},{5,13},{6,14},{7,15},{8,0},{9,1},... | collective-permute-start | bytes 614408 | tf_op jit(solution)/shard_map/ppermute | solution.py:473
  484.2 24.7 %collective-permute-start.42 = (bf16[40,2560]{1,0:T(8,128)(2,1)S(1)}, bf16[40,2560]{1,0:T(8,128)(2,1)S(1)}, u32[]{:S(2)}, u32[]{:S(2)}) collective-permute-start(bf16[40,2560]{1,0:T(8,128)(2,1)S(1)} %get-tuple-element.112), channel_id=1, source_target_pairs={{0,12},{1,13},{2,14},{3,15},{4,0},{5,1},{6,2},{7,3},{8,4},{9,5},{1... | collective-permute-start | bytes 614408 | tf_op jit(solution)/shard_map/ppermute | solution.py:473
  486.5 40.3 %collective-permute-start.41 = (bf16[40,2560]{1,0:T(8,128)(2,1)S(1)}, bf16[40,2560]{1,0:T(8,128)(2,1)S(1)}, u32[]{:S(2)}, u32[]{:S(2)}) collective-permute-start(bf16[40,2560]{1,0:T(8,128)(2,1)S(1)} %get-tuple-element.113), channel_id=1, source_target_pairs={{0,8},{1,9},{2,10},{3,11},{4,12},{5,13},{6,14},{7,15},{8,0},{9,1},... | collective-permute-start | bytes 614408 | tf_op jit(solution)/shard_map/ppermute | solution.py:473
  489.2 37.7 %collective-permute-start.40 = (bf16[40,2560]{1,0:T(8,128)(2,1)S(1)}, bf16[40,2560]{1,0:T(8,128)(2,1)S(1)}, u32[]{:S(2)}, u32[]{:S(2)}) collective-permute-start(bf16[40,2560]{1,0:T(8,128)(2,1)S(1)} %get-tuple-element.114), channel_id=1, source_target_pairs={{0,4},{1,5},{2,6},{3,7},{4,8},{5,9},{6,10},{7,11},{8,12},{9,13},{1... | collective-permute-start | bytes 614408 | tf_op jit(solution)/shard_map/ppermute | solution.py:473
  500.9 26.1 %collective-permute-start.39 = (bf16[4,40,2688]{2,1,0:T(8,128)(2,1)S(1)}, bf16[4,40,2688]{2,1,0:T(8,128)(2,1)S(1)}, u32[]{:S(2)}, u32[]{:S(2)}) collective-permute-start(bf16[4,40,2688]{2,1,0:T(8,128)(2,1)S(1)} %dynamic-slice_bitcast_fusion), channel_id=1, source_target_pairs={{0,2},{1,3},{2,0},{3,1},{4,6},{5,7},{6,4},{7,5},{8,10},{9,11},{10,... | collective-permute-start | bytes 2580488 | tf_op jit(solution)/shard_map/ppermute | solution.py:473
  531.2 18.5 %collective-permute-start.44 = (bf16[40,2688]{1,0:T(8,128)(2,1)S(1)}, bf16[40,2688]{1,0:T(8,128)(2,1)S(1)}, u32[]{:S(2)}, u32[]{:S(2)}) collective-permute-start(bf16[40,2688]{1,0:T(8,128)(2,1)S(1)} %get-tuple-element.108), channel_id=1, source_target_pairs={{0,8},{1,9},{2,10},{3,11},{4,12},{5,13},{6,14},{7,15},{8,0},{9,1},... | collective-permute-start | bytes 645128 | tf_op jit(solution)/shard_map/ppermute | solution.py:473
  (57 other events, 1153.4 us)
Sparse Core Ops, SparseCore 0:
  10.7 78.9 all-gather.1
  408.4 114.8 reduce-scatter.1

commit v3 on v2

--- a/solution.py
+++ b/solution.py
@@ -49,14 +49,14 @@
     return back, jnp.sum(grad * hat, axis=0, keepdims=True), jnp.sum(grad, axis=0, keepdims=True)
 
 
-def attn_fwd_body(save, len_ref, h_ref, wqkv_ref, vec_ref, *outs):
+def attn_fwd_body(save, first_window, len_ref, h_ref, wqkv_ref, vec_ref, *outs):
     if save:
         m_ref, c_ref, qkv_ref, e_ref, o_ref, a_ref, inv_ref = outs
     else:
         m_ref, c_ref = outs
     width = h_ref.shape[2]
     seq = h_ref.shape[1]
-    length = len_ref[pl.program_id(0)]
+    length = len_ref[pl.program_id(0) + first_window]
     h = h_ref[0].astype(F32)
     vec = vec_ref[...]
     a = normed(h, vec[0:1], vec[2:3]).astype(BF16)
@@ -107,26 +107,28 @@
     return pl.BlockSpec(shape, lambda *_: (0,) * len(shape))
 
 
-def attn_fwd(h, lengths, proj, vec, save, after=()):
-    n, seq, width = h.shape
-    row = lambda *tail: pl.BlockSpec((1,) + tail, lambda i, *_: (i,) + (0,) * len(tail))
+def attn_fwd(h, lengths, proj, vec, save, at=0, parts=1, earlier=(), after=()):
+    count, seq, width = h.shape
+    n = count * parts
+    row = lambda *tail: pl.BlockSpec((1,) + tail, lambda i, *_: (i + at * count,) + (0,) * len(tail))
     shapes = [((seq, width), F32), ((seq, width), BF16)]
     if save:
         shapes += [((seq, 3 * width), BF16), ((HEADS, seq, seq), BF16), ((seq, width), BF16), ((seq, width), BF16), ((seq, width), F32)]
-    waits = len(after)
-    return pl.pallas_call(
-        lambda *refs: attn_fwd_body(save, *refs[:4], *refs[4 + waits:]),
+    waits = len(earlier) + len(after)
+    return pl.pallas_call(
+        lambda *refs: attn_fwd_body(save, at * count, *refs[:4], *refs[4 + waits:]),
         grid_spec=pltpu.PrefetchScalarGridSpec(
             num_scalar_prefetch=1,
-            grid=(n,),
-            in_specs=[row(seq, width), whole(proj.shape), whole(vec.shape)] + tied(waits),
+            grid=(count,),
+            in_specs=[pl.BlockSpec((1, seq, width), lambda i, *_: (i, 0, 0)), whole(proj.shape), whole(vec.shape)] + tied(waits),
             out_specs=[row(*s) for s, _ in shapes],
         ),
         out_shape=[jax.ShapeDtypeStruct((n,) + s, d) for s, d in shapes],
-        compiler_params=pltpu.CompilerParams(vmem_limit_bytes=VMEM_LIMIT),
-        cost_estimate=cost(7 * n),
+        input_output_aliases={4 + i: i for i in range(len(earlier))},
+        compiler_params=pltpu.CompilerParams(vmem_limit_bytes=VMEM_LIMIT),
+        cost_estimate=cost(4.5 * count),
         name="attention_forward",
-    )(lengths, h, proj, vec, *after)
+    )(lengths, h, proj, vec, *earlier, *after)
 
 
 def mlp_fwd_body(save, rows, c_ref, m_ref, wup_ref, wdown_ref, bup_ref, vec_ref, *outs):
@@ -172,7 +174,7 @@
         out_shape=outs,
         scratch_shapes=[pltpu.VMEM((n, width), F32)],
         compiler_params=pltpu.CompilerParams(vmem_limit_bytes=VMEM_LIMIT),
-        cost_estimate=cost(38),
+        cost_estimate=cost(26),
         name="feed_forward",
     )(c, m, wup, wdown, bup, vec)
 
@@ -194,7 +196,7 @@
         out_specs=pl.BlockSpec((n, chunk), lambda i: (0, i)),
         out_shape=jax.ShapeDtypeStruct((n, ff), BF16),
         compiler_params=pltpu.CompilerParams(vmem_limit_bytes=VMEM_LIMIT),
-        cost_estimate=cost(0.027 * n),
+        cost_estimate=cost(0.0125 * n),
         name="feed_forward_up",
     )(c, wup, bup, *after)
 
@@ -226,100 +228,102 @@
         out_shape=jax.ShapeDtypeStruct((rows, width), BF16),
         scratch_shapes=[pltpu.VMEM((rows, width), F32)],
         compiler_params=pltpu.CompilerParams(vmem_limit_bytes=VMEM_LIMIT),
-        cost_estimate=cost(6),
+        cost_estimate=cost(0.017 * rows),
         name="feed_forward_down",
     )(g, m, wdown, vec, *after)
 
 
-def mlp_bwd_body(grads, rows, base_ref, dz_ref, gp_ref, wup_ref, wdown_ref, *rest):
-    if grads:
-        c_ref, dc_ref, gup_ref, gbu_ref, du_ref, ct_ref = rest
-    else:
-        dc_ref, = rest
-    step = pl.program_id(0)
-    n, width = dz_ref.shape
-
-    @pl.when(step == 0)
+def mlp_bwd_body(save, rows, dz_ref, gp_ref, wup_ref, wdown_ref, dc_ref, *outs):
+    @pl.when(pl.program_id(0) == 0)
     def _():
-        dc_ref[...] = jnp.zeros_like(dc_ref) if base_ref is None else base_ref[...]
-        if grads:
-            ct_ref[:width] = c_ref[...].T
-            ct_ref[width:] = jnp.ones_like(ct_ref[width:])
-
-    for r in range(n // rows):
+        dc_ref[...] = jnp.zeros_like(dc_ref)
+
+    for r in range(dz_ref.shape[0] // rows):
         at = slice(r * rows, r * rows + rows)
         dg = dot(dz_ref[at], wdown_ref[...], ((1,), (1,)))
         du = (dg * gp_ref[at].astype(F32)).astype(BF16)
-        if grads:
-            du_ref[at] = du
+        if save:
+            outs[0][at] = du
         dc_ref[at] += dot(du, wup_ref[...], ((1,), (1,)))
-    if grads:
-        gup = dot(ct_ref[...], du_ref[...])
-        gup_ref[...] = gup[:width].astype(BF16)
-        gbu_ref[...] = gup[width:width + 8]
-
-
-def mlp_bwd(dz, gp, wup, wdown, c=None, at=0, parts=1, carry=None, after=(), chunk=1280, rows=256):
+
+
+def mlp_bwd(dz, gp, wup, wdown, save, at=0, parts=1, earlier=(), after=(), chunk=1280, rows=256):
     n, width = dz.shape
-    ff = wup.shape[1] // parts
-    first = at * ff // chunk
-    grads = c is not None
-    args = [dz, gp, wup, wdown]
-    in_specs = [whole(dz.shape), pl.BlockSpec((n, chunk), lambda i: (0, i + first)), pl.BlockSpec((width, chunk), lambda i: (0, i + first)),
-                pl.BlockSpec((chunk, width), lambda i: (i + first, 0))]
-    outs = [jax.ShapeDtypeStruct((n, width), F32)]
-    specs = [whole((n, width))]
-    scratch = []
-    if grads:
-        args += [c]
-        in_specs += [whole(c.shape)]
-        outs += [jax.ShapeDtypeStruct((width, ff), BF16), jax.ShapeDtypeStruct((8, ff), F32)]
-        specs += [pl.BlockSpec((width, chunk), lambda i: (0, i)), pl.BlockSpec((8, chunk), lambda i: (0, i))]
-        scratch = [pltpu.VMEM((n, chunk), BF16), pltpu.VMEM((width + 16, n), BF16)]
-    if carry is not None:
-        args += [carry]
-        in_specs += [whole(carry.shape)]
-    used, waits = len(args), len(after)
-    args += after
-    in_specs += tied(waits)
-
-    def body(*refs):
-        base = refs[used - 1] if carry is not None else None
-        mlp_bwd_body(grads, rows, base, *refs[:5 if grads else 4], *refs[used + waits:])
-
-    return pl.pallas_call(
-        body,
+    ff = wup.shape[1]
+    args = [dz, gp, wup, wdown, *earlier, *after]
+    outs = [jax.ShapeDtypeStruct((n * parts, width), F32)]
+    specs = [pl.BlockSpec((n, width), lambda i: (at, 0))]
+    if save:
+        outs += [jax.ShapeDtypeStruct((n * parts, ff), BF16)]
+        specs += [pl.BlockSpec((n, chunk), lambda i: (at, i))]
+    return pl.pallas_call(
+        lambda *refs: mlp_bwd_body(save, rows, *refs[:4], *refs[len(args):]),
         grid=(ff // chunk,),
-        in_specs=in_specs,
+        in_specs=[whole(dz.shape), pl.BlockSpec((n, chunk), lambda i: (at, i)), pl.BlockSpec((width, chunk), lambda i: (0, i)),
+                  pl.BlockSpec((chunk, width), lambda i: (i, 0))] + tied(len(args) - 4),
         out_specs=specs,
         out_shape=outs,
-        scratch_shapes=scratch,
-        compiler_params=pltpu.CompilerParams(vmem_limit_bytes=VMEM_LIMIT),
-        cost_estimate=cost((34 if grads else 26) / parts),
+        input_output_aliases={4 + i: i for i in range(len(earlier))},
+        compiler_params=pltpu.CompilerParams(vmem_limit_bytes=VMEM_LIMIT),
+        cost_estimate=cost(22 / parts),
         name="feed_forward_back",
     )(*args)
 
 
+def up_grad_body(c_ref, order_ref, du_ref, keep_ref, send_ref, sum_ref, ct_ref):
+    half = keep_ref.shape[0]
+
+    @pl.when(pl.program_id(0) == 0)
+    def _():
+        ct_ref[:2 * half] = dot(order_ref[...], c_ref[...], ((1,), (1,))).astype(BF16)
+        ct_ref[2 * half:] = jnp.ones_like(ct_ref[2 * half:])
+
+    grad = dot(ct_ref[...], du_ref[...])
+    keep_ref[...] = grad[:half].astype(BF16)
+    send_ref[...] = grad[half:2 * half].astype(BF16)
+    sum_ref[...] = grad[2 * half:2 * half + 8]
+
+
+def up_grad(c, order, du, at, parts, after=(), chunk=1280):
+    n, width = c.shape
+    ff = du.shape[1] // parts
+    first = at * ff // chunk
+    waits = len(after)
+    column = lambda rows: pl.BlockSpec((rows, chunk), lambda i: (0, i))
+    return pl.pallas_call(
+        lambda *refs: up_grad_body(*refs[:3], *refs[3 + waits:]),
+        grid=(ff // chunk,),
+        in_specs=[whole(c.shape), whole(order.shape), pl.BlockSpec((n, chunk), lambda i: (0, i + first))] + tied(waits),
+        out_specs=[column(width // 2), column(width // 2), column(8)],
+        out_shape=[jax.ShapeDtypeStruct((width // 2, ff), BF16)] * 2 + [jax.ShapeDtypeStruct((8, ff), F32)],
+        scratch_shapes=[pltpu.VMEM((width + 16, n), BF16)],
+        compiler_params=pltpu.CompilerParams(vmem_limit_bytes=VMEM_LIMIT),
+        cost_estimate=cost(13 / parts),
+        name="up_gradient",
+    )(c, order, du, *after)
+
+
 def down_grad_body(g_ref, dz_ref, out_ref):
     out_ref[...] = dot(g_ref[...], dz_ref[...], ((0,), (0,))).astype(BF16)
 
 
-def down_grad(g, dz, chunk=1280):
+def down_grad(g, dz, after=(), chunk=1280):
     n, ff = g.shape
     width = dz.shape[1]
-    return pl.pallas_call(
-        down_grad_body,
+    waits = len(after)
+    return pl.pallas_call(
+        lambda *refs: down_grad_body(*refs[:2], *refs[2 + waits:]),
         grid=(ff // chunk,),
-        in_specs=[pl.BlockSpec((n, chunk), lambda i: (0, i)), whole(dz.shape)],
+        in_specs=[pl.BlockSpec((n, chunk), lambda i: (0, i)), whole(dz.shape)] + tied(waits),
         out_specs=pl.BlockSpec((chunk, width), lambda i: (i, 0)),
         out_shape=jax.ShapeDtypeStruct((ff, width), BF16),
         compiler_params=pltpu.CompilerParams(vmem_limit_bytes=VMEM_LIMIT),
-        cost_estimate=cost(10),
+        cost_estimate=cost(12),
         name="down_gradient",
-    )(g, dz)
-
-
-def attn_bwd_body(grads, dc_ref, dz_ref, m_ref, h_ref, qkv_ref, e_ref, o_ref, inv_ref, proj_ref, vec_ref, dh_ref, *outs):
+    )(g, dz, *after)
+
+
+def attn_bwd_body(grads, base_ref, dc_ref, dz_ref, m_ref, h_ref, qkv_ref, e_ref, o_ref, inv_ref, proj_ref, vec_ref, dh_ref, *outs):
     if grads:
         dr_ref, dqkv_ref, small_ref = outs
     width = h_ref.shape[2]
@@ -328,7 +332,7 @@
     if grads:
         @pl.when(pl.program_id(0) == 0)
         def _():
-            small_ref[...] = jnp.zeros_like(small_ref)
+            small_ref[...] = jnp.zeros_like(small_ref) if base_ref is None else base_ref[...]
 
     dz = dz_ref[0].astype(F32)
     back, g_gain1, g_shift1 = norm_back(m_ref[0], vec[1:2], dc_ref[0])
@@ -379,58 +383,80 @@
         [g_gain0, g_gain1, g_shift0, g_shift1, total(dqkv[:, :width]), total(dqkv[:, 2 * width:]), total(dr), total(dz)], axis=0)
 
 
-def attn_bwd(dc, dz, m, h, qkv, e, o, inv, proj, vec, at, parts, grads, after=()):
+def attn_bwd(dc, dz, m, h, qkv, e, o, inv, proj, vec, at, parts, grads, earlier=(), after=()):
     n, seq, width = h.shape
-    n //= parts
-    row = lambda *tail: pl.BlockSpec((1,) + tail, lambda i: (i + at * n,) + (0,) * len(tail))
-    out = lambda *tail: pl.BlockSpec((1,) + tail, lambda i: (i,) + (0,) * len(tail))
-    shapes = [((seq, width), F32), ((seq, width), BF16), ((seq, 3 * width), BF16)]
-    specs = [out(*s) for s, _ in shapes] + [whole((8, width))]
-    results = [jax.ShapeDtypeStruct((n,) + s, d) for s, d in shapes] + [jax.ShapeDtypeStruct((8, width), F32)]
-    if not grads:
-        specs, results = specs[:1], [jax.ShapeDtypeStruct((n, seq, width), BF16)]
-    waits = len(after)
-    return pl.pallas_call(
-        lambda *refs: attn_bwd_body(grads, *refs[:10], *refs[10 + waits:]),
-        grid=(n,),
-        in_specs=[row(seq, width), row(seq, width), row(seq, width), row(seq, width), row(seq, 3 * width), row(HEADS, seq, seq), row(seq, width), row(seq, width),
-                  whole(proj.shape), whole(vec.shape)] + tied(waits),
+    count = n // parts
+    row = lambda *tail: pl.BlockSpec((1,) + tail, lambda i: (i + at * count,) + (0,) * len(tail))
+    if grads:
+        shapes = [((seq, width), F32), ((seq, width), BF16), ((seq, 3 * width), BF16)]
+        specs = [row(*s) for s, _ in shapes] + [whole((8, width))]
+        results = [jax.ShapeDtypeStruct((n,) + s, d) for s, d in shapes] + [jax.ShapeDtypeStruct((8, width), F32)]
+    else:
+        specs = [pl.BlockSpec((1, seq, width), lambda i: (i, 0, 0))]
+        results = [jax.ShapeDtypeStruct((count, seq, width), BF16)]
+    args = [dc, dz, m, h, qkv, e, o, inv, proj, vec]
+    in_specs = [row(seq, width), row(seq, width), row(seq, width), row(seq, width), row(seq, 3 * width), row(HEADS, seq, seq),
+                row(seq, width), row(seq, width), whole(proj.shape), whole(vec.shape)]
+    base = len(args)
+    if earlier:
+        args += [earlier[3], *earlier[:3]]
+        in_specs += [whole(earlier[3].shape)] + tied(3)
+    aliases = {base + 1 + i: i for i in range(3)} if earlier else {}
+    args += after
+    in_specs += tied(len(after))
+    used = len(args)
+
+    def body(*refs):
+        attn_bwd_body(grads, refs[base] if earlier else None, *refs[:base], *refs[used:])
+
+    return pl.pallas_call(
+        body,
+        grid=(count,),
+        in_specs=in_specs,
         out_specs=specs,
         out_shape=results,
-        compiler_params=pltpu.CompilerParams(vmem_limit_bytes=VMEM_LIMIT),
-        cost_estimate=cost(9 * n),
+        input_output_aliases=aliases,
+        compiler_params=pltpu.CompilerParams(vmem_limit_bytes=VMEM_LIMIT),
+        cost_estimate=cost(7 * count),
         name="attention_back",
-    )(dc, dz, m, h, qkv, e, o, inv, proj, vec, *after)
-
-
-def proj_grad_body(a_ref, dqkv_ref, o_ref, dr_ref, table_ref, out_ref, at_ref):
+    )(*args)
+
+
+def proj_grad_body(a_ref, dqkv_ref, o_ref, dr_ref, table_ref, order_ref, keep_ref, send_ref, at_ref):
     step = pl.program_id(0)
     width = a_ref.shape[1]
+    half = width // 2
+    order = order_ref[...]
+
+    def put(at, value):
+        keep_ref[:, at] = value[:half].astype(BF16)
+        send_ref[:, at] = value[half:].astype(BF16)
 
     @pl.when(step == 0)
     def _():
-        at_ref[...] = a_ref[...].T
-        out_ref[:, 3 * width:4 * width] = dot(o_ref[...], dr_ref[...], ((0,), (0,))).astype(BF16)
-        out_ref[:, 4 * width:] = table_ref[...].astype(BF16)
-
-    out_ref[:, pl.ds(pl.multiple_of(step * width, 128), width)] = dot(at_ref[...], dqkv_ref[...]).astype(BF16)
-
-
-def proj_grad(a, dqkv, o, dr, table, after=()):
+        at_ref[...] = dot(order, a_ref[...], ((1,), (1,))).astype(BF16)
+        put(slice(3 * width, 4 * width), dot(dot(order, o_ref[...], ((1,), (1,))).astype(BF16), dr_ref[...]))
+        put(slice(4 * width, None), dot(order, table_ref[...].astype(BF16)))
+
+    put(pl.ds(pl.multiple_of(step * width, 128), width), dot(at_ref[...], dqkv_ref[...]))
+
+
+def proj_grad(a, dqkv, o, dr, table, order, after=()):
     n, width = a.shape
     waits = len(after)
-    shape = (width, 4 * width + table.shape[1])
-    return pl.pallas_call(
-        lambda *refs: proj_grad_body(*refs[:5], *refs[5 + waits:]),
+    shape = (width // 2, 4 * width + table.shape[1])
+    return pl.pallas_call(
+        lambda *refs: proj_grad_body(*refs[:6], *refs[6 + waits:]),
         grid=(3,),
-        in_specs=[whole(a.shape), pl.BlockSpec((n, width), lambda i: (0, i)), whole(o.shape), whole(dr.shape), whole(table.shape)] + tied(waits),
-        out_specs=whole(shape),
-        out_shape=jax.ShapeDtypeStruct(shape, BF16),
+        in_specs=[whole(a.shape), pl.BlockSpec((n, width), lambda i: (0, i)), whole(o.shape), whole(dr.shape), whole(table.shape),
+                  whole(order.shape)] + tied(waits),
+        out_specs=[whole(shape)] * 2,
+        out_shape=[jax.ShapeDtypeStruct(shape, BF16)] * 2,
         scratch_shapes=[pltpu.VMEM((width, n), BF16)],
         compiler_params=pltpu.CompilerParams(vmem_limit_bytes=VMEM_LIMIT),
         cost_estimate=cost(9),
         name="projection_gradients",
-    )(a, dqkv, o, dr, table, *after)
+    )(a, dqkv, o, dr, table, order, *after)
 
 
 def place_body(count, to_ref, *refs):
@@ -473,10 +499,6 @@
     return lax.ppermute(value, "dp", pairs)
 
 
-def pick(value, index, axis):
-    return lax.dynamic_index_in_dim(value, index, axis, keepdims=False)
-
-
 def behind_me():
     zs, ys, cores = places(lax.axis_size("dp"))
     me = lax.axis_index("dp")
@@ -491,43 +513,46 @@
     return (mine.astype(F32) + got.astype(F32)).astype(BF16)
 
 
-def core_step(grad, rows):
+def scatter_order(shard):
     zs, ys, cores = places(lax.axis_size("dp"))
-    _, _, c = behind_me()
-    parts = grad.reshape(zs, ys, cores, rows, grad.shape[1])
-    return hop(pick(parts, 1 - c, 2), "core"), pick(parts, c, 2)
-
-
-def y_step(parts):
-    _, y, _ = behind_me()
-    return hop(pick(parts, 1 - y, 1), "y"), pick(parts, y, 1)
-
-
-def z_step(parts):
+    z, y, c = behind_me()
+    row = jnp.arange(zs * ys * cores * shard)
+    block = row // shard
+    to = (((z + block % zs) % zs) * ys + (y ^ (block // zs % ys))) * cores + (c ^ (block // (zs * ys)))
+    return (jnp.arange(zs * ys * cores * shard)[None, :] == (to * shard + row % shard)[:, None]).astype(BF16)
+
+
+def y_step(mine, got):
+    half = mine.shape[0] // 2
+    return both(mine[:half], got[:half]), hop(both(mine[half:], got[half:]), "y")
+
+
+def z_step(mine, got):
     zs, _, _ = places(lax.axis_size("dp"))
-    z, _, _ = behind_me()
-    return [hop(pick(parts, (z + step) % zs, 0), "z", step) for step in range(1, zs)], pick(parts, z, 0)
-
-
-def z_total(got, mine):
-    total = mine.astype(F32)
-    for piece in got:
-        total = total + piece.astype(F32)
-    return total
+    rows = mine.shape[0] // zs
+    at = lambda v, k: v[k * rows:k * rows + rows]
+    return [at(mine, 0), at(got, 0)] + [hop(both(at(mine, k), at(got, k)), "z", k) for k in range(1, zs)]
+
+
+def total(terms):
+    out = terms[0].astype(F32)
+    for term in terms[1:]:
+        out = out + term.astype(F32)
+    return out
 
 
 def held(value, *after):
     return lax.optimization_barrier((value, *after))[0]
 
 
-def assemble(line, other, siblings):
+def assemble(line, other, siblings, after=()):
     zs, ys, cores = places(lax.axis_size("dp"))
     z, y, c = behind_me()
     to = []
     for core in (c, 1 - c):
         for row in (y, 1 - y):
             to += [(((z + zs - step) % zs) * ys + row) * cores + core for step in range(zs)]
-    return place(line + other + siblings, jnp.stack(to).astype(jnp.int32))
+    return place(line + other + siblings, jnp.stack(to).astype(jnp.int32), after)
 
 
 def on_device(tokens, lengths, cotangent, w_qkv, w_out, w_up, w_down, norm_gain, norm_bias, bias_vec, up_bias):
@@ -545,72 +570,104 @@
     used = table.shape[1]
     table = jnp.pad(table, ((0, 0), (0, 128 - used)))
     packed = jnp.concatenate([w_qkv[0], w_out[0], table], axis=1)
-    proj = lax.all_gather(packed, "dp", axis=0, tiled=True)
     if by_hand:
-        up_line = along_line(w_up[0])
-        up_other = [hop(piece, "y") for piece in up_line]
-        wup = assemble(up_line, up_other, [hop(piece, "core") for piece in up_line + up_other])
-        own = w_down[0]
-        near = held(own, *up_line[1:])
-        near = [hop(near, "z", step) for step in (1, 3)]
-        far = hop(held(own, near[0]), "z", 2)
-        down_line = [own, near[0], far, near[1]]
-        down_other = [hop(piece, "y") for piece in down_line]
+        up, down = w_up[0], w_down[0]
+        order = scatter_order(shard)
+        proj_1, proj_3, proj_2 = hop(packed, "z", 1), hop(packed, "z", 3), hop(packed, "z", 2)
+        proj_y0, up_y0 = hop(packed, "y"), hop(up, "y")
+        now = (proj_1, proj_2, proj_3, proj_y0)
+        up_1, up_3 = hop(held(up, *now), "z", 1), hop(held(up, *now), "z", 3)
+        proj_y = [hop(held(piece, *now), "y") for piece in (proj_1, proj_2, proj_3)]
+        now = (up_1, up_3, up_y0, *proj_y)
+        up_2 = hop(held(up, *now), "z", 2)
+        up_y1, up_y3 = hop(held(up_1, *now), "y"), hop(held(up_3, *now), "y")
+        line, other = [packed, proj_1, proj_2, proj_3], [proj_y0, *proj_y]
+        proj = assemble(line, other, [hop(held(piece, *now), "core") for piece in line + other])
+        now = (up_2, up_y1, up_y3)
+        down_1, down_3 = hop(held(down, *now), "z", 1), hop(held(down, *now), "z", 3)
+        up_y2, down_y0 = hop(held(up_2, *now), "y"), hop(held(down, *now), "y")
     else:
-        up_line, up_other, down_line, down_other = (), (), (), ()
+        order = (jnp.arange(width)[None, :] == jnp.arange(width)[:, None]).astype(BF16)
+        proj = lax.all_gather(packed, "dp", axis=0, tiled=True)
         wup = lax.all_gather(w_up[0], "dp", axis=0, tiled=True)
         wdown = lax.all_gather(w_down[0], "dp", axis=0, tiled=True)
     small = proj[:, 4 * width:4 * width + used]
     vec = small[:, :8].T.astype(F32)
     bup = small[:, 8:].reshape(1, ff).astype(F32)
 
-    mid, c = attn_fwd(tokens, lengths, proj, vec, False, (*up_line, *down_other[:1]))
-    act = mlp_up(c.reshape(n, width), wup, bup, (*down_line, *down_other[1::2]))
+    mid, c = attn_fwd(tokens, lengths, proj, vec, False)
+    c = c.reshape(n, width)
     if by_hand:
-        wdown = assemble(down_line, down_other, [hop(piece, "core") for piece in down_line + down_other])
+        now = (down_1, down_3, up_y2, down_y0, c)
+        down_2 = hop(held(down, *now), "z", 2)
+        down_y1, down_y3 = hop(held(down_1, *now), "y"), hop(held(down_3, *now), "y")
+        line, other = [up, up_1, up_2, up_3], [up_y0, up_y1, up_y2, up_y3]
+        wup = assemble(line, other, [hop(held(piece, *now), "core") for piece in line + other])
+    act = mlp_up(c, wup, bup)
+    if by_hand:
+        now = (down_2, down_y1, down_y3, act)
+        down_y2 = hop(held(down_2, *now), "y")
+    if by_hand:
+        line, other = [down, down_1, down_2, down_3], [down_y0, down_y1, down_y2, down_y3]
+        wdown = assemble(line, other, [hop(piece, "core") for piece in line + other])
     mid = mid.reshape(n, width)
+    kept = ()
     arrived = []
     for at in range(parts):
         y = mlp_down(act, mid, wdown, vec, at, parts)
         arrived.append(lax.ppermute(y.reshape(part, seq, width), "section", [(0, 1)]))
-    h = jnp.where(section == 0, tokens, jnp.concatenate(arrived))
-
-    m, c, qkv, e, o, a, inv = attn_fwd(h, lengths, proj, vec, True)
+    h = []
+    for at in range(parts):
+        h.append(jnp.where(section == 0, tokens[at * part:at * part + part], held(arrived[at], *kept[:1])))
+        kept = attn_fwd(h[at], lengths, proj, vec, True, at, parts, kept)
+    h = jnp.concatenate(h)
+    m, c, qkv, e, o, a, inv = kept
     c = c.reshape(n, width)
     y, g, gp = mlp_fwd(c, m.reshape(n, width), wup, wdown, bup, vec, True)
 
-    dc, = mlp_bwd(cotangent.reshape(n, width), gp, wup, wdown)
+    dc, = mlp_bwd(cotangent.reshape(n, width), gp, wup, wdown, False)
     dc = dc.reshape(tokens.shape)
     arrived = []
     for at in range(parts):
         back, = attn_bwd(dc, cotangent, m, h, qkv, e, o, inv, proj, vec, at, parts, False)
         arrived.append(lax.ppermute(back, "section", [(1, 0)]))
-    dz = jnp.where(section == 1, cotangent, jnp.concatenate(arrived))
-
+    dz, more = [], ()
+    for at in range(parts):
+        dz.append(jnp.where(section == 1, cotangent[at * part:at * part + part], held(arrived[at], *more[:1])))
+        more = mlp_bwd(dz[at].reshape(part * seq, width), gp, wup, wdown, True, at, parts, more)
+    dz = jnp.concatenate(dz)
+    dc, du = more
+    dc = dc.reshape(tokens.shape)
     g_down = down_grad(g, dz.reshape(n, width))
     sum_down = lax.psum_scatter(g_down, "dp", scatter_dimension=0, tiled=True).astype(F32)
-    flat = dz.reshape(n, width)
-    dc, g_up_a, g_bup_a = mlp_bwd(flat, gp, wup, wdown, c, 0, 2, None, (g_down,))
-    got_a, mine_a = core_step(g_up_a, shard)
-    dc, g_up_b, g_bup_b = mlp_bwd(flat, gp, wup, wdown, c, 1, 2, dc)
-    dc = dc.reshape(tokens.shape)
-    got_b, mine_b = core_step(g_up_b, shard)
-    ya = y_step(both(mine_a, got_a))
-    back_a = attn_bwd(dc, dz, m, h, qkv, e, o, inv, proj, vec, 0, 2, True, (got_a,))
-    yb = y_step(both(mine_b, got_b))
-    za = z_step(both(ya[1], ya[0]))
-    back_b = attn_bwd(dc, dz, m, h, qkv, e, o, inv, proj, vec, 1, 2, True, (back_a[0], got_b, ya[0]))
-    dh, dr, dqkv = [jnp.concatenate([back_a[i], back_b[i]]) for i in range(3)]
-    smalls = back_a[3] + back_b[3]
-    g_bup = jnp.concatenate([g_bup_a[0], g_bup_b[0]])
-    g_table = jnp.concatenate([smalls.T, g_bup.reshape(width, per_row)], axis=1)
+    keep_u, send_u, bup_u = up_grad(c, order, du, 0, 1, (g_down,))
+    if by_hand:
+        got_u = hop(send_u, "core")
+        half = ff // 2
+        mine_a, got_a = y_step(keep_u[:, :half], got_u[:, :half])
+        mine_b, got_b = y_step(keep_u[:, half:], held(got_u[:, half:], got_a))
+        back = attn_bwd(dc, dz, m, h, qkv, e, o, inv, proj, vec, 0, 2, True, (), (got_u,))
+        terms_a = z_step(mine_a, got_a)
+        back = attn_bwd(dc, dz, m, h, qkv, e, o, inv, proj, vec, 1, 2, True, back, (got_a,))
+        terms_b = z_step(mine_b, got_b)
+        wait = (got_b, *terms_a[2:])
+    else:
+        back = attn_bwd(dc, dz, m, h, qkv, e, o, inv, proj, vec, 0, 1, True)
+        wait = ()
+    dh, dr, dqkv, smalls = back
+    g_bup = bup_u[0].reshape(width, per_row)
+    g_table = jnp.concatenate([smalls.T, g_bup], axis=1)
     g_table = jnp.pad(g_table, ((0, 0), (0, 128 - used)))
-    zb = z_step(both(yb[1], yb[0]))
-    g_proj = proj_grad(a.reshape(n, width), dqkv.reshape(n, 3 * width), o.reshape(n, width), dr.reshape(n, width), g_table, (yb[0],))
-    got_p, mine_p = core_step(g_proj, shard)
-    yp = y_step(both(mine_p, got_p))
-    sum_up = jnp.concatenate([z_total(*za), z_total(*zb)], axis=1)
-    sum_proj = z_total(*z_step(held(both(yp[1], yp[0]), *zb[0])))
+    keep_p, send_p = proj_grad(
+        a.reshape(n, width), dqkv.reshape(n, 3 * width), o.reshape(n, width), dr.reshape(n, width), g_table, order, wait)
+    if by_hand:
+        sum_up = jnp.concatenate([total(terms_a), total(terms_b)], axis=1)
+        mine_p, got_p = y_step(keep_p, hop(send_p, "core"))
+        sum_proj = total(z_step(mine_p, held(got_p, *terms_b)))
+    else:
+        scatter = lambda *halves: lax.psum_scatter(jnp.concatenate(halves), "dp", scatter_dimension=0, tiled=True).astype(F32)
+        sum_up = scatter(keep_u, send_u)
+        sum_proj = scatter(keep_p, send_p)
     vectors = sum_proj[:, 4 * width:4 * width + 8].T
     return (
         y.reshape((1,) + tokens.shape),

time: 572 us -> 507 us (0.89)
  the two profiles are of different devices: /device:TPU:0 before, /device:TPU:11 now
where the time goes in v3:
time: 507 us; the launch traced here: 497 us
  Pallas kernels  265 us (52%)
  waiting for transfers between devices  121 us (24%)
  starting transfers between devices  59 us (12%)
  other arithmetic  24.6 us (5%)
  between operations  14.8 us (3%)
  local copies, waits for them, and re-layouts  13.1 us (3%)
    ppermute x59, waiting for transfers between devices, hop(): return lax.ppermute(value, 'dp', pairs)  112 us
    pallas_call x4, Pallas kernels, attn_bwd(): pl.pallas_call(body, grid=(count,), in_specs=in_specs, out_specs=specs, o...  64.9 us
    ppermute x59, starting transfers between devices, hop(): return lax.ppermute(value, 'dp', pairs)  53 us
    pallas_call x3, Pallas kernels, mlp_bwd(): pl.pallas_call(lambda *refs: mlp_bwd_body(save, rows, *refs[:4], *refs[le...  49.4 us
    pallas_call x3, Pallas kernels, attn_fwd(): pl.pallas_call(lambda *refs: attn_fwd_body(save, at * count, *refs[:4], *...  39.4 us
    pallas_call x1, Pallas kernels, mlp_fwd(): pl.pallas_call(lambda *refs: mlp_fwd_body(save, rows, *refs), grid=(ff //...  26.5 us
    pallas_call x2, Pallas kernels, mlp_down(): pl.pallas_call(lambda *refs: mlp_down_body(*refs[:4], *refs[4 + waits:]),...  17.6 us
    pallas_call x3, Pallas kernels, place(): pl.pallas_call(lambda *refs: place_body(count, *refs[:count + 1], *refs[c...  17.2 us
  transfers between devices with their start and end apart: 64, of which 27 were waited for; matrix products, arithmetic and copies ran while one was open for 5% of the time, Pallas kernels for 27%

profile of v3, /device:TPU:11, one launch (start us, length us, event | category | flops | bytes accessed | tf_op | source)
XLA Modules:
  0.0 497.0 jit_solution(18020409082937721323)
XLA Ops:
  16.1 12.9 %collective-permute-done.1.refs_3_ = bf16[40,2688]{1,0:T(8,128)(2,1)S(1)} collective-permute-done((bf16[40,2688]{1,0:T(8,128)(2,1)S(1)}, bf16[40,2688]{1,0:T(8,128)(2,1)S(1)}, u32[]{:S(2)}, u32[]{:S(2)}) %collective-permute-start.1) | collective-permute-done | bytes 215072 | tf_op jit(solution)/shard_map/ppermute | solution.py:499
  39.1 4.7 collective-permute-done.5.refs_7_
  43.9 4.6 collective-permute-done.4.refs_6_
  60.2 4.6 place_pieces.3
  66.6 8.3 %collective-permute-done.18.refs_3_ = bf16[40,5120]{1,0:T(8,128)(2,1)} collective-permute-done((bf16[40,5120]{1,0:T(8,128)(2,1)}, bf16[40,5120]{1,0:T(8,128)(2,1)}, u32[]{:S(2)}, u32[]{:S(2)}) %collective-permute-start.18) | collective-permute-done | bytes 409632 | tf_op jit(solution)/shard_map/ppermute | solution.py:499
  81.7 16.7 %attention_forward.3 = (f32[4,256,640]{2,1,0:T(8,128)}, bf16[4,256,640]{2,1,0:T(8,128)(2,1)}) custom-call(s32[4]{0:T(128)} %refs_0_.5, bf16[4,256,640]{2,1,0:T(8,128)(2,1)} %refs_1_.3, bf16[640,2688]{1,0:T(8,128)(2,1)} %bitcast.72, f32[8,640]{1,0:T(8,128)} %convert_bitcast_fusion.refs_3_.refs_5_.refs_9_), custom_call_target="tpu_custom_call" | custom-call | flops 19800000512 | bytes 1024 | tf_op jit(solution)/shard_map/attention_forward/pallas_call | solution.py:118
  109.4 6.3 %place_pieces.4 = bf16[16,40,5120]{2,1,0:T(8,128)(2,1)} custom-call(s32[16]{0:T(128)} %stack.50.refs_0_, bf16[40,5120]{1,0:T(8,128)(2,1)} %bitcast.90, bf16[40,5120]{1,0:T(8,128)(2,1)} %copy-done.16, bf16[40,5120]{1,0:T(8,128)(2,1)} %collective-permute-done.18.refs_3_, bf16[40,5120]{1,0:T(8,128)(2,1)} %copy-done.17, bf16[40,5120]{1,0:T(8,128)(2,1)} %copy-done.15, ...), custom_call_target="tpu_custom_call" | custom-call | flops 4400000000 | bytes 1024 | tf_op jit(solution)/shard_map/place_pieces/pallas_call | solution.py:474
  115.7 12.9 %feed_forward_up.1.refs_0_ = bf16[1024,5120]{1,0:T(8,128)(2,1)} custom-call(bf16[1024,640]{1,0:T(8,128)(2,1)} %bitcast.119, bf16[640,5120]{1,0:T(8,128)(2,1)} %bitcast.98, f32[1,5120]{1,0:T(1,128)} %reshape.207.refs_2_.refs_4_), custom_call_target="tpu_custom_call" | custom-call | flops 14080000000 | bytes 1024 | tf_op jit(solution)/shard_map/feed_forward_up/pallas_call | solution.py:192
  131.4 8.1 %collective-permute-done.36.refs_7_ = bf16[320,640]{1,0:T(8,128)(2,1)} collective-permute-done((bf16[320,640]{1,0:T(8,128)(2,1)S(1)}, bf16[320,640]{1,0:T(8,128)(2,1)}, u32[]{:S(2)}, u32[]{:S(2)}) %collective-permute-start.36) | collective-permute-done | bytes 409632 | tf_op jit(solution)/shard_map/ppermute | solution.py:499
  143.0 6.3 %place_pieces.5 = bf16[16,320,640]{2,1,0:T(8,128)(2,1)} custom-call(s32[16]{0:T(128)} %stack.50.refs_0_, bf16[320,640]{1,0:T(8,128)(2,1)} %bitcast.92, bf16[320,640]{1,0:T(8,128)(2,1)} %copy-done.18, bf16[320,640]{1,0:T(8,128)(2,1)} %copy-done.28, bf16[320,640]{1,0:T(8,128)(2,1)} %copy-done.19, bf16[320,640]{1,0:T(8,128)(2,1)} %copy-done.20, ...), custom_call_target="tpu_custom_call" | custom-call | flops 4400000000 | bytes 1024 | tf_op jit(solution)/shard_map/place_pieces/pallas_call | solution.py:474
  149.3 8.8 %feed_forward_down.3 = bf16[512,640]{1,0:T(8,128)(2,1)} custom-call(bf16[1024,5120]{1,0:T(8,128)(2,1)} %feed_forward_up.1.refs_0_, f32[1024,640]{1,0:T(8,128)} %bitcast.110, bf16[5120,640]{1,0:T(8,128)(2,1)} %bitcast.103, f32[8,640]{1,0:T(8,128)} %convert_bitcast_fusion.refs_3_.refs_5_.refs_9_), custom_call_target="tpu_custom_call" | custom-call | flops 9574400000 | bytes 1024 | tf_op jit(solution)/shard_map/feed_forward_down/pallas_call | solution.py:222
  159.5 8.8 %feed_forward_down.2 = bf16[512,640]{1,0:T(8,128)(2,1)} custom-call(bf16[1024,5120]{1,0:T(8,128)(2,1)} %feed_forward_up.1.refs_0_, f32[1024,640]{1,0:T(8,128)} %bitcast.111, bf16[5120,640]{1,0:T(8,128)(2,1)} %bitcast.104, f32[8,640]{1,0:T(8,128)} %convert_bitcast_fusion.refs_3_.refs_5_.refs_9_), custom_call_target="tpu_custom_call" | custom-call | flops 9574400000 | bytes 1024 | tf_op jit(solution)/shard_map/feed_forward_down/pallas_call | solution.py:222
  170.1 6.6 %collective-permute-done.46 = bf16[2,256,640]{2,1,0:T(8,128)(2,1)S(1)} collective-permute-done((bf16[2,256,640]{2,1,0:T(8,128)(2,1)}, bf16[2,256,640]{2,1,0:T(8,128)(2,1)S(1)}, u32[]{:S(2)}, u32[]{:S(2)}) %collective-permute-start.46) | collective-permute-done | bytes 655392 | tf_op jit(solution)/shard_map/ppermute | solution.py:618
  177.6 11.4 %attention_forward.4 = (f32[4,256,640]{2,1,0:T(8,128)}, bf16[4,256,640]{2,1,0:T(8,128)(2,1)}, bf16[4,256,1920]{2,1,0:T(8,128)(2,1)}, bf16[4,20,256,256]{3,2,1,0:...) custom-call(s32[4]{0:T(128)} %refs_0_.5, ...), custom_call_target="tpu_custom_call" | custom-call | flops 9900000256 | bytes 1024 | tf_op jit(solution)/shard_map/attention_forward/pallas_call | solution.py:118
  192.2 11.4 %attention_forward.5 = (f32[4,256,640]{2,1,0:T(8,128)}, bf16[4,256,640]{2,1,0:T(8,128)(2,1)}, bf16[4,256,1920]{2,1,0:T(8,128)(2,1)}, bf16[4,20,256,256]{3,2,1,0:...) custom-call(s32[4]{0:T(128)} %refs_0_.5, ...), custom_call_target="tpu_custom_call", output_to_operand_aliasing={{0}: (4, {}), {1}: (5, {}), {2}: (6, {}), {3}: (7, {}), {4}... | custom-call | flops 9900000256 | bytes 1024 | tf_op jit(solution)/shard_map/attention_forward/pallas_call | solution.py:118
  203.5 26.5 %feed_forward.1 = (bf16[1024,640]{1,0:T(8,128)(2,1)}, bf16[1024,5120]{1,0:T(8,128)(2,1)}, bf16[1024,5120]{1,0:T(8,128)(2,1)}) custom-call(bf16[1024,640]{1,0:T(8,128)(2,1)} %bitcast.121, f32[1024,640]{1,0:T(8,128)} %bitcast.113, bf16[640,5120]{1,0:T(8,128)(2,1)} %bitcast.99, bf16[5120,640]{1,0:T(8,128)(2,1)} %bitcast.105, ...), custom_call_target="tpu_custom_call" | custom-call | flops 28600000512 | bytes 1024 | tf_op jit(solution)/shard_map/feed_forward/pallas_call | solution.py:168
  230.1 22.6 %feed_forward_back.3 = f32[1024,640]{1,0:T(8,128)} custom-call(bf16[1024,640]{1,0:T(8,128)(2,1)} %bitcast.65, bf16[1024,5120]{1,0:T(8,128)(2,1)} %get-tuple-element.121.refs_1_, bf16[640,5120]{1,0:T(8,128)(2,1)} %bitcast.100, bf16[5120,640]{1,0:T(8,128)(2,1)} %bitcast.106), custom_call_target="tpu_custom_call" | custom-call | flops 24199999488 | bytes 1024 | tf_op jit(solution)/shard_map/feed_forward_back/pallas_call | solution.py:259
  252.7 15.6 %attention_back.5 = bf16[2,256,640]{2,1,0:T(8,128)(2,1)} custom-call(f32[4,256,640]{2,1,0:T(8,128)} %bitcast.116, bf16[4,256,640]{2,1,0:T(8,128)(2,1)} %refs_1_.5, f32[4,256,640]{2,1,0:T(8,128)} %get-tuple-element.119.refs_2_, bf16[4,256,640]{2,1,0:T(8,128)(2,1)} %pad_maximum_fusion.refs_3_, bf16[4,256,1920]{2,1,0:T(8,128)(2,1)} %get-tuple-element.122.refs_4_, ...), custom_call_target="tpu_custom_call" | custom-call | flops 15399999488 | bytes 1024 | tf_op jit(solution)/shard_map/attention_back/pallas_call | solution.py:412
  269.8 15.6 %attention_back.4 = bf16[2,256,640]{2,1,0:T(8,128)(2,1)} custom-call(f32[4,256,640]{2,1,0:T(8,128)} %bitcast.117, bf16[4,256,640]{2,1,0:T(8,128)(2,1)} %refs_1_.5, f32[4,256,640]{2,1,0:T(8,128)} %get-tuple-element.119.refs_2_, bf16[4,256,640]{2,1,0:T(8,128)(2,1)} %pad_maximum_fusion.refs_3_, bf16[4,256,1920]{2,1,0:T(8,128)(2,1)} %get-tuple-element.122.refs_4_, ...), custom_call_target="tpu_custom_call" | custom-call | flops 15399999488 | bytes 1024 | tf_op jit(solution)/shard_map/attention_back/pallas_call | solution.py:412
  287.6 13.5 %feed_forward_back.4 = (f32[1024,640]{1,0:T(8,128)}, bf16[1024,5120]{1,0:T(8,128)(2,1)}) custom-call(bf16[512,640]{1,0:T(8,128)(2,1)} %bitcast.64, bf16[1024,5120]{1,0:T(8,128)(2,1)} %get-tuple-element.121.refs_1_, bf16[640,5120]{1,0:T(8,128)(2,1)} %bitcast.101, bf16[5120,640]{1,0:T(8,128)(2,1)} %bitcast.107), custom_call_target="tpu_custom_call" | custom-call | flops 12099999744 | bytes 1024 | tf_op jit(solution)/shard_map/feed_forward_back/pallas_call | solution.py:259
  303.5 12.4 %down_gradient.1.refs_3_ = bf16[5120,640]{1,0:T(8,128)(2,1)} custom-call(bf16[1024,5120]{1,0:T(8,128)(2,1)} %get-tuple-element.131.refs_0_, bf16[1024,640]{1,0:T(8,128)(2,1)} %bitcast.66), custom_call_target="tpu_custom_call" | custom-call | flops 13200000000 | bytes 1024 | tf_op jit(solution)/shard_map/down_gradient/pallas_call | solution.py:314
  315.9 13.3 %feed_forward_back.5 = (f32[1024,640]{1,0:T(8,128)}, bf16[1024,5120]{1,0:T(8,128)(2,1)}) custom-call(bf16[512,640]{1,0:T(8,128)(2,1)} %bitcast.63, bf16[1024,5120]{1,0:T(8,128)(2,1)} %get-tuple-element.121.refs_1_, bf16[640,5120]{1,0:T(8,128)(2,1)} %bitcast.102, bf16[5120,640]{1,0:T(8,128)(2,1)} %bitcast.108, ...), custom_call_target="tpu_custom_call", output_to_operand_aliasing={{0}: (4, {}), {1}: (5, {})} | custom-call | flops 12099999744 | bytes 1024 | tf_op jit(solution)/shard_map/feed_forward_back/pallas_call | solution.py:259
  329.2 12.8 %up_gradient.1 = (bf16[320,5120]{1,0:T(8,128)(2,1)}, bf16[320,5120]{1,0:T(8,128)(2,1)}, f32[8,5120]{1,0:T(8,128)}) custom-call(bf16[1024,640]{1,0:T(8,128)(2,1)} %bitcast.122, bf16[640,640]{1,0:T(8,128)(2,1)} %fusion.refs_1_.refs_5_, bf16[1024,5120]{1,0:T(8,128)(2,1)} %get-tuple-element.130.refs_2_, bf16[5120,640]{1,0:T(8,128)(2,1)} %down_gradient.1.refs_3_), custom_call_target="tpu_custom_call" | custom-call | flops 14300000256 | bytes 1024 | tf_op jit(solution)/shard_map/up_gradient/pallas_call | solution.py:293
  345.0 3.8 collective-permute-done.49.refs_10_
  348.7 3.9 add_convert_fusion.3
  353.9 17.6 %attention_back.6 = (f32[4,256,640]{2,1,0:T(8,128)}, bf16[4,256,640]{2,1,0:T(8,128)(2,1)}, bf16[4,256,1920]{2,1,0:T(8,128)(2,1)}, f32[8,640]{1,0:T(8,128)}) custom-call(f32[4,256,640]{2,1,0:T(8,128)} %bitcast.114, bf16[4,256,640]{2,1,0:T(8,128)(2,1)} %pad_maximum_fusion.1.refs_1_, f32[4,256,640]{2,1,0:T(8,128)} %get-tuple-element.119.refs_2_, ...), custom_call_target="tpu_custom_call" | custom-call | flops 15399999488 | bytes 1024 | tf_op jit(solution)/shard_map/attention_back/pallas_call | solution.py:412
  379.8 16.1 %attention_back.7 = (f32[4,256,640]{2,1,0:T(8,128)}, bf16[4,256,640]{2,1,0:T(8,128)(2,1)}, bf16[4,256,1920]{2,1,0:T(8,128)(2,1)}, f32[8,640]{1,0:T(8,128)}) custom-call(f32[4,256,640]{2,1,0:T(8,128)} %bitcast.115, bf16[4,256,640]{2,1,0:T(8,128)(2,1)} %pad_maximum_fusion.1.refs_1_, ...), custom_call_target="tpu_custom_call", output_to_operand_aliasing={{0}: (11, {}), {1}: (12, {}), {2}: (13, {})} | custom-call | flops 15399999488 | bytes 1024 | tf_op jit(solution)/shard_map/attention_back/pallas_call | solution.py:412
  397.7 14.3 %collective-permute-done.53.refs_8_ = bf16[40,2560]{1,0:T(8,128)(2,1)} collective-permute-done((bf16[40,2560]{1,0:T(8,128)(2,1)S(1)}, bf16[40,2560]{1,0:T(8,128)(2,1)}, u32[]{:S(2)}, u32[]{:S(2)}) %collective-permute-start.53) | collective-permute-done | bytes 204832 | tf_op jit(solution)/shard_map/ppermute | solution.py:499
  412.8 11.8 %projection_gradients.1 = (bf16[320,2688]{1,0:T(8,128)(2,1)}, bf16[320,2688]{1,0:T(8,128)(2,1)}) custom-call(bf16[1024,640]{1,0:T(8,128)(2,1)} %bitcast.124, bf16[1024,1920]{1,0:T(8,128)(2,1)} %bitcast.109, bf16[1024,640]{1,0:T(8,128)(2,1)} %bitcast.123, bf16[1024,640]{1,0:T(8,128)(2,1)} %bitcast.120, f32[640,128]{1,0:T(8,128)} %select_maximum_fusion.refs_4_, ...), custom_call_target="tpu_custom_call" | custom-call | flops 9900000256 | bytes 1024 | tf_op jit(solution)/shard_map/projection_gradients/pallas_call | solution.py:448
  428.9 3.7 collective-permute-start.58
  442.5 17.1 %collective-permute-done.58 = bf16[40,2560]{1,0:T(8,128)(2,1)S(1)} collective-permute-done((bf16[40,2560]{1,0:T(8,128)(2,1)S(1)}, bf16[40,2560]{1,0:T(8,128)(2,1)S(1)}, u32[]{:S(2)}, u32[]{:S(2)}) %collective-permute-start.58) | collective-permute-done | bytes 204832 | tf_op jit(solution)/shard_map/ppermute | solution.py:499
  469.3 11.9 %collective-permute-done.61 = bf16[40,2688]{1,0:T(8,128)(2,1)S(1)} collective-permute-done((bf16[40,2688]{1,0:T(8,128)(2,1)S(1)}, bf16[40,2688]{1,0:T(8,128)(2,1)S(1)}, u32[]{:S(2)}, u32[]{:S(2)}) %collective-permute-start.61) | collective-permute-done | bytes 215072 | tf_op jit(solution)/shard_map/ppermute | solution.py:499
  (254 shorter events, 117.3 us)
Async XLA Ops:
  7.2 480.8 %reduce-scatter.2.cloned.1.call-start = ((), (), s32[]{:S(2)}) async-start(), calls=%async_computation.1 | async-start | bytes 6963200 | tf_op jit(solution)/shard_map/reduce_scatter | solution.py:642
  11.2 17.8 %collective-permute-start.1 = (bf16[40,2688]{1,0:T(8,128)(2,1)S(1)}, bf16[40,2688]{1,0:T(8,128)(2,1)S(1)}, u32[]{:S(2)}, u32[]{:S(2)}) collective-permute-start(bf16[40,2688]{1,0:T(8,128)(2,1)S(1)} %pad_maximum_fusion.2.refs_1_), channel_id=1, source_target_pairs={{0,8},{1,9},{2,10},{3,11},{4,12},{5,13},{6,14},{7,15},{8,0},{9,1},... | collective-permute-start | bytes 645128 | tf_op jit(solution)/shard_map/ppermute | solution.py:499
  12.3 19.5 %collective-permute-start.2 = (bf16[40,2688]{1,0:T(8,128)(2,1)S(1)}, bf16[40,2688]{1,0:T(8,128)(2,1)S(1)}, u32[]{:S(2)}, u32[]{:S(2)}) collective-permute-start(bf16[40,2688]{1,0:T(8,128)(2,1)S(1)} %pad_maximum_fusion.2.refs_1_), channel_id=1, source_target_pairs={{0,12},{1,13},{2,14},{3,15},{4,0},{5,1},{6,2},{7,3},{8,4},{9,5},{1... | collective-permute-start | bytes 645128 | tf_op jit(solution)/shard_map/ppermute | solution.py:499
  13.7 18.2 %collective-permute-start.3 = (bf16[40,2688]{1,0:T(8,128)(2,1)S(1)}, bf16[40,2688]{1,0:T(8,128)(2,1)S(1)}, u32[]{:S(2)}, u32[]{:S(2)}) collective-permute-start(bf16[40,2688]{1,0:T(8,128)(2,1)S(1)} %pad_maximum_fusion.2.refs_1_), channel_id=1, source_target_pairs={{0,2},{1,3},{2,0},{3,1},{4,6},{5,7},{6,4},{7,5},{8,10},{9,11},{10,... | collective-permute-start | bytes 645128 | tf_op jit(solution)/shard_map/ppermute | solution.py:499
  15.0 19.9 %collective-permute-start.9 = (bf16[40,5120]{1,0:T(8,128)(2,1)}, bf16[40,5120]{1,0:T(8,128)(2,1)S(1)}, u32[]{:S(2)}, u32[]{:S(2)}) collective-permute-start(bf16[40,5120]{1,0:T(8,128)(2,1)} %bitcast.86), channel_id=1, source_target_pairs={{0,2},{1,3},{2,0},{3,1},{4,6},{5,7},{6,4},{7,5},{8,10},{9,11},{10,... | collective-permute-start | bytes 1228808 | tf_op jit(solution)/shard_map/ppermute | solution.py:499
  31.9 16.6 %collective-permute-start.7 = (bf16[40,5120]{1,0:T(8,128)(2,1)}, bf16[40,5120]{1,0:T(8,128)(2,1)S(1)}, u32[]{:S(2)}, u32[]{:S(2)}) collective-permute-start(bf16[40,5120]{1,0:T(8,128)(2,1)} %bitcast.87), channel_id=1, source_target_pairs={{0,4},{1,5},{2,6},{3,7},{4,8},{5,9},{6,10},{7,11},{8,12},{9,13},{1... | collective-permute-start | bytes 1228808 | tf_op jit(solution)/shard_map/ppermute | solution.py:499
  31.9 19.2 %collective-permute-start.8 = (bf16[40,5120]{1,0:T(8,128)(2,1)}, bf16[40,5120]{1,0:T(8,128)(2,1)S(1)}, u32[]{:S(2)}, u32[]{:S(2)}) collective-permute-start(bf16[40,5120]{1,0:T(8,128)(2,1)} %bitcast.88), channel_id=1, source_target_pairs={{0,12},{1,13},{2,14},{3,15},{4,0},{5,1},{6,2},{7,3},{8,4},{9,5},{1... | collective-permute-start | bytes 1228808 | tf_op jit(solution)/shard_map/ppermute | solution.py:499
  55.4 19.5 %collective-permute-start.18 = (bf16[40,5120]{1,0:T(8,128)(2,1)}, bf16[40,5120]{1,0:T(8,128)(2,1)}, u32[]{:S(2)}, u32[]{:S(2)}) collective-permute-start(bf16[40,5120]{1,0:T(8,128)(2,1)} %bitcast.89), channel_id=1, source_target_pairs={{0,8},{1,9},{2,10},{3,11},{4,12},{5,13},{6,14},{7,15},{8,0},{9,1},... | collective-permute-start | bytes 1228808 | tf_op jit(solution)/shard_map/ppermute | solution.py:499
  58.6 16.3 %collective-permute-start.19 = (bf16[40,5120]{1,0:T(8,128)(2,1)S(1)}, bf16[40,5120]{1,0:T(8,128)(2,1)S(1)}, u32[]{:S(2)}, u32[]{:S(2)}) collective-permute-start(bf16[40,5120]{1,0:T(8,128)(2,1)S(1)} %collective-permute-done.7.refs_2_), channel_id=1, source_target_pairs={{0,2},{1,3},{2,0},{3,1},{4,6},{5,7},{6,4},{7,5},{8,10},{9,11},{10,... | collective-permute-start | bytes 1228808 | tf_op jit(solution)/shard_map/ppermute | solution.py:499
  59.9 18.1 %collective-permute-start.20 = (bf16[40,5120]{1,0:T(8,128)(2,1)S(1)}, bf16[40,5120]{1,0:T(8,128)(2,1)S(1)}, u32[]{:S(2)}, u32[]{:S(2)}) collective-permute-start(bf16[40,5120]{1,0:T(8,128)(2,1)S(1)} %collective-permute-done.8.refs_4_), channel_id=1, source_target_pairs={{0,2},{1,3},{2,0},{3,1},{4,6},{5,7},{6,4},{7,5},{8,10},{9,11},{10,... | collective-permute-start | bytes 1228808 | tf_op jit(solution)/shard_map/ppermute | solution.py:499
  78.8 19.6 %collective-permute-start.22 = (bf16[320,640]{1,0:T(8,128)(2,1)S(1)}, bf16[320,640]{1,0:T(8,128)(2,1)S(1)}, u32[]{:S(2)}, u32[]{:S(2)}) collective-permute-start(bf16[320,640]{1,0:T(8,128)(2,1)S(1)} %bitcast.93), channel_id=1, source_target_pairs={{0,4},{1,5},{2,6},{3,7},{4,8},{5,9},{6,10},{7,11},{8,12},{9,13},{1... | collective-permute-start | bytes 1228808 | tf_op jit(solution)/shard_map/ppermute | solution.py:499
  78.8 19.6 %collective-permute-start.23 = (bf16[320,640]{1,0:T(8,128)(2,1)S(1)}, bf16[320,640]{1,0:T(8,128)(2,1)S(1)}, u32[]{:S(2)}, u32[]{:S(2)}) collective-permute-start(bf16[320,640]{1,0:T(8,128)(2,1)S(1)} %bitcast.94), channel_id=1, source_target_pairs={{0,12},{1,13},{2,14},{3,15},{4,0},{5,1},{6,2},{7,3},{8,4},{9,5},{1... | collective-permute-start | bytes 1228808 | tf_op jit(solution)/shard_map/ppermute | solution.py:499
  80.3 18.2 %collective-permute-start.24 = (bf16[320,640]{1,0:T(8,128)(2,1)S(1)}, bf16[320,640]{1,0:T(8,128)(2,1)S(1)}, u32[]{:S(2)}, u32[]{:S(2)}) collective-permute-start(bf16[320,640]{1,0:T(8,128)(2,1)S(1)} %bitcast.95), channel_id=1, source_target_pairs={{0,2},{1,3},{2,0},{3,1},{4,6},{5,7},{6,4},{7,5},{8,10},{9,11},{10,... | collective-permute-start | bytes 1228808 | tf_op jit(solution)/shard_map/ppermute | solution.py:499
  81.5 17.0 %collective-permute-start.21 = (bf16[40,5120]{1,0:T(8,128)(2,1)}, bf16[40,5120]{1,0:T(8,128)(2,1)S(1)}, u32[]{:S(2)}, u32[]{:S(2)}) collective-permute-start(bf16[40,5120]{1,0:T(8,128)(2,1)} %collective-permute-done.18.refs_3_), channel_id=1, source_target_pairs={{0,2},{1,3},{2,0},{3,1},{4,6},{5,7},{6,4},{7,5},{8,10},{9,11},{10,... | collective-permute-start | bytes 1228808 | tf_op jit(solution)/shard_map/ppermute | solution.py:499
  105.7 25.1 %collective-permute-start.37 = (bf16[320,640]{1,0:T(8,128)(2,1)S(1)}, bf16[320,640]{1,0:T(8,128)(2,1)S(1)}, u32[]{:S(2)}, u32[]{:S(2)}) collective-permute-start(bf16[320,640]{1,0:T(8,128)(2,1)S(1)} %bitcast.96), channel_id=1, source_target_pairs={{0,1},{1,0},{2,3},{3,2},{4,5},{5,4},{6,7},{7,6},{8,9},{9,8},{10,11... | collective-permute-start | bytes 1228808 | tf_op jit(solution)/shard_map/ppermute | solution.py:499
  106.1 22.5 %collective-permute-start.35 = (bf16[320,640]{1,0:T(8,128)(2,1)S(1)}, bf16[320,640]{1,0:T(8,128)(2,1)S(1)}, u32[]{:S(2)}, u32[]{:S(2)}) collective-permute-start(bf16[320,640]{1,0:T(8,128)(2,1)S(1)} %collective-permute-done.23.refs_4_), channel_id=1, source_target_pairs={{0,2},{1,3},{2,0},{3,1},{4,6},{5,7},{6,4},{7,5},{8,10},{9,11},{10,... | collective-permute-start | bytes 1228808 | tf_op jit(solution)/shard_map/ppermute | solution.py:499
  107.4 21.3 %collective-permute-start.34 = (bf16[320,640]{1,0:T(8,128)(2,1)S(1)}, bf16[320,640]{1,0:T(8,128)(2,1)}, u32[]{:S(2)}, u32[]{:S(2)}) collective-permute-start(bf16[320,640]{1,0:T(8,128)(2,1)S(1)} %collective-permute-done.22.refs_2_), channel_id=1, source_target_pairs={{0,2},{1,3},{2,0},{3,1},{4,6},{5,7},{6,4},{7,5},{8,10},{9,11},{10,... | collective-permute-start | bytes 1228808 | tf_op jit(solution)/shard_map/ppermute | solution.py:499
  107.5 21.2 %collective-permute-start.33 = (bf16[320,640]{1,0:T(8,128)(2,1)S(1)}, bf16[320,640]{1,0:T(8,128)(2,1)S(1)}, u32[]{:S(2)}, u32[]{:S(2)}) collective-permute-start(bf16[320,640]{1,0:T(8,128)(2,1)S(1)} %bitcast.97), channel_id=1, source_target_pairs={{0,8},{1,9},{2,10},{3,11},{4,12},{5,13},{6,14},{7,15},{8,0},{9,1},... | collective-permute-start | bytes 1228808 | tf_op jit(solution)/shard_map/ppermute | solution.py:499
  108.4 22.5 %collective-permute-start.38 = (bf16[320,640]{1,0:T(8,128)(2,1)S(1)}, bf16[320,640]{1,0:T(8,128)(2,1)S(1)}, u32[]{:S(2)}, u32[]{:S(2)}) collective-permute-start(bf16[320,640]{1,0:T(8,128)(2,1)S(1)} %collective-permute-done.22.refs_2_), channel_id=1, source_target_pairs={{0,1},{1,0},{2,3},{3,2},{4,5},{5,4},{6,7},{7,6},{8,9},{9,8},{10,11... | collective-permute-start | bytes 1228808 | tf_op jit(solution)/shard_map/ppermute | solution.py:499
  158.1 18.6 %collective-permute-start.46 = (bf16[2,256,640]{2,1,0:T(8,128)(2,1)}, bf16[2,256,640]{2,1,0:T(8,128)(2,1)S(1)}, u32[]{:S(2)}, u32[]{:S(2)}) collective-permute-start(bf16[2,256,640]{2,1,0:T(8,128)(2,1)} %bitcast.85), channel_id=1, source_target_pairs={{0,16},{1,17},{2,18},{3,19},{4,20},{5,21},{6,22},{7,23},{8,24},{9,... | collective-permute-start | bytes 1966088 | tf_op jit(solution)/shard_map/ppermute | solution.py:618
  168.3 22.4 %collective-permute-start.45 = (bf16[2,256,640]{2,1,0:T(8,128)(2,1)}, bf16[2,256,640]{2,1,0:T(8,128)(2,1)S(1)}, u32[]{:S(2)}, u32[]{:S(2)}) collective-permute-start(bf16[2,256,640]{2,1,0:T(8,128)(2,1)} %bitcast.84), channel_id=1, source_target_pairs={{0,16},{1,17},{2,18},{3,19},{4,20},{5,21},{6,22},{7,23},{8,24},{9,... | collective-permute-start | bytes 1966088 | tf_op jit(solution)/shard_map/ppermute | solution.py:618
  268.3 18.4 %collective-permute-start.48 = (bf16[2,256,640]{2,1,0:T(8,128)(2,1)}, bf16[2,256,640]{2,1,0:T(8,128)(2,1)S(1)}, u32[]{:S(2)}, u32[]{:S(2)}) collective-permute-start(bf16[2,256,640]{2,1,0:T(8,128)(2,1)} %attention_back.5), channel_id=1, source_target_pairs={{16,0},{17,1},{18,2},{19,3},{20,4},{21,5},{22,6},{23,7},{24,8},{25... | collective-permute-start | bytes 1966088 | tf_op jit(solution)/shard_map/ppermute | solution.py:633
  352.7 19.8 %collective-permute-start.50 = (bf16[160,2560]{1,0:T(8,128)(2,1)}, bf16[160,2560]{1,0:T(8,128)(2,1)}, u32[]{:S(2)}, u32[]{:S(2)}) collective-permute-start(bf16[160,2560]{1,0:T(8,128)(2,1)} %get-tuple-element.189), channel_id=1, source_target_pairs={{0,2},{1,3},{2,0},{3,1},{4,6},{5,7},{6,4},{7,5},{8,10},{9,11},{10,... | collective-permute-start | bytes 2457608 | tf_op jit(solution)/shard_map/ppermute | solution.py:499
  374.4 23.3 %collective-permute-start.52 = (bf16[40,2560]{1,0:T(8,128)(2,1)}, bf16[40,2560]{1,0:T(8,128)(2,1)}, u32[]{:S(2)}, u32[]{:S(2)}) collective-permute-start(bf16[40,2560]{1,0:T(8,128)(2,1)} %get-tuple-element.204), channel_id=1, source_target_pairs={{0,4},{1,5},{2,6},{3,7},{4,8},{5,9},{6,10},{7,11},{8,12},{9,13},{1... | collective-permute-start | bytes 614408 | tf_op jit(solution)/shard_map/ppermute | solution.py:499
  376.8 35.2 %collective-permute-start.53 = (bf16[40,2560]{1,0:T(8,128)(2,1)S(1)}, bf16[40,2560]{1,0:T(8,128)(2,1)}, u32[]{:S(2)}, u32[]{:S(2)}) collective-permute-start(bf16[40,2560]{1,0:T(8,128)(2,1)S(1)} %get-tuple-element.203), channel_id=1, source_target_pairs={{0,8},{1,9},{2,10},{3,11},{4,12},{5,13},{6,14},{7,15},{8,0},{9,1},... | collective-permute-start | bytes 614408 | tf_op jit(solution)/shard_map/ppermute | solution.py:499
  377.5 34.5 %collective-permute-start.54 = (bf16[40,2560]{1,0:T(8,128)(2,1)S(1)}, bf16[40,2560]{1,0:T(8,128)(2,1)}, u32[]{:S(2)}, u32[]{:S(2)}) collective-permute-start(bf16[40,2560]{1,0:T(8,128)(2,1)S(1)} %get-tuple-element.202), channel_id=1, source_target_pairs={{0,12},{1,13},{2,14},{3,15},{4,0},{5,1},{6,2},{7,3},{8,4},{9,5},{1... | collective-permute-start | bytes 614408 | tf_op jit(solution)/shard_map/ppermute | solution.py:499
  378.5 33.5 %collective-permute-start.51 = (bf16[160,2560]{1,0:T(8,128)(2,1)S(1)}, bf16[160,2560]{1,0:T(8,128)(2,1)S(1)}, u32[]{:S(2)}, u32[]{:S(2)}) collective-permute-start(bf16[160,2560]{1,0:T(8,128)(2,1)S(1)} %get-tuple-element.191), channel_id=1, source_target_pairs={{0,2},{1,3},{2,0},{3,1},{4,6},{5,7},{6,4},{7,5},{8,10},{9,11},{10,... | collective-permute-start | bytes 2457608 | tf_op jit(solution)/shard_map/ppermute | solution.py:499
  428.9 30.7 %collective-permute-start.58 = (bf16[40,2560]{1,0:T(8,128)(2,1)S(1)}, bf16[40,2560]{1,0:T(8,128)(2,1)S(1)}, u32[]{:S(2)}, u32[]{:S(2)}) collective-permute-start(bf16[40,2560]{1,0:T(8,128)(2,1)S(1)} %get-tuple-element.200), channel_id=1, source_target_pairs={{0,8},{1,9},{2,10},{3,11},{4,12},{5,13},{6,14},{7,15},{8,0},{9,1},... | collective-permute-start | bytes 614408 | tf_op jit(solution)/shard_map/ppermute | solution.py:499
  432.6 28.9 %collective-permute-start.59 = (bf16[40,2560]{1,0:T(8,128)(2,1)S(1)}, bf16[40,2560]{1,0:T(8,128)(2,1)S(1)}, u32[]{:S(2)}, u32[]{:S(2)}) collective-permute-start(bf16[40,2560]{1,0:T(8,128)(2,1)S(1)} %get-tuple-element.199), channel_id=1, source_target_pairs={{0,12},{1,13},{2,14},{3,15},{4,0},{5,1},{6,2},{7,3},{8,4},{9,5},{1... | collective-permute-start | bytes 614408 | tf_op jit(solution)/shard_map/ppermute | solution.py:499
  434.4 28.2 %collective-permute-start.56 = (bf16[160,2688]{1,0:T(8,128)(2,1)S(1)}, bf16[160,2688]{1,0:T(8,128)(2,1)S(1)}, u32[]{:S(2)}, u32[]{:S(2)}) collective-permute-start(bf16[160,2688]{1,0:T(8,128)(2,1)S(1)} %get-tuple-element.192), channel_id=1, source_target_pairs={{0,2},{1,3},{2,0},{3,1},{4,6},{5,7},{6,4},{7,5},{8,10},{9,11},{10,... | collective-permute-start | bytes 2580488 | tf_op jit(solution)/shard_map/ppermute | solution.py:499
  462.9 18.4 %collective-permute-start.61 = (bf16[40,2688]{1,0:T(8,128)(2,1)S(1)}, bf16[40,2688]{1,0:T(8,128)(2,1)S(1)}, u32[]{:S(2)}, u32[]{:S(2)}) collective-permute-start(bf16[40,2688]{1,0:T(8,128)(2,1)S(1)} %get-tuple-element.198), channel_id=1, source_target_pairs={{0,8},{1,9},{2,10},{3,11},{4,12},{5,13},{6,14},{7,15},{8,0},{9,1},... | collective-permute-start | bytes 645128 | tf_op jit(solution)/shard_map/ppermute | solution.py:499
  464.1 19.5 %collective-permute-start.62 = (bf16[40,2688]{1,0:T(8,128)(2,1)S(1)}, bf16[40,2688]{1,0:T(8,128)(2,1)S(1)}, u32[]{:S(2)}, u32[]{:S(2)}) collective-permute-start(bf16[40,2688]{1,0:T(8,128)(2,1)S(1)} %get-tuple-element.197), channel_id=1, source_target_pairs={{0,12},{1,13},{2,14},{3,15},{4,0},{5,1},{6,2},{7,3},{8,4},{9,5},{1... | collective-permute-start | bytes 645128 | tf_op jit(solution)/shard_map/ppermute | solution.py:499
  (79 other events, 960.3 us)
Sparse Core Ops, SparseCore 0:
  343.2 115.3 reduce-scatter.1

commit v4 on v3

--- a/solution.py
+++ b/solution.py
@@ -179,6 +179,49 @@
     )(c, m, wup, wdown, bup, vec)
 
 
+def mlp_both_body(rows, c_ref, m_ref, dz_ref, wup_ref, wdown_ref, bup_ref, vec_ref, y_ref, g_ref, gp_ref, dc_ref, acc_ref):
+    step = pl.program_id(0)
+
+    @pl.when(step == 0)
+    def _():
+        acc_ref[...] = m_ref[...] + vec_ref[7:8]
+        dc_ref[...] = jnp.zeros_like(dc_ref)
+
+    for r in range(c_ref.shape[0] // rows):
+        at = slice(r * rows, r * rows + rows)
+        u = dot(c_ref[at], wup_ref[...]) + bup_ref[...]
+        dg = dot(dz_ref[at], wdown_ref[...], ((1,), (1,)))
+        act, slope = gelu_pair(u)
+        act, slope = act.astype(BF16), slope.astype(BF16)
+        g_ref[at] = act
+        gp_ref[at] = slope
+        acc_ref[at] += dot(act, wdown_ref[...])
+        dc_ref[at] += dot((dg * slope.astype(F32)).astype(BF16), wup_ref[...], ((1,), (1,)))
+
+    @pl.when(step == pl.num_programs(0) - 1)
+    def _():
+        y_ref[...] = acc_ref[...].astype(BF16)
+
+
+def mlp_both(c, m, dz, wup, wdown, bup, vec, chunk=1280, rows=256):
+    n, width = c.shape
+    ff = wup.shape[1]
+    column = pl.BlockSpec((n, chunk), lambda i: (0, i))
+    return pl.pallas_call(
+        lambda *refs: mlp_both_body(rows, *refs),
+        grid=(ff // chunk,),
+        in_specs=[whole(c.shape), whole(m.shape), whole(dz.shape), pl.BlockSpec((width, chunk), lambda i: (0, i)),
+                  pl.BlockSpec((chunk, width), lambda i: (i, 0)), pl.BlockSpec((1, chunk), lambda i: (0, i)), whole(vec.shape)],
+        out_specs=[whole((n, width)), column, column, whole((n, width))],
+        out_shape=[jax.ShapeDtypeStruct((n, width), BF16), jax.ShapeDtypeStruct((n, ff), BF16), jax.ShapeDtypeStruct((n, ff), BF16),
+                   jax.ShapeDtypeStruct((n, width), F32)],
+        scratch_shapes=[pltpu.VMEM((n, width), F32)],
+        compiler_params=pltpu.CompilerParams(vmem_limit_bytes=VMEM_LIMIT),
+        cost_estimate=cost(42),
+        name="feed_forward_both",
+    )(c, m, dz, wup, wdown, bup, vec)
+
+
 def mlp_up_body(rows, c_ref, wup_ref, bup_ref, g_ref):
     for r in range(c_ref.shape[0] // rows):
         at = slice(r * rows, r * rows + rows)
@@ -254,8 +297,8 @@
     outs = [jax.ShapeDtypeStruct((n * parts, width), F32)]
     specs = [pl.BlockSpec((n, width), lambda i: (at, 0))]
     if save:
-        outs += [jax.ShapeDtypeStruct((n * parts, ff), BF16)]
-        specs += [pl.BlockSpec((n, chunk), lambda i: (at, i))]
+        outs += [jax.ShapeDtypeStruct((n, ff), BF16)]
+        specs += [pl.BlockSpec((n, chunk), lambda i: (0, i))]
     return pl.pallas_call(
         lambda *refs: mlp_bwd_body(save, rows, *refs[:4], *refs[len(args):]),
         grid=(ff // chunk,),
@@ -301,6 +344,49 @@
         cost_estimate=cost(13 / parts),
         name="up_gradient",
     )(c, order, du, *after)
+
+
+def mlp_grad_body(rows, dz_ref, gp_ref, wup_ref, wdown_ref, early_ref, c_ref, order_ref, dc_ref, keep_ref, send_ref, sum_ref, du_ref, ct_ref):
+    half = keep_ref.shape[0]
+    count = early_ref.shape[0]
+
+    @pl.when(pl.program_id(0) == 0)
+    def _():
+        dc_ref[...] = jnp.zeros_like(dc_ref)
+        ct_ref[:2 * half] = dot(order_ref[...], c_ref[...], ((1,), (1,))).astype(BF16)
+        ct_ref[2 * half:] = jnp.ones_like(ct_ref[2 * half:])
+
+    for r in range(dz_ref.shape[0] // rows):
+        at = slice(r * rows, r * rows + rows)
+        dg = dot(dz_ref[at], wdown_ref[...], ((1,), (1,)))
+        du = (dg * gp_ref[at].astype(F32)).astype(BF16)
+        du_ref[at] = du
+        dc_ref[at] += dot(du, wup_ref[...], ((1,), (1,)))
+    grad = dot(ct_ref[:, :count], early_ref[...]) + dot(ct_ref[:, count:], du_ref[...])
+    keep_ref[...] = grad[:half].astype(BF16)
+    send_ref[...] = grad[half:2 * half].astype(BF16)
+    sum_ref[...] = grad[2 * half:2 * half + 8]
+
+
+def mlp_grad(dz, gp, wup, wdown, early, c, order, dc, after=(), chunk=1280, rows=256):
+    count, width = dz.shape
+    n, ff = gp.shape
+    at = n // count - 1
+    waits = 1 + len(after)
+    column = lambda rows: pl.BlockSpec((rows, chunk), lambda i: (0, i))
+    return pl.pallas_call(
+        lambda *refs: mlp_grad_body(rows, *refs[:7], *refs[7 + waits:]),
+        grid=(ff // chunk,),
+        in_specs=[whole(dz.shape), pl.BlockSpec((count, chunk), lambda i: (at, i)), column(width), pl.BlockSpec((chunk, width), lambda i: (i, 0)),
+                  column(n - count), whole(c.shape), whole(order.shape)] + tied(waits),
+        out_specs=[pl.BlockSpec((count, width), lambda i: (at, 0)), column(width // 2), column(width // 2), column(8)],
+        out_shape=[jax.ShapeDtypeStruct((n, width), F32)] + [jax.ShapeDtypeStruct((width // 2, ff), BF16)] * 2 + [jax.ShapeDtypeStruct((8, ff), F32)],
+        scratch_shapes=[pltpu.VMEM((count, chunk), BF16), pltpu.VMEM((width + 16, n), BF16)],
+        input_output_aliases={7: 0},
+        compiler_params=pltpu.CompilerParams(vmem_limit_bytes=VMEM_LIMIT),
+        cost_estimate=cost(21),
+        name="feed_forward_gradients",
+    )(dz, gp, wup, wdown, early, c, order, dc, *after)
 
 
 def down_grad_body(g_ref, dz_ref, out_ref):
@@ -484,6 +570,36 @@
     return out.reshape(count * rows, columns)
 
 
+def place_down_body(count, to_ref, g_ref, m_ref, vec_ref, *refs):
+    pieces, (w_ref, y_ref), sems = refs[:count], refs[count:count + 2], refs[count + 2]
+    rows = pieces[0].shape[0]
+    copies = [pltpu.make_async_copy(piece, w_ref.at[pl.ds(pl.multiple_of(to_ref[i] * rows, rows), rows)], sems.at[i])
+              for i, piece in enumerate(pieces)]
+    for copy in copies:
+        copy.start()
+    for copy in copies:
+        copy.wait()
+    y_ref[...] = (m_ref[...] + vec_ref[7:8] + dot(g_ref[...], w_ref[...])).astype(BF16)
+
+
+def place_down(pieces, to, g, m, vec, parts):
+    rows, width = pieces[0].shape
+    count = len(pieces)
+    ff = count * rows
+    n = g.shape[0] // parts
+    return pl.pallas_call(
+        lambda *refs: place_down_body(count, *refs),
+        grid=(1,),
+        in_specs=[pl.BlockSpec(memory_space=pltpu.SMEM), whole((n, ff)), whole((n, width)), whole(vec.shape)] + tied(count),
+        out_specs=[whole((ff, width)), whole((n, width))],
+        out_shape=[jax.ShapeDtypeStruct((ff, width), BF16), jax.ShapeDtypeStruct((n, width), BF16)],
+        scratch_shapes=[pltpu.SemaphoreType.DMA((count,))],
+        compiler_params=pltpu.CompilerParams(vmem_limit_bytes=VMEM_LIMIT),
+        cost_estimate=cost(10),
+        name="place_and_feed_forward_down",
+    )(to, g, m, vec, *pieces)
+
+
 def places(count):
     return count // 4, 2, 2
 
@@ -524,14 +640,14 @@
 
 def y_step(mine, got):
     half = mine.shape[0] // 2
-    return both(mine[:half], got[:half]), hop(both(mine[half:], got[half:]), "y")
+    return (mine[:half], got[:half]), hop(both(mine[half:], got[half:]), "y")
 
 
 def z_step(mine, got):
     zs, _, _ = places(lax.axis_size("dp"))
-    rows = mine.shape[0] // zs
-    at = lambda v, k: v[k * rows:k * rows + rows]
-    return [at(mine, 0), at(got, 0)] + [hop(both(at(mine, k), at(got, k)), "z", k) for k in range(1, zs)]
+    rows = got.shape[0] // zs
+    terms = [[term[k * rows:k * rows + rows] for term in (*mine, got)] for k in range(zs)]
+    return terms[0] + [hop(total(terms[k]).astype(BF16), "z", k) for k in range(1, zs)]
 
 
 def total(terms):
@@ -545,14 +661,18 @@
     return lax.optimization_barrier((value, *after))[0]
 
 
-def assemble(line, other, siblings, after=()):
+def siblings(pieces, *after):
+    return [hop(held(piece, *after), "core") for piece in pieces]
+
+
+def places_of_pieces():
     zs, ys, cores = places(lax.axis_size("dp"))
     z, y, c = behind_me()
     to = []
     for core in (c, 1 - c):
         for row in (y, 1 - y):
             to += [(((z + zs - step) % zs) * ys + row) * cores + core for step in range(zs)]
-    return place(line + other + siblings, jnp.stack(to).astype(jnp.int32), after)
+    return jnp.stack(to).astype(jnp.int32)
 
 
 def on_device(tokens, lengths, cotangent, w_qkv, w_out, w_up, w_down, norm_gain, norm_bias, bias_vec, up_bias):
@@ -571,21 +691,19 @@
     table = jnp.pad(table, ((0, 0), (0, 128 - used)))
     packed = jnp.concatenate([w_qkv[0], w_out[0], table], axis=1)
     if by_hand:
-        up, down = w_up[0], w_down[0]
-        order = scatter_order(shard)
-        proj_1, proj_3, proj_2 = hop(packed, "z", 1), hop(packed, "z", 3), hop(packed, "z", 2)
-        proj_y0, up_y0 = hop(packed, "y"), hop(up, "y")
-        now = (proj_1, proj_2, proj_3, proj_y0)
-        up_1, up_3 = hop(held(up, *now), "z", 1), hop(held(up, *now), "z", 3)
-        proj_y = [hop(held(piece, *now), "y") for piece in (proj_1, proj_2, proj_3)]
-        now = (up_1, up_3, up_y0, *proj_y)
-        up_2 = hop(held(up, *now), "z", 2)
-        up_y1, up_y3 = hop(held(up_1, *now), "y"), hop(held(up_3, *now), "y")
-        line, other = [packed, proj_1, proj_2, proj_3], [proj_y0, *proj_y]
-        proj = assemble(line, other, [hop(held(piece, *now), "core") for piece in line + other])
-        now = (up_2, up_y1, up_y3)
+        down = w_down[0]
+        order, to = scatter_order(shard), places_of_pieces()
+        wup = lax.all_gather(w_up[0], "dp", axis=0, tiled=True)
+        proj_z = [hop(packed, "z", step) for step in (1, 2, 3)]
+        proj_y0, down_y0 = hop(packed, "y"), hop(down, "y")
+        now = (*proj_z, proj_y0, down_y0)
         down_1, down_3 = hop(held(down, *now), "z", 1), hop(held(down, *now), "z", 3)
-        up_y2, down_y0 = hop(held(up_2, *now), "y"), hop(held(down, *now), "y")
+        proj_y = [hop(held(piece, *now), "y") for piece in proj_z]
+        now = (down_1, down_3, *proj_y)
+        pieces = [packed, *proj_z, proj_y0, *proj_y]
+        proj = place(pieces + siblings(pieces, *now), to)
+        down_2 = hop(held(down, *now), "z", 2)
+        down_y1, down_y3 = hop(held(down_1, *now), "y"), hop(held(down_3, *now), "y")
     else:
         order = (jnp.arange(width)[None, :] == jnp.arange(width)[:, None]).astype(BF16)
         proj = lax.all_gather(packed, "dp", axis=0, tiled=True)
@@ -597,25 +715,19 @@
 
     mid, c = attn_fwd(tokens, lengths, proj, vec, False)
     c = c.reshape(n, width)
+    mid = mid.reshape(n, width)
     if by_hand:
-        now = (down_1, down_3, up_y2, down_y0, c)
-        down_2 = hop(held(down, *now), "z", 2)
-        down_y1, down_y3 = hop(held(down_1, *now), "y"), hop(held(down_3, *now), "y")
-        line, other = [up, up_1, up_2, up_3], [up_y0, up_y1, up_y2, up_y3]
-        wup = assemble(line, other, [hop(held(piece, *now), "core") for piece in line + other])
+        now = (down_2, down_y1, down_y3, c)
+        down_y2 = hop(held(down_2, *now), "y")
     act = mlp_up(c, wup, bup)
     if by_hand:
-        now = (down_2, down_y1, down_y3, act)
-        down_y2 = hop(held(down_2, *now), "y")
-    if by_hand:
-        line, other = [down, down_1, down_2, down_3], [down_y0, down_y1, down_y2, down_y3]
-        wdown = assemble(line, other, [hop(piece, "core") for piece in line + other])
-    mid = mid.reshape(n, width)
+        pieces = [down, down_1, down_2, down_3, down_y0, down_y1, down_y2, down_y3]
+        wdown, y_a = place_down(pieces + siblings(pieces, act), to, act, mid, vec, parts)
+    else:
+        y_a = mlp_down(act, mid, wdown, vec, 0, parts)
+    y_b = mlp_down(act, mid, wdown, vec, 1, parts)
     kept = ()
-    arrived = []
-    for at in range(parts):
-        y = mlp_down(act, mid, wdown, vec, at, parts)
-        arrived.append(lax.ppermute(y.reshape(part, seq, width), "section", [(0, 1)]))
+    arrived = [lax.ppermute(y.reshape(part, seq, width), "section", [(0, 1)]) for y in (y_a, y_b)]
     h = []
     for at in range(parts):
         h.append(jnp.where(section == 0, tokens[at * part:at * part + part], held(arrived[at], *kept[:1])))
@@ -623,34 +735,29 @@
     h = jnp.concatenate(h)
     m, c, qkv, e, o, a, inv = kept
     c = c.reshape(n, width)
-    y, g, gp = mlp_fwd(c, m.reshape(n, width), wup, wdown, bup, vec, True)
-
-    dc, = mlp_bwd(cotangent.reshape(n, width), gp, wup, wdown, False)
+    y, g, gp, dc = mlp_both(c, m.reshape(n, width), cotangent.reshape(n, width), wup, wdown, bup, vec)
     dc = dc.reshape(tokens.shape)
     arrived = []
     for at in range(parts):
         back, = attn_bwd(dc, cotangent, m, h, qkv, e, o, inv, proj, vec, at, parts, False)
         arrived.append(lax.ppermute(back, "section", [(1, 0)]))
-    dz, more = [], ()
-    for at in range(parts):
-        dz.append(jnp.where(section == 1, cotangent[at * part:at * part + part], held(arrived[at], *more[:1])))
-        more = mlp_bwd(dz[at].reshape(part * seq, width), gp, wup, wdown, True, at, parts, more)
+    dz = [jnp.where(section == 1, cotangent[:part], arrived[0])]
+    dc, du = mlp_bwd(dz[0].reshape(part * seq, width), gp, wup, wdown, True, 0, parts)
+    dz.append(jnp.where(section == 1, cotangent[part:], held(arrived[1], dc)))
+    last = dz[1].reshape(part * seq, width)
     dz = jnp.concatenate(dz)
-    dc, du = more
-    dc = dc.reshape(tokens.shape)
     g_down = down_grad(g, dz.reshape(n, width))
     sum_down = lax.psum_scatter(g_down, "dp", scatter_dimension=0, tiled=True).astype(F32)
-    keep_u, send_u, bup_u = up_grad(c, order, du, 0, 1, (g_down,))
+    dc, keep_u, send_u, bup_u = mlp_grad(last, gp, wup, wdown, du, c, order, dc, (g_down,))
+    dc = dc.reshape(tokens.shape)
     if by_hand:
         got_u = hop(send_u, "core")
         half = ff // 2
         mine_a, got_a = y_step(keep_u[:, :half], got_u[:, :half])
-        mine_b, got_b = y_step(keep_u[:, half:], held(got_u[:, half:], got_a))
-        back = attn_bwd(dc, dz, m, h, qkv, e, o, inv, proj, vec, 0, 2, True, (), (got_u,))
-        terms_a = z_step(mine_a, got_a)
-        back = attn_bwd(dc, dz, m, h, qkv, e, o, inv, proj, vec, 1, 2, True, back, (got_a,))
-        terms_b = z_step(mine_b, got_b)
-        wait = (got_b, *terms_a[2:])
+        mine_b, got_b = y_step(keep_u[:, half:], got_u[:, half:])
+        back = attn_bwd(dc, dz, m, h, qkv, e, o, inv, proj, vec, 0, 1, True, (), (got_u,))
+        terms_a = z_step(mine_a, held(got_a, back[3]))
+        wait = (got_a,)
     else:
         back = attn_bwd(dc, dz, m, h, qkv, e, o, inv, proj, vec, 0, 1, True)
         wait = ()
@@ -661,8 +768,9 @@
     keep_p, send_p = proj_grad(
         a.reshape(n, width), dqkv.reshape(n, 3 * width), o.reshape(n, width), dr.reshape(n, width), g_table, order, wait)
     if by_hand:
+        terms_b = z_step(mine_b, got_b)
         sum_up = jnp.concatenate([total(terms_a), total(terms_b)], axis=1)
-        mine_p, got_p = y_step(keep_p, hop(send_p, "core"))
+        mine_p, got_p = y_step(keep_p, hop(held(send_p, got_b, *terms_a[3:]), "core"))
         sum_proj = total(z_step(mine_p, held(got_p, *terms_b)))
     else:
         scatter = lambda *halves: lax.psum_scatter(jnp.concatenate(halves), "dp", scatter_dimension=0, tiled=True).astype(F32)

time: 507 us -> 478 us (0.943)
  the two profiles are of different devices: /device:TPU:11 before, /device:TPU:10 now
where the time goes in v4:
time: 478 us; the launch traced here: 468 us
  Pallas kernels  240 us (50%)
  waiting for transfers between devices  135 us (28%)
  starting transfers between devices  42.4 us (9%)
  other arithmetic  23.2 us (5%)
  between operations  14.9 us (3%)
  local copies, waits for them, and re-layouts  13 us (3%)
    ppermute x44, waiting for transfers between devices, hop(): return lax.ppermute(value, 'dp', pairs)  125 us
    pallas_call x3, Pallas kernels, attn_bwd(): pl.pallas_call(body, grid=(count,), in_specs=in_specs, out_specs=specs, o...  58.6 us
    pallas_call x1, Pallas kernels, mlp_both(): pl.pallas_call(lambda *refs: mlp_both_body(rows, *refs), grid=(ff // chun...  43.8 us
    pallas_call x3, Pallas kernels, attn_fwd(): pl.pallas_call(lambda *refs: attn_fwd_body(save, at * count, *refs[:4], *...  39.6 us
    ppermute x44, starting transfers between devices, hop(): return lax.ppermute(value, 'dp', pairs)  36.5 us
    pallas_call x1, Pallas kernels, mlp_grad(): pl.pallas_call(lambda *refs: mlp_grad_body(rows, *refs[:7], *refs[7 + wai...  22.5 us
    pallas_call x1, Pallas kernels, mlp_bwd(): pl.pallas_call(lambda *refs: mlp_bwd_body(save, rows, *refs[:4], *refs[le...  13.5 us
    pallas_call x1, Pallas kernels, mlp_up(): pl.pallas_call(lambda *refs: mlp_up_body(rows, *refs[:3], *refs[3 + waits...  13.1 us
  transfers between devices with their start and end apart: 50, of which 26 were waited for; matrix products, arithmetic and copies ran while one was open for 6% of the time, Pallas kernels for 26%

profile of v4, /device:TPU:10, one launch (start us, length us, event | category | flops | bytes accessed | tf_op | source)
XLA Modules:
  0.0 468.0 jit_solution(10827443356071500462)
XLA Ops:
  17.4 12.2 %collective-permute-done.refs_2_ = bf16[40,2688]{1,0:T(8,128)(2,1)S(1)} collective-permute-done((bf16[40,2688]{1,0:T(8,128)(2,1)S(1)}, bf16[40,2688]{1,0:T(8,128)(2,1)S(1)}, u32[]{:S(2)}, u32[]{:S(2)}) %collective-permute-start) | collective-permute-done | bytes 215072 | tf_op jit(solution)/shard_map/ppermute | solution.py:615
  29.6 14.9 %collective-permute-done.1.refs_3_ = bf16[40,2688]{1,0:T(8,128)(2,1)S(1)} collective-permute-done((bf16[40,2688]{1,0:T(8,128)(2,1)S(1)}, bf16[40,2688]{1,0:T(8,128)(2,1)S(1)}, u32[]{:S(2)}, u32[]{:S(2)}) %collective-permute-start.1) | collective-permute-done | bytes 215072 | tf_op jit(solution)/shard_map/ppermute | solution.py:615
  44.5 4.0 collective-permute-done.2.refs_4_
  53.3 9.5 %collective-permute-done.7.refs_8_ = bf16[40,2688]{1,0:T(8,128)(2,1)S(1)} collective-permute-done((bf16[40,2688]{1,0:T(8,128)(2,1)S(1)}, bf16[40,2688]{1,0:T(8,128)(2,1)S(1)}, u32[]{:S(2)}, u32[]{:S(2)}) %collective-permute-start.7) | collective-permute-done | bytes 215072 | tf_op jit(solution)/shard_map/ppermute | solution.py:615
  62.8 9.3 %collective-permute-done.6.refs_7_ = bf16[40,2688]{1,0:T(8,128)(2,1)} collective-permute-done((bf16[40,2688]{1,0:T(8,128)(2,1)S(1)}, bf16[40,2688]{1,0:T(8,128)(2,1)}, u32[]{:S(2)}, u32[]{:S(2)}) %collective-permute-start.6) | collective-permute-done | bytes 215072 | tf_op jit(solution)/shard_map/ppermute | solution.py:615
  72.1 7.6 %collective-permute-done.5.refs_6_ = bf16[40,2688]{1,0:T(8,128)(2,1)} collective-permute-done((bf16[40,2688]{1,0:T(8,128)(2,1)S(1)}, bf16[40,2688]{1,0:T(8,128)(2,1)}, u32[]{:S(2)}, u32[]{:S(2)}) %collective-permute-start.5) | collective-permute-done | bytes 215072 | tf_op jit(solution)/shard_map/ppermute | solution.py:615
  84.6 6.6 %collective-permute-start.18 = (bf16[320,640]{1,0:T(8,128)(2,1)}, bf16[320,640]{1,0:T(8,128)(2,1)S(1)}, u32[]{:S(2)}, u32[]{:S(2)}) collective-permute-start(bf16[320,640]{1,0:T(8,128)(2,1)} %bitcast.90), channel_id=1, source_target_pairs={{0,8},{1,9},{2,10},{3,11},{4,12},{5,13},{6,14},{7,15},{8,0},{9,1},... | collective-permute-start | bytes 1228808 | tf_op jit(solution)/shard_map/ppermute | solution.py:615
  93.2 4.7 %place_pieces.1 = bf16[16,40,2688]{2,1,0:T(8,128)(2,1)} custom-call(s32[16]{0:T(128)} %stack.67.refs_0_, bf16[40,2688]{1,0:T(8,128)(2,1)} %copy-done.8, bf16[40,2688]{1,0:T(8,128)(2,1)} %copy-done.22, bf16[40,2688]{1,0:T(8,128)(2,1)} %copy-done.23, bf16[40,2688]{1,0:T(8,128)(2,1)} %copy-done.24, bf16[40,2688]{1,0:T(8,128)(2,1)} %copy-done.25, ...), custom_call_target="tpu_custom_call" | custom-call | flops 4400000000 | bytes 1024 | tf_op jit(solution)/shard_map/place_pieces/pallas_call | solution.py:560
  99.7 16.8 %attention_forward.3 = (f32[4,256,640]{2,1,0:T(8,128)}, bf16[4,256,640]{2,1,0:T(8,128)(2,1)}) custom-call(s32[4]{0:T(128)} %refs_0_.5, bf16[4,256,640]{2,1,0:T(8,128)(2,1)} %refs_1_.3, bf16[640,2688]{1,0:T(8,128)(2,1)} %bitcast.70, f32[8,640]{1,0:T(8,128)} %convert_bitcast_fusion.refs_3_.refs_6_.refs_9_), custom_call_target="tpu_custom_call" | custom-call | flops 19800000512 | bytes 1024 | tf_op jit(solution)/shard_map/attention_forward/pallas_call | solution.py:118
  117.4 13.1 %feed_forward_up.1.refs_1_.refs_0_ = bf16[1024,5120]{1,0:T(8,128)(2,1)} custom-call(bf16[1024,640]{1,0:T(8,128)(2,1)} %bitcast.107, bf16[640,5120]{1,0:T(8,128)(2,1)} %bitcast.81, f32[1,5120]{1,0:T(1,128)} %reshape.199.refs_2_.refs_5_), custom_call_target="tpu_custom_call" | custom-call | flops 14080000000 | bytes 1024 | tf_op jit(solution)/shard_map/feed_forward_up/pallas_call | solution.py:235
  137.3 11.0 %place_and_feed_forward_down.1 = (bf16[5120,640]{1,0:T(8,128)(2,1)}, bf16[512,640]{1,0:T(8,128)(2,1)}) custom-call(s32[16]{0:T(128)} %stack.67.refs_0_, bf16[1024,5120]{1,0:T(8,128)(2,1)} %feed_forward_up.1.refs_1_.refs_0_, f32[1024,640]{1,0:T(8,128)} %bitcast.95, f32[8,640]{1,0:T(8,128)} %convert_bitcast_fusion.refs_3_.refs_6_.refs_9_, ...), custom_call_target="tpu_custom_call" | custom-call | flops 11000000512 | bytes 1024 | tf_op jit(solution)/shard_map/place_and_feed_forward_down/pallas_call | solution.py:590
  149.8 8.9 %feed_forward_down.1 = bf16[512,640]{1,0:T(8,128)(2,1)} custom-call(bf16[1024,5120]{1,0:T(8,128)(2,1)} %feed_forward_up.1.refs_1_.refs_0_, f32[1024,640]{1,0:T(8,128)} %bitcast.96, bf16[5120,640]{1,0:T(8,128)(2,1)} %get-tuple-element.99.refs_2_.refs_4_.refs_3_, f32[8,640]{1,0:T(8,128)} %convert_bitcast_fusion.refs_3_.refs_6_.refs_9_), custom_call_target="tpu_custom_call" | custom-call | flops 9574400000 | bytes 1024 | tf_op jit(solution)/shard_map/feed_forward_down/pallas_call | solution.py:265
  160.0 8.0 %collective-permute-done.31 = bf16[2,256,640]{2,1,0:T(8,128)(2,1)S(1)} collective-permute-done((bf16[2,256,640]{2,1,0:T(8,128)(2,1)}, bf16[2,256,640]{2,1,0:T(8,128)(2,1)S(1)}, u32[]{:S(2)}, u32[]{:S(2)}) %collective-permute-start.31) | collective-permute-done | bytes 655392 | tf_op jit(solution)/shard_map/ppermute | solution.py:730
  168.9 11.4 %attention_forward.4 = (f32[4,256,640]{2,1,0:T(8,128)}, bf16[4,256,640]{2,1,0:T(8,128)(2,1)}, bf16[4,256,1920]{2,1,0:T(8,128)(2,1)}, bf16[4,20,256,256]{3,2,1,0:...) custom-call(s32[4]{0:T(128)} %refs_0_.5, ...), custom_call_target="tpu_custom_call" | custom-call | flops 9900000256 | bytes 1024 | tf_op jit(solution)/shard_map/attention_forward/pallas_call | solution.py:118
  182.7 11.4 %attention_forward.5 = (f32[4,256,640]{2,1,0:T(8,128)}, bf16[4,256,640]{2,1,0:T(8,128)(2,1)}, bf16[4,256,1920]{2,1,0:T(8,128)(2,1)}, bf16[4,20,256,256]{3,2,1,0:...) custom-call(s32[4]{0:T(128)} %refs_0_.5, ...), custom_call_target="tpu_custom_call", output_to_operand_aliasing={{0}: (4, {}), {1}: (5, {}), {2}: (6, {}), {3}: (7, {}), {4}... | custom-call | flops 9900000256 | bytes 1024 | tf_op jit(solution)/shard_map/attention_forward/pallas_call | solution.py:118
  194.1 43.8 %feed_forward_both.1 = (bf16[1024,640]{1,0:T(8,128)(2,1)}, bf16[1024,5120]{1,0:T(8,128)(2,1)}, bf16[1024,5120]{1,0:T(8,128)(2,1)}, f32[1024,640]{1,0:T(8,128)}) custom-call(bf16[1024,640]{1,0:T(8,128)(2,1)} %bitcast.103, f32[1024,640]{1,0:T(8,128)} %bitcast.97, bf16[1024,640]{1,0:T(8,128)(2,1)} %bitcast.63, bf16[640,5120]{1,0:T(8,128)(2,1)} %bitcast.82, ...), custom_call_target="tpu_custom_call" | custom-call | flops 46200000512 | bytes 1024 | tf_op jit(solution)/shard_map/feed_forward_both/pallas_call | solution.py:210
  238.0 15.8 %attention_back.4 = bf16[2,256,640]{2,1,0:T(8,128)(2,1)} custom-call(f32[4,256,640]{2,1,0:T(8,128)} %bitcast.99, bf16[4,256,640]{2,1,0:T(8,128)(2,1)} %refs_1_.5, f32[4,256,640]{2,1,0:T(8,128)} %get-tuple-element.110.refs_2_, bf16[4,256,640]{2,1,0:T(8,128)(2,1)} %pad_maximum_fusion.refs_3_, bf16[4,256,1920]{2,1,0:T(8,128)(2,1)} %get-tuple-element.113.refs_4_, ...), custom_call_target="tpu_custom_call" | custom-call | flops 15399999488 | bytes 1024 | tf_op jit(solution)/shard_map/attention_back/pallas_call | solution.py:498
  255.4 15.6 %attention_back.3 = bf16[2,256,640]{2,1,0:T(8,128)(2,1)} custom-call(f32[4,256,640]{2,1,0:T(8,128)} %bitcast.100, bf16[4,256,640]{2,1,0:T(8,128)(2,1)} %refs_1_.5, f32[4,256,640]{2,1,0:T(8,128)} %get-tuple-element.110.refs_2_, bf16[4,256,640]{2,1,0:T(8,128)(2,1)} %pad_maximum_fusion.refs_3_, bf16[4,256,1920]{2,1,0:T(8,128)(2,1)} %get-tuple-element.113.refs_4_, ...), custom_call_target="tpu_custom_call" | custom-call | flops 15399999488 | bytes 1024 | tf_op jit(solution)/shard_map/attention_back/pallas_call | solution.py:498
  273.3 13.5 %feed_forward_back.1 = (f32[1024,640]{1,0:T(8,128)}, bf16[512,5120]{1,0:T(8,128)(2,1)}) custom-call(bf16[512,640]{1,0:T(8,128)(2,1)} %bitcast.62, bf16[1024,5120]{1,0:T(8,128)(2,1)} %get-tuple-element.117.refs_1_, bf16[640,5120]{1,0:T(8,128)(2,1)} %bitcast.83, bf16[5120,640]{1,0:T(8,128)(2,1)} %get-tuple-element.99.refs_2_.refs_4_.refs_3_), custom_call_target="tpu_custom_call" | custom-call | flops 12099999744 | bytes 1024 | tf_op jit(solution)/shard_map/feed_forward_back/pallas_call | solution.py:302
  289.2 12.4 %down_gradient.1.refs_8_ = bf16[5120,640]{1,0:T(8,128)(2,1)} custom-call(bf16[1024,5120]{1,0:T(8,128)(2,1)} %get-tuple-element.121.refs_0_, bf16[1024,640]{1,0:T(8,128)(2,1)} %bitcast.64), custom_call_target="tpu_custom_call" | custom-call | flops 13200000000 | bytes 1024 | tf_op jit(solution)/shard_map/down_gradient/pallas_call | solution.py:400
  301.6 22.5 %feed_forward_gradients.1 = (f32[1024,640]{1,0:T(8,128)}, bf16[320,5120]{1,0:T(8,128)(2,1)}, bf16[320,5120]{1,0:T(8,128)(2,1)}, f32[8,5120]{1,0:T(8,128)}) custom-call(bf16[512,640]{1,0:T(8,128)(2,1)} %bitcast.61, bf16[1024,5120]{1,0:T(8,128)(2,1)} %get-tuple-element.117.refs_1_, bf16[640,5120]{1,0:T(8,128)(2,1)} %bitcast.84, ...), custom_call_target="tpu_custom_call", output_to_operand_aliasing={{0}: (7, {})} | custom-call | flops 23100000256 | bytes 1024 | tf_op jit(solution)/shard_map/feed_forward_gradients/pallas_call | solution.py:377
  326.3 4.1 collective-permute-done.34.refs_10_
  330.4 3.0 add_convert_fusion.1
  335.3 27.3 %attention_back.5 = (f32[4,256,640]{2,1,0:T(8,128)}, bf16[4,256,640]{2,1,0:T(8,128)(2,1)}, bf16[4,256,1920]{2,1,0:T(8,128)(2,1)}, f32[8,640]{1,0:T(8,128)}) custom-call(f32[4,256,640]{2,1,0:T(8,128)} %bitcast.98, bf16[4,256,640]{2,1,0:T(8,128)(2,1)} %pad_maximum_fusion.1.refs_1_, f32[4,256,640]{2,1,0:T(8,128)} %get-tuple-element.110.refs_2_, ...), custom_call_target="tpu_custom_call" | custom-call | flops 30799998976 | bytes 1024 | tf_op jit(solution)/shard_map/attention_back/pallas_call | solution.py:498
  369.9 11.8 %projection_gradients.1 = (bf16[320,2688]{1,0:T(8,128)(2,1)}, bf16[320,2688]{1,0:T(8,128)(2,1)}) custom-call(bf16[1024,640]{1,0:T(8,128)(2,1)} %bitcast.106, bf16[1024,1920]{1,0:T(8,128)(2,1)} %bitcast.93, bf16[1024,640]{1,0:T(8,128)(2,1)} %bitcast.105, bf16[1024,640]{1,0:T(8,128)(2,1)} %bitcast.102, f32[640,128]{1,0:T(8,128)} %select_maximum_fusion.refs_4_, ...), custom_call_target="tpu_custom_call" | custom-call | flops 9900000256 | bytes 1024 | tf_op jit(solution)/shard_map/projection_gradients/pallas_call | solution.py:534
  381.7 5.8 %collective-permute-done.36 = bf16[160,2560]{1,0:T(8,128)(2,1)} collective-permute-done((bf16[160,2560]{1,0:T(8,128)(2,1)}, bf16[160,2560]{1,0:T(8,128)(2,1)}, u32[]{:S(2)}, u32[]{:S(2)}) %collective-permute-start.36) | collective-permute-done | bytes 819232 | tf_op jit(solution)/shard_map/ppermute | solution.py:615
  387.4 8.9 %collective-permute-done.38 = bf16[40,2560]{1,0:T(8,128)(2,1)S(1)} collective-permute-done((bf16[40,2560]{1,0:T(8,128)(2,1)S(1)}, bf16[40,2560]{1,0:T(8,128)(2,1)S(1)}, u32[]{:S(2)}, u32[]{:S(2)}) %collective-permute-start.38) | collective-permute-done | bytes 204832 | tf_op jit(solution)/shard_map/ppermute | solution.py:615
  405.7 3.5 collective-permute-done.42
  409.2 19.3 %collective-permute-done.43 = bf16[40,2560]{1,0:T(8,128)(2,1)S(1)} collective-permute-done((bf16[40,2560]{1,0:T(8,128)(2,1)S(1)}, bf16[40,2560]{1,0:T(8,128)(2,1)S(1)}, u32[]{:S(2)}, u32[]{:S(2)}) %collective-permute-start.43) | collective-permute-done | bytes 204832 | tf_op jit(solution)/shard_map/ppermute | solution.py:615
  428.5 2.8 collective-permute-done.44
  437.2 3.8 collective-permute-done.45
  441.0 10.8 %collective-permute-done.46 = bf16[40,2688]{1,0:T(8,128)(2,1)S(1)} collective-permute-done((bf16[40,2688]{1,0:T(8,128)(2,1)S(1)}, bf16[40,2688]{1,0:T(8,128)(2,1)S(1)}, u32[]{:S(2)}, u32[]{:S(2)}) %collective-permute-start.46) | collective-permute-done | bytes 215072 | tf_op jit(solution)/shard_map/ppermute | solution.py:615
  (186 shorter events, 79.2 us)
Async XLA Ops:
  7.2 110.2 %all-gather.3.cloned.1.call-start = ((), (), s32[]{:S(2)}) async-start(), calls=%async_computation.2 | async-start | bytes 6963200 | tf_op jit(solution)/shard_map/all_gather | solution.py:696
  7.9 450.9 %reduce-scatter.2.cloned.1.call-start = ((), (), s32[]{:S(2)}) async-start(), calls=%async_computation.1 | async-start | bytes 6963200 | tf_op jit(solution)/shard_map/reduce_scatter | solution.py:750
  8.0 40.6 %collective-permute-start.4 = (bf16[320,640]{1,0:T(8,128)(2,1)}, bf16[320,640]{1,0:T(8,128)(2,1)S(1)}, u32[]{:S(2)}, u32[]{:S(2)}) collective-permute-start(bf16[320,640]{1,0:T(8,128)(2,1)} %bitcast.87), channel_id=1, source_target_pairs={{0,2},{1,3},{2,0},{3,1},{4,6},{5,7},{6,4},{7,5},{8,10},{9,11},{10,... | collective-permute-start | bytes 1228808 | tf_op jit(solution)/shard_map/ppermute | solution.py:615
  12.2 17.3 %collective-permute-start = (bf16[40,2688]{1,0:T(8,128)(2,1)S(1)}, bf16[40,2688]{1,0:T(8,128)(2,1)S(1)}, u32[]{:S(2)}, u32[]{:S(2)}) collective-permute-start(bf16[40,2688]{1,0:T(8,128)(2,1)S(1)} %pad_maximum_fusion.2.refs_1_), channel_id=1, source_target_pairs={{0,4},{1,5},{2,6},{3,7},{4,8},{5,9},{6,10},{7,11},{8,12},{9,13},{1... | collective-permute-start | bytes 645128 | tf_op jit(solution)/shard_map/ppermute | solution.py:615
  13.8 30.6 %collective-permute-start.1 = (bf16[40,2688]{1,0:T(8,128)(2,1)S(1)}, bf16[40,2688]{1,0:T(8,128)(2,1)S(1)}, u32[]{:S(2)}, u32[]{:S(2)}) collective-permute-start(bf16[40,2688]{1,0:T(8,128)(2,1)S(1)} %pad_maximum_fusion.2.refs_1_), channel_id=1, source_target_pairs={{0,8},{1,9},{2,10},{3,11},{4,12},{5,13},{6,14},{7,15},{8,0},{9,1},... | collective-permute-start | bytes 645128 | tf_op jit(solution)/shard_map/ppermute | solution.py:615
  15.1 33.4 %collective-permute-start.2 = (bf16[40,2688]{1,0:T(8,128)(2,1)S(1)}, bf16[40,2688]{1,0:T(8,128)(2,1)S(1)}, u32[]{:S(2)}, u32[]{:S(2)}) collective-permute-start(bf16[40,2688]{1,0:T(8,128)(2,1)S(1)} %pad_maximum_fusion.2.refs_1_), channel_id=1, source_target_pairs={{0,12},{1,13},{2,14},{3,15},{4,0},{5,1},{6,2},{7,3},{8,4},{9,5},{1... | collective-permute-start | bytes 645128 | tf_op jit(solution)/shard_map/ppermute | solution.py:615
  16.9 31.6 %collective-permute-start.3 = (bf16[40,2688]{1,0:T(8,128)(2,1)S(1)}, bf16[40,2688]{1,0:T(8,128)(2,1)S(1)}, u32[]{:S(2)}, u32[]{:S(2)}) collective-permute-start(bf16[40,2688]{1,0:T(8,128)(2,1)S(1)} %pad_maximum_fusion.2.refs_1_), channel_id=1, source_target_pairs={{0,2},{1,3},{2,0},{3,1},{4,6},{5,7},{6,4},{7,5},{8,10},{9,11},{10,... | collective-permute-start | bytes 645128 | tf_op jit(solution)/shard_map/ppermute | solution.py:615
  48.5 31.2 %collective-permute-start.8 = (bf16[320,640]{1,0:T(8,128)(2,1)}, bf16[320,640]{1,0:T(8,128)(2,1)S(1)}, u32[]{:S(2)}, u32[]{:S(2)}) collective-permute-start(bf16[320,640]{1,0:T(8,128)(2,1)} %bitcast.88), channel_id=1, source_target_pairs={{0,4},{1,5},{2,6},{3,7},{4,8},{5,9},{6,10},{7,11},{8,12},{9,13},{1... | collective-permute-start | bytes 1228808 | tf_op jit(solution)/shard_map/ppermute | solution.py:615
  48.6 31.4 %collective-permute-start.9 = (bf16[320,640]{1,0:T(8,128)(2,1)}, bf16[320,640]{1,0:T(8,128)(2,1)S(1)}, u32[]{:S(2)}, u32[]{:S(2)}) collective-permute-start(bf16[320,640]{1,0:T(8,128)(2,1)} %bitcast.89), channel_id=1, source_target_pairs={{0,12},{1,13},{2,14},{3,15},{4,0},{5,1},{6,2},{7,3},{8,4},{9,5},{1... | collective-permute-start | bytes 1228808 | tf_op jit(solution)/shard_map/ppermute | solution.py:615
  50.6 12.2 %collective-permute-start.7 = (bf16[40,2688]{1,0:T(8,128)(2,1)S(1)}, bf16[40,2688]{1,0:T(8,128)(2,1)S(1)}, u32[]{:S(2)}, u32[]{:S(2)}) collective-permute-start(bf16[40,2688]{1,0:T(8,128)(2,1)S(1)} %collective-permute-done.2.refs_4_), channel_id=1, source_target_pairs={{0,2},{1,3},{2,0},{3,1},{4,6},{5,7},{6,4},{7,5},{8,10},{9,11},{10,... | collective-permute-start | bytes 645128 | tf_op jit(solution)/shard_map/ppermute | solution.py:615
  51.3 20.8 %collective-permute-start.6 = (bf16[40,2688]{1,0:T(8,128)(2,1)S(1)}, bf16[40,2688]{1,0:T(8,128)(2,1)}, u32[]{:S(2)}, u32[]{:S(2)}) collective-permute-start(bf16[40,2688]{1,0:T(8,128)(2,1)S(1)} %collective-permute-done.1.refs_3_), channel_id=1, source_target_pairs={{0,2},{1,3},{2,0},{3,1},{4,6},{5,7},{6,4},{7,5},{8,10},{9,11},{10,... | collective-permute-start | bytes 645128 | tf_op jit(solution)/shard_map/ppermute | solution.py:615
  52.6 27.1 %collective-permute-start.5 = (bf16[40,2688]{1,0:T(8,128)(2,1)S(1)}, bf16[40,2688]{1,0:T(8,128)(2,1)}, u32[]{:S(2)}, u32[]{:S(2)}) collective-permute-start(bf16[40,2688]{1,0:T(8,128)(2,1)S(1)} %collective-permute-done.refs_2_), channel_id=1, source_target_pairs={{0,2},{1,3},{2,0},{3,1},{4,6},{5,7},{6,4},{7,5},{8,10},{9,11},{10,... | collective-permute-start | bytes 645128 | tf_op jit(solution)/shard_map/ppermute | solution.py:615
  81.7 11.4 %collective-permute-start.16 = (bf16[40,2688]{1,0:T(8,128)(2,1)}, bf16[40,2688]{1,0:T(8,128)(2,1)}, u32[]{:S(2)}, u32[]{:S(2)}) collective-permute-start(bf16[40,2688]{1,0:T(8,128)(2,1)} %collective-permute-done.6.refs_7_), channel_id=1, source_target_pairs={{0,1},{1,0},{2,3},{3,2},{4,5},{5,4},{6,7},{7,6},{8,9},{9,8},{10,11... | collective-permute-start | bytes 645128 | tf_op jit(solution)/shard_map/ppermute | solution.py:615
  82.7 10.4 %collective-permute-start.15 = (bf16[40,2688]{1,0:T(8,128)(2,1)}, bf16[40,2688]{1,0:T(8,128)(2,1)}, u32[]{:S(2)}, u32[]{:S(2)}) collective-permute-start(bf16[40,2688]{1,0:T(8,128)(2,1)} %collective-permute-done.5.refs_6_), channel_id=1, source_target_pairs={{0,1},{1,0},{2,3},{3,2},{4,5},{5,4},{6,7},{7,6},{8,9},{9,8},{10,11... | collective-permute-start | bytes 645128 | tf_op jit(solution)/shard_map/ppermute | solution.py:615
  83.6 33.7 %collective-permute-start.20 = (bf16[320,640]{1,0:T(8,128)(2,1)S(1)}, bf16[320,640]{1,0:T(8,128)(2,1)S(1)}, u32[]{:S(2)}, u32[]{:S(2)}) collective-permute-start(bf16[320,640]{1,0:T(8,128)(2,1)S(1)} %collective-permute-done.9.refs_7_), channel_id=1, source_target_pairs={{0,2},{1,3},{2,0},{3,1},{4,6},{5,7},{6,4},{7,5},{8,10},{9,11},{10,... | collective-permute-start | bytes 1228808 | tf_op jit(solution)/shard_map/ppermute | solution.py:615
  84.6 32.7 %collective-permute-start.18 = (bf16[320,640]{1,0:T(8,128)(2,1)}, bf16[320,640]{1,0:T(8,128)(2,1)S(1)}, u32[]{:S(2)}, u32[]{:S(2)}) collective-permute-start(bf16[320,640]{1,0:T(8,128)(2,1)} %bitcast.90), channel_id=1, source_target_pairs={{0,8},{1,9},{2,10},{3,11},{4,12},{5,13},{6,14},{7,15},{8,0},{9,1},... | collective-permute-start | bytes 1228808 | tf_op jit(solution)/shard_map/ppermute | solution.py:615
  91.2 26.1 %collective-permute-start.19 = (bf16[320,640]{1,0:T(8,128)(2,1)S(1)}, bf16[320,640]{1,0:T(8,128)(2,1)S(1)}, u32[]{:S(2)}, u32[]{:S(2)}) collective-permute-start(bf16[320,640]{1,0:T(8,128)(2,1)S(1)} %collective-permute-done.8.refs_5_), channel_id=1, source_target_pairs={{0,2},{1,3},{2,0},{3,1},{4,6},{5,7},{6,4},{7,5},{8,10},{9,11},{10,... | collective-permute-start | bytes 1228808 | tf_op jit(solution)/shard_map/ppermute | solution.py:615
  117.3 13.2 %collective-permute-start.21 = (bf16[320,640]{1,0:T(8,128)(2,1)S(1)}, bf16[320,640]{1,0:T(8,128)(2,1)S(1)}, u32[]{:S(2)}, u32[]{:S(2)}) collective-permute-start(bf16[320,640]{1,0:T(8,128)(2,1)S(1)} %collective-permute-done.18.refs_6_), channel_id=1, source_target_pairs={{0,2},{1,3},{2,0},{3,1},{4,6},{5,7},{6,4},{7,5},{8,10},{9,11},{10,... | collective-permute-start | bytes 1228808 | tf_op jit(solution)/shard_map/ppermute | solution.py:615
  148.3 19.7 %collective-permute-start.31 = (bf16[2,256,640]{2,1,0:T(8,128)(2,1)}, bf16[2,256,640]{2,1,0:T(8,128)(2,1)S(1)}, u32[]{:S(2)}, u32[]{:S(2)}) collective-permute-start(bf16[2,256,640]{2,1,0:T(8,128)(2,1)} %bitcast.85), channel_id=1, source_target_pairs={{0,16},{1,17},{2,18},{3,19},{4,20},{5,21},{6,22},{7,23},{8,24},{9,... | collective-permute-start | bytes 1966088 | tf_op jit(solution)/shard_map/ppermute | solution.py:730
  158.7 22.5 %collective-permute-start.30 = (bf16[2,256,640]{2,1,0:T(8,128)(2,1)}, bf16[2,256,640]{2,1,0:T(8,128)(2,1)S(1)}, u32[]{:S(2)}, u32[]{:S(2)}) collective-permute-start(bf16[2,256,640]{2,1,0:T(8,128)(2,1)} %bitcast.86), channel_id=1, source_target_pairs={{0,16},{1,17},{2,18},{3,19},{4,20},{5,21},{6,22},{7,23},{8,24},{9,... | collective-permute-start | bytes 1966088 | tf_op jit(solution)/shard_map/ppermute | solution.py:730
  253.7 18.6 %collective-permute-start.33 = (bf16[2,256,640]{2,1,0:T(8,128)(2,1)}, bf16[2,256,640]{2,1,0:T(8,128)(2,1)S(1)}, u32[]{:S(2)}, u32[]{:S(2)}) collective-permute-start(bf16[2,256,640]{2,1,0:T(8,128)(2,1)} %attention_back.4), channel_id=1, source_target_pairs={{16,0},{17,1},{18,2},{19,3},{20,4},{21,5},{22,6},{23,7},{24,8},{25... | collective-permute-start | bytes 1966088 | tf_op jit(solution)/shard_map/ppermute | solution.py:743
  271.0 15.8 %collective-permute-start.32 = (bf16[2,256,640]{2,1,0:T(8,128)(2,1)}, bf16[2,256,640]{2,1,0:T(8,128)(2,1)S(1)}, u32[]{:S(2)}, u32[]{:S(2)}) collective-permute-start(bf16[2,256,640]{2,1,0:T(8,128)(2,1)} %attention_back.3), channel_id=1, source_target_pairs={{16,0},{17,1},{18,2},{19,3},{20,4},{21,5},{22,6},{23,7},{24,8},{25... | collective-permute-start | bytes 1966088 | tf_op jit(solution)/shard_map/ppermute | solution.py:743
  333.3 32.9 %collective-permute-start.35 = (bf16[160,2560]{1,0:T(8,128)(2,1)}, bf16[160,2560]{1,0:T(8,128)(2,1)}, u32[]{:S(2)}, u32[]{:S(2)}) collective-permute-start(bf16[160,2560]{1,0:T(8,128)(2,1)} %get-tuple-element.184), channel_id=1, source_target_pairs={{0,2},{1,3},{2,0},{3,1},{4,6},{5,7},{6,4},{7,5},{8,10},{9,11},{10,... | collective-permute-start | bytes 2457608 | tf_op jit(solution)/shard_map/ppermute | solution.py:615
  335.0 52.5 %collective-permute-start.36 = (bf16[160,2560]{1,0:T(8,128)(2,1)}, bf16[160,2560]{1,0:T(8,128)(2,1)}, u32[]{:S(2)}, u32[]{:S(2)}) collective-permute-start(bf16[160,2560]{1,0:T(8,128)(2,1)} %get-tuple-element.183), channel_id=1, source_target_pairs={{0,2},{1,3},{2,0},{3,1},{4,6},{5,7},{6,4},{7,5},{8,10},{9,11},{10,... | collective-permute-start | bytes 2457608 | tf_op jit(solution)/shard_map/ppermute | solution.py:615
  367.8 19.6 %collective-permute-start.37 = (bf16[40,2560]{1,0:T(8,128)(2,1)S(1)}, bf16[40,2560]{1,0:T(8,128)(2,1)S(1)}, u32[]{:S(2)}, u32[]{:S(2)}) collective-permute-start(bf16[40,2560]{1,0:T(8,128)(2,1)S(1)} %get-tuple-element.181), channel_id=1, source_target_pairs={{0,4},{1,5},{2,6},{3,7},{4,8},{5,9},{6,10},{7,11},{8,12},{9,13},{1... | collective-permute-start | bytes 614408 | tf_op jit(solution)/shard_map/ppermute | solution.py:615
  367.9 28.5 %collective-permute-start.38 = (bf16[40,2560]{1,0:T(8,128)(2,1)S(1)}, bf16[40,2560]{1,0:T(8,128)(2,1)S(1)}, u32[]{:S(2)}, u32[]{:S(2)}) collective-permute-start(bf16[40,2560]{1,0:T(8,128)(2,1)S(1)} %get-tuple-element.180), channel_id=1, source_target_pairs={{0,8},{1,9},{2,10},{3,11},{4,12},{5,13},{6,14},{7,15},{8,0},{9,1},... | collective-permute-start | bytes 614408 | tf_op jit(solution)/shard_map/ppermute | solution.py:615
  368.3 30.9 %collective-permute-start.39 = (bf16[40,2560]{1,0:T(8,128)(2,1)S(1)}, bf16[40,2560]{1,0:T(8,128)(2,1)S(1)}, u32[]{:S(2)}, u32[]{:S(2)}) collective-permute-start(bf16[40,2560]{1,0:T(8,128)(2,1)S(1)} %get-tuple-element.179), channel_id=1, source_target_pairs={{0,12},{1,13},{2,14},{3,15},{4,0},{5,1},{6,2},{7,3},{8,4},{9,5},{1... | collective-permute-start | bytes 614408 | tf_op jit(solution)/shard_map/ppermute | solution.py:615
  401.3 27.2 %collective-permute-start.43 = (bf16[40,2560]{1,0:T(8,128)(2,1)S(1)}, bf16[40,2560]{1,0:T(8,128)(2,1)S(1)}, u32[]{:S(2)}, u32[]{:S(2)}) collective-permute-start(bf16[40,2560]{1,0:T(8,128)(2,1)S(1)} %get-tuple-element.177), channel_id=1, source_target_pairs={{0,8},{1,9},{2,10},{3,11},{4,12},{5,13},{6,14},{7,15},{8,0},{9,1},... | collective-permute-start | bytes 614408 | tf_op jit(solution)/shard_map/ppermute | solution.py:615
  402.9 28.4 %collective-permute-start.44 = (bf16[40,2560]{1,0:T(8,128)(2,1)S(1)}, bf16[40,2560]{1,0:T(8,128)(2,1)S(1)}, u32[]{:S(2)}, u32[]{:S(2)}) collective-permute-start(bf16[40,2560]{1,0:T(8,128)(2,1)S(1)} %get-tuple-element.176), channel_id=1, source_target_pairs={{0,12},{1,13},{2,14},{3,15},{4,0},{5,1},{6,2},{7,3},{8,4},{9,5},{1... | collective-permute-start | bytes 614408 | tf_op jit(solution)/shard_map/ppermute | solution.py:615
  405.0 27.5 %collective-permute-start.41 = (bf16[160,2688]{1,0:T(8,128)(2,1)S(1)}, bf16[160,2688]{1,0:T(8,128)(2,1)S(1)}, u32[]{:S(2)}, u32[]{:S(2)}) collective-permute-start(bf16[160,2688]{1,0:T(8,128)(2,1)S(1)} %add_convert_fusion), channel_id=1, source_target_pairs={{0,2},{1,3},{2,0},{3,1},{4,6},{5,7},{6,4},{7,5},{8,10},{9,11},{10,... | collective-permute-start | bytes 2580488 | tf_op jit(solution)/shard_map/ppermute | solution.py:615
  432.9 18.9 %collective-permute-start.46 = (bf16[40,2688]{1,0:T(8,128)(2,1)S(1)}, bf16[40,2688]{1,0:T(8,128)(2,1)S(1)}, u32[]{:S(2)}, u32[]{:S(2)}) collective-permute-start(bf16[40,2688]{1,0:T(8,128)(2,1)S(1)} %get-tuple-element.187), channel_id=1, source_target_pairs={{0,8},{1,9},{2,10},{3,11},{4,12},{5,13},{6,14},{7,15},{8,0},{9,1},... | collective-permute-start | bytes 645128 | tf_op jit(solution)/shard_map/ppermute | solution.py:615
  434.3 20.1 %collective-permute-start.47 = (bf16[40,2688]{1,0:T(8,128)(2,1)S(1)}, bf16[40,2688]{1,0:T(8,128)(2,1)S(1)}, u32[]{:S(2)}, u32[]{:S(2)}) collective-permute-start(bf16[40,2688]{1,0:T(8,128)(2,1)S(1)} %get-tuple-element.186), channel_id=1, source_target_pairs={{0,12},{1,13},{2,14},{3,15},{4,0},{5,1},{6,2},{7,3},{8,4},{9,5},{1... | collective-permute-start | bytes 645128 | tf_op jit(solution)/shard_map/ppermute | solution.py:615
  (48 other events, 705.1 us)
Sparse Core Ops, SparseCore 0:
  10.3 94.3 all-gather.2
  324.3 116.2 reduce-scatter.1

commit v5 on v4

--- a/solution.py
+++ b/solution.py
@@ -49,16 +49,22 @@
     return back, jnp.sum(grad * hat, axis=0, keepdims=True), jnp.sum(grad, axis=0, keepdims=True)
 
 
-def attn_fwd_body(save, first_window, len_ref, h_ref, wqkv_ref, vec_ref, *outs):
+def attn_fwd_body(save, first_window, len_ref, h_ref, *rest):
     if save:
-        m_ref, c_ref, qkv_ref, e_ref, o_ref, a_ref, inv_ref = outs
+        arrived_ref, wqkv_ref, vec_ref, m_ref, c_ref, qkv_ref, e_ref, o_ref, a_ref, inv_ref, taken_ref = rest
     else:
-        m_ref, c_ref = outs
+        wqkv_ref, m_ref, c_ref = rest
     width = h_ref.shape[2]
     seq = h_ref.shape[1]
     length = len_ref[pl.program_id(0) + first_window]
-    h = h_ref[0].astype(F32)
-    vec = vec_ref[...]
+    if save:
+        taken = jnp.where(len_ref[len_ref.shape[0] - 1] == 0, h_ref[0], arrived_ref[0])
+        taken_ref[0] = taken
+        h = taken.astype(F32)
+        vec = vec_ref[...]
+    else:
+        h = h_ref[0].astype(F32)
+        vec = wqkv_ref[:, 4 * width:].astype(F32).T
     a = normed(h, vec[0:1], vec[2:3]).astype(BF16)
     q_all = (dot(a, wqkv_ref[:, :width]) + vec[4:5]).astype(BF16)
     k_all = dot(a, wqkv_ref[:, width:2 * width]).astype(BF16)
@@ -81,9 +87,10 @@
         q, v = q_all[:, at], v_all[:, at]
         k = jnp.concatenate([k_all[:, at], past], axis=1)
         acc, inv = None, None
+        stacked = dot(jnp.concatenate([jnp.concatenate([jnp.where(head_of == j, q, zero), first], axis=1) for j in range(GROUP)], axis=0), k, ((1,), (1,)))
         for j in range(GROUP):
             mine = head_of == j
-            s = dot(jnp.concatenate([jnp.where(mine, q, zero), first], axis=1), k, ((1,), (1,)))
+            s = stacked[seq * j:seq * j + seq]
             e = jnp.exp2((s - jnp.max(s, axis=1, keepdims=True)) * (SCALE * LOG2E)).astype(BF16)
             if save:
                 e_ref[0, GROUP * g + j] = e
@@ -107,28 +114,34 @@
     return pl.BlockSpec(shape, lambda *_: (0,) * len(shape))
 
 
-def attn_fwd(h, lengths, proj, vec, save, at=0, parts=1, earlier=(), after=()):
-    count, seq, width = h.shape
-    n = count * parts
+def attn_fwd(h, lengths, proj, save, at=0, parts=1, arrived=None, vec=None, earlier=(), after=()):
+    n, seq, width = h.shape
+    count = n // parts
     row = lambda *tail: pl.BlockSpec((1,) + tail, lambda i, *_: (i + at * count,) + (0,) * len(tail))
     shapes = [((seq, width), F32), ((seq, width), BF16)]
+    args, in_specs = [h], [row(seq, width)]
     if save:
-        shapes += [((seq, 3 * width), BF16), ((HEADS, seq, seq), BF16), ((seq, width), BF16), ((seq, width), BF16), ((seq, width), F32)]
-    waits = len(earlier) + len(after)
-    return pl.pallas_call(
-        lambda *refs: attn_fwd_body(save, at * count, *refs[:4], *refs[4 + waits:]),
+        shapes += [((seq, 3 * width), BF16), ((HEADS, seq, seq), BF16), ((seq, width), BF16), ((seq, width), BF16), ((seq, width), F32), ((seq, width), BF16)]
+        args += [arrived, proj, vec]
+        in_specs += [pl.BlockSpec((1, seq, width), lambda i, *_: (i, 0, 0)), whole(proj.shape), whole(vec.shape)]
+    else:
+        args += [proj]
+        in_specs += [whole(proj.shape)]
+    used, waits = 1 + len(args), len(earlier) + len(after)
+    return pl.pallas_call(
+        lambda *refs: attn_fwd_body(save, at * count, *refs[:used], *refs[used + waits:]),
         grid_spec=pltpu.PrefetchScalarGridSpec(
             num_scalar_prefetch=1,
             grid=(count,),
-            in_specs=[pl.BlockSpec((1, seq, width), lambda i, *_: (i, 0, 0)), whole(proj.shape), whole(vec.shape)] + tied(waits),
+            in_specs=in_specs + tied(waits),
             out_specs=[row(*s) for s, _ in shapes],
         ),
         out_shape=[jax.ShapeDtypeStruct((n,) + s, d) for s, d in shapes],
-        input_output_aliases={4 + i: i for i in range(len(earlier))},
+        input_output_aliases={used + i: i for i in range(len(earlier))},
         compiler_params=pltpu.CompilerParams(vmem_limit_bytes=VMEM_LIMIT),
         cost_estimate=cost(4.5 * count),
         name="attention_forward",
-    )(lengths, h, proj, vec, *earlier, *after)
+    )(lengths, *args, *earlier, *after)
 
 
 def mlp_fwd_body(save, rows, c_ref, m_ref, wup_ref, wdown_ref, bup_ref, vec_ref, *outs):
@@ -443,12 +456,14 @@
         do_t, q_t = do.T, q.T
         dq = None
         dk_t, dv_t = [], []
+        stacked = dot(jnp.concatenate([jnp.concatenate([jnp.where(head_of == j, do, zero), jnp.where(head_of == j, less, zero)], axis=1)
+                                       for j in range(GROUP)], axis=0), v, ((1,), (1,)))
         for j in range(GROUP):
             mine = head_of == j
             e = e_ref[0, GROUP * g + j]
             rows = slice(HEAD_DIM * j, HEAD_DIM * j + HEAD_DIM)
             dv_t.append(dot(do_t[rows], e))
-            dp = dot(jnp.concatenate([jnp.where(mine, do, zero), jnp.where(mine, less, zero)], axis=1), v, ((1,), (1,)))
+            dp = stacked[seq * j:seq * j + seq]
             ds = (e.astype(F32) * dp).astype(BF16)
             part = dot(ds, jnp.where(mine, k, zero))
             dq = part if dq is None else dq + part
@@ -508,7 +523,7 @@
     )(*args)
 
 
-def proj_grad_body(a_ref, dqkv_ref, o_ref, dr_ref, table_ref, order_ref, keep_ref, send_ref, at_ref):
+def proj_grad_body(a_ref, dqkv_ref, o_ref, dr_ref, small_ref, bias_ref, order_ref, keep_ref, send_ref, at_ref):
     step = pl.program_id(0)
     width = a_ref.shape[1]
     half = width // 2
@@ -522,19 +537,20 @@
     def _():
         at_ref[...] = dot(order, a_ref[...], ((1,), (1,))).astype(BF16)
         put(slice(3 * width, 4 * width), dot(dot(order, o_ref[...], ((1,), (1,))).astype(BF16), dr_ref[...]))
-        put(slice(4 * width, None), dot(order, table_ref[...].astype(BF16)))
+        table = jnp.concatenate([small_ref[...], bias_ref[...], jnp.zeros((112, width), F32)], axis=0).astype(BF16)
+        put(slice(4 * width, None), dot(order, table, ((1,), (1,))))
 
     put(pl.ds(pl.multiple_of(step * width, 128), width), dot(at_ref[...], dqkv_ref[...]))
 
 
-def proj_grad(a, dqkv, o, dr, table, order, after=()):
+def proj_grad(a, dqkv, o, dr, small, bias, order, after=()):
     n, width = a.shape
     waits = len(after)
-    shape = (width // 2, 4 * width + table.shape[1])
-    return pl.pallas_call(
-        lambda *refs: proj_grad_body(*refs[:6], *refs[6 + waits:]),
+    shape = (width // 2, 4 * width + 128)
+    return pl.pallas_call(
+        lambda *refs: proj_grad_body(*refs[:7], *refs[7 + waits:]),
         grid=(3,),
-        in_specs=[whole(a.shape), pl.BlockSpec((n, width), lambda i: (0, i)), whole(o.shape), whole(dr.shape), whole(table.shape),
+        in_specs=[whole(a.shape), pl.BlockSpec((n, width), lambda i: (0, i)), whole(o.shape), whole(dr.shape), whole(small.shape), whole(bias.shape),
                   whole(order.shape)] + tied(waits),
         out_specs=[whole(shape)] * 2,
         out_shape=[jax.ShapeDtypeStruct(shape, BF16)] * 2,
@@ -542,7 +558,7 @@
         compiler_params=pltpu.CompilerParams(vmem_limit_bytes=VMEM_LIMIT),
         cost_estimate=cost(9),
         name="projection_gradients",
-    )(a, dqkv, o, dr, table, order, *after)
+    )(a, dqkv, o, dr, small, bias, order, *after)
 
 
 def place_body(count, to_ref, *refs):
@@ -598,6 +614,41 @@
         cost_estimate=cost(10),
         name="place_and_feed_forward_down",
     )(to, g, m, vec, *pieces)
+
+
+def finish_body(rows, per_row, width, *refs):
+    *terms, qkv_ref, out_ref, gain_ref, shift_ref, bias_ref, up_ref = refs
+    total = terms[0][:rows].astype(F32)
+    for term in terms[1:]:
+        total = total + term[:rows].astype(F32)
+    qkv_ref[0] = total[:, :3 * width]
+    out_ref[0] = total[:, 3 * width:4 * width]
+    small = total[:, 4 * width:]
+    vectors = small.T
+    gain_ref[0] = vectors[0:2]
+    shift_ref[0] = vectors[2:4]
+    bias_ref[0] = vectors[4:8]
+    flat = rows * per_row
+    spread = lax.broadcasted_iota(jnp.int32, (128, flat), 1) % per_row + 8 == lax.broadcasted_iota(jnp.int32, (128, flat), 0)
+    wide = lax.dot_general(small, spread.astype(F32), (((1,), (0,)), ((), ())), precision=lax.Precision.HIGHEST, preferred_element_type=F32)
+    here = lax.broadcasted_iota(jnp.int32, (rows, flat), 1) // per_row == lax.broadcasted_iota(jnp.int32, (rows, flat), 0)
+    up_ref[...] = jnp.sum(jnp.where(here, wide, 0.0), axis=0, keepdims=True)
+
+
+def finish(large, pieces, rows, per_row):
+    columns = large[0].shape[1]
+    width = (columns - 128) // 4
+    shapes = [(1, rows, 3 * width), (1, rows, width), (1, 2, rows), (1, 2, rows), (1, 4, rows), (1, rows * per_row)]
+    return pl.pallas_call(
+        lambda *refs: finish_body(rows, per_row, width, *refs),
+        grid=(1,),
+        in_specs=[pl.BlockSpec((2 * rows, columns), lambda i: (0, 0))] * len(large) + [whole(piece.shape) for piece in pieces],
+        out_specs=[whole(s) for s in shapes],
+        out_shape=[jax.ShapeDtypeStruct(s, F32) for s in shapes],
+        compiler_params=pltpu.CompilerParams(vmem_limit_bytes=VMEM_LIMIT),
+        cost_estimate=cost(2),
+        name="gather_projection_gradients",
+    )(*large, *pieces)
 
 
 def places(count):
@@ -694,16 +745,19 @@
         down = w_down[0]
         order, to = scatter_order(shard), places_of_pieces()
         wup = lax.all_gather(w_up[0], "dp", axis=0, tiled=True)
-        proj_z = [hop(packed, "z", step) for step in (1, 2, 3)]
+        proj_1, proj_3 = hop(packed, "z", 1), hop(packed, "z", 3)
         proj_y0, down_y0 = hop(packed, "y"), hop(down, "y")
-        now = (*proj_z, proj_y0, down_y0)
-        down_1, down_3 = hop(held(down, *now), "z", 1), hop(held(down, *now), "z", 3)
-        proj_y = [hop(held(piece, *now), "y") for piece in proj_z]
-        now = (down_1, down_3, *proj_y)
-        pieces = [packed, *proj_z, proj_y0, *proj_y]
-        proj = place(pieces + siblings(pieces, *now), to)
-        down_2 = hop(held(down, *now), "z", 2)
-        down_y1, down_y3 = hop(held(down_1, *now), "y"), hop(held(down_3, *now), "y")
+        now = (proj_1, proj_3, proj_y0, order)
+        proj_2 = hop(held(packed, *now), "z", 2)
+        proj_y1, proj_y3 = hop(held(proj_1, *now), "y"), hop(held(proj_3, *now), "y")
+        now = (proj_2, proj_y1, proj_y3, down_y0)
+        down_1 = hop(held(down, *now), "z", 1)
+        proj_y2 = hop(held(proj_2, *now), "y")
+        now = (down_1, proj_y2)
+        pieces = [packed, proj_1, proj_2, proj_3, proj_y0, proj_y1, proj_y2, proj_y3]
+        proj = place(pieces + siblings(pieces, proj_y2), to)
+        down_2, down_3 = hop(held(down, *now), "z", 2), hop(held(down, *now), "z", 3)
+        down_y1 = hop(held(down_1, *now), "y")
     else:
         order = (jnp.arange(width)[None, :] == jnp.arange(width)[:, None]).astype(BF16)
         proj = lax.all_gather(packed, "dp", axis=0, tiled=True)
@@ -713,12 +767,12 @@
     vec = small[:, :8].T.astype(F32)
     bup = small[:, 8:].reshape(1, ff).astype(F32)
 
-    mid, c = attn_fwd(tokens, lengths, proj, vec, False)
+    mid, c = attn_fwd(tokens, lengths, proj, False)
     c = c.reshape(n, width)
     mid = mid.reshape(n, width)
     if by_hand:
-        now = (down_2, down_y1, down_y3, c)
-        down_y2 = hop(held(down_2, *now), "y")
+        now = (down_2, down_3, down_y1, c)
+        down_y2, down_y3 = hop(held(down_2, *now), "y"), hop(held(down_3, *now), "y")
     act = mlp_up(c, wup, bup)
     if by_hand:
         pieces = [down, down_1, down_2, down_3, down_y0, down_y1, down_y2, down_y3]
@@ -728,12 +782,10 @@
     y_b = mlp_down(act, mid, wdown, vec, 1, parts)
     kept = ()
     arrived = [lax.ppermute(y.reshape(part, seq, width), "section", [(0, 1)]) for y in (y_a, y_b)]
-    h = []
+    lengths = jnp.append(lengths, section)
     for at in range(parts):
-        h.append(jnp.where(section == 0, tokens[at * part:at * part + part], held(arrived[at], *kept[:1])))
-        kept = attn_fwd(h[at], lengths, proj, vec, True, at, parts, kept)
-    h = jnp.concatenate(h)
-    m, c, qkv, e, o, a, inv = kept
+        kept = attn_fwd(tokens, lengths, proj, True, at, parts, held(arrived[at], *kept[:1]), vec, kept)
+    m, c, qkv, e, o, a, inv, h = kept
     c = c.reshape(n, width)
     y, g, gp, dc = mlp_both(c, m.reshape(n, width), cotangent.reshape(n, width), wup, wdown, bup, vec)
     dc = dc.reshape(tokens.shape)
@@ -753,8 +805,12 @@
     if by_hand:
         got_u = hop(send_u, "core")
         half = ff // 2
-        mine_a, got_a = y_step(keep_u[:, :half], got_u[:, :half])
-        mine_b, got_b = y_step(keep_u[:, half:], got_u[:, half:])
+        rest = keep_u.shape[0] // 2
+        mine_a, mine_b = [(keep_u[:rest, at], got_u[:rest, at]) for at in (slice(0, half), slice(half, ff))]
+        send_a = both(keep_u[rest:, :half], got_u[rest:, :half])
+        got_a = hop(send_a, "y")
+        send_b = both(held(keep_u, send_a)[rest:, half:], held(got_u, send_a)[rest:, half:])
+        got_b = hop(send_b, "y")
         back = attn_bwd(dc, dz, m, h, qkv, e, o, inv, proj, vec, 0, 1, True, (), (got_u,))
         terms_a = z_step(mine_a, held(got_a, back[3]))
         wait = (got_a,)
@@ -762,33 +818,30 @@
         back = attn_bwd(dc, dz, m, h, qkv, e, o, inv, proj, vec, 0, 1, True)
         wait = ()
     dh, dr, dqkv, smalls = back
-    g_bup = bup_u[0].reshape(width, per_row)
-    g_table = jnp.concatenate([smalls.T, g_bup], axis=1)
-    g_table = jnp.pad(g_table, ((0, 0), (0, 128 - used)))
+    g_bup = bup_u[0].reshape(width, per_row).T
     keep_p, send_p = proj_grad(
-        a.reshape(n, width), dqkv.reshape(n, 3 * width), o.reshape(n, width), dr.reshape(n, width), g_table, order, wait)
+        a.reshape(n, width), dqkv.reshape(n, 3 * width), o.reshape(n, width), dr.reshape(n, width), smalls, g_bup, order, wait)
     if by_hand:
         terms_b = z_step(mine_b, got_b)
         sum_up = jnp.concatenate([total(terms_a), total(terms_b)], axis=1)
-        mine_p, got_p = y_step(keep_p, hop(held(send_p, got_b, *terms_a[3:]), "core"))
-        sum_proj = total(z_step(mine_p, held(got_p, *terms_b)))
+        core_p = hop(held(send_p, got_b, *terms_a[3:]), "core")
+        mine_p, got_p = y_step(keep_p, core_p)
+        pieces = z_step(mine_p, held(got_p, *terms_b))[3:]
+        rest = finish((keep_p, core_p, got_p), pieces, shard, per_row)
     else:
         scatter = lambda *halves: lax.psum_scatter(jnp.concatenate(halves), "dp", scatter_dimension=0, tiled=True).astype(F32)
         sum_up = scatter(keep_u, send_u)
         sum_proj = scatter(keep_p, send_p)
-    vectors = sum_proj[:, 4 * width:4 * width + 8].T
-    return (
-        y.reshape((1,) + tokens.shape),
-        dh[None],
-        sum_proj[None, :, :3 * width],
-        sum_proj[None, :, 3 * width:4 * width],
-        sum_up[None],
-        sum_down[None],
-        vectors[None, 0:2],
-        vectors[None, 2:4],
-        vectors[None, 4:8],
-        sum_proj[:, 4 * width + 8:4 * width + used].reshape(1, -1),
-    )
+        vectors = sum_proj[:, 4 * width:4 * width + 8].T
+        rest = (
+            sum_proj[None, :, :3 * width],
+            sum_proj[None, :, 3 * width:4 * width],
+            vectors[None, 0:2],
+            vectors[None, 2:4],
+            vectors[None, 4:8],
+            sum_proj[:, 4 * width + 8:4 * width + used].reshape(1, -1),
+        )
+    return (y.reshape((1,) + tokens.shape), dh[None], rest[0], rest[1], sum_up[None], sum_down[None], *rest[2:])
 
 
 def solution(mesh):

time: 478 us -> 469 us (0.981)
  the two profiles are of different devices: /device:TPU:10 before, /device:TPU:0 now
where the time goes in v5:
time: 469 us; the launch traced here: 466 us
  Pallas kernels  239 us (51%)
  waiting for transfers between devices  133 us (28%)
  starting transfers between devices  49.2 us (10%)
  other arithmetic  18.8 us (4%)
  between operations  14.7 us (3%)
  local copies, waits for them, and re-layouts  11.1 us (2%)
    ppermute x44, waiting for transfers between devices, hop(): return lax.ppermute(value, 'dp', pairs)  124 us
    pallas_call x3, Pallas kernels, attn_bwd(): pl.pallas_call(body, grid=(count,), in_specs=in_specs, out_specs=specs, o...  55.2 us
    pallas_call x1, Pallas kernels, mlp_both(): pl.pallas_call(lambda *refs: mlp_both_body(rows, *refs), grid=(ff // chun...  43.6 us
    ppermute x44, starting transfers between devices, hop(): return lax.ppermute(value, 'dp', pairs)  41.6 us
    pallas_call x3, Pallas kernels, attn_fwd(): pl.pallas_call(lambda *refs: attn_fwd_body(save, at * count, *refs[:used]...  40.2 us
    pallas_call x1, Pallas kernels, mlp_grad(): pl.pallas_call(lambda *refs: mlp_grad_body(rows, *refs[:7], *refs[7 + wai...  22.5 us
    pallas_call x1, Pallas kernels, mlp_bwd(): pl.pallas_call(lambda *refs: mlp_bwd_body(save, rows, *refs[:4], *refs[le...  13.8 us
    pallas_call x1, Pallas kernels, mlp_up(): pl.pallas_call(lambda *refs: mlp_up_body(rows, *refs[:3], *refs[3 + waits...  12.7 us
  transfers between devices with their start and end apart: 50, of which 20 were waited for; matrix products, arithmetic and copies ran while one was open for 5% of the time, Pallas kernels for 26%

profile of v5, /device:TPU:0, one launch (start us, length us, event | category | flops | bytes accessed | tf_op | source)
XLA Modules:
  0.0 466.0 jit_solution(4759176215701521327)
XLA Ops:
  10.6 3.0 collective-permute-start.2
  13.7 3.6 collective-permute-start.1
  19.0 5.1 %collective-permute-done.1.refs_4_ = bf16[40,2688]{1,0:T(8,128)(2,1)S(1)} collective-permute-done((bf16[40,2688]{1,0:T(8,128)(2,1)S(1)}, bf16[40,2688]{1,0:T(8,128)(2,1)S(1)}, u32[]{:S(2)}, u32[]{:S(2)}) %collective-permute-start.1) | collective-permute-done | bytes 215072 | tf_op jit(solution)/shard_map/ppermute | solution.py:666
  24.1 9.1 %collective-permute-done.refs_2_ = bf16[40,2688]{1,0:T(8,128)(2,1)S(1)} collective-permute-done((bf16[40,2688]{1,0:T(8,128)(2,1)S(1)}, bf16[40,2688]{1,0:T(8,128)(2,1)S(1)}, u32[]{:S(2)}, u32[]{:S(2)}) %collective-permute-start) | collective-permute-done | bytes 215072 | tf_op jit(solution)/shard_map/ppermute | solution.py:666
  36.2 13.3 %collective-permute-done.3.refs_3_ = bf16[40,2688]{1,0:T(8,128)(2,1)S(1)} collective-permute-done((bf16[40,2688]{1,0:T(8,128)(2,1)S(1)}, bf16[40,2688]{1,0:T(8,128)(2,1)S(1)}, u32[]{:S(2)}, u32[]{:S(2)}) %collective-permute-start.3) | collective-permute-done | bytes 215072 | tf_op jit(solution)/shard_map/ppermute | solution.py:666
  50.1 8.7 %collective-permute-done.7.refs_7_ = bf16[40,2688]{1,0:T(8,128)(2,1)} collective-permute-done((bf16[40,2688]{1,0:T(8,128)(2,1)S(1)}, bf16[40,2688]{1,0:T(8,128)(2,1)}, u32[]{:S(2)}, u32[]{:S(2)}) %collective-permute-start.7) | collective-permute-done | bytes 215072 | tf_op jit(solution)/shard_map/ppermute | solution.py:666
  59.8 10.2 %collective-permute-done.16.refs_5_ = bf16[320,640]{1,0:T(8,128)(2,1)S(1)} collective-permute-done((bf16[320,640]{1,0:T(8,128)(2,1)S(1)}, bf16[320,640]{1,0:T(8,128)(2,1)S(1)}, u32[]{:S(2)}, u32[]{:S(2)}) %collective-permute-start.16) | collective-permute-done | bytes 409632 | tf_op jit(solution)/shard_map/ppermute | solution.py:666
  72.4 9.0 %collective-permute-start.18 = (bf16[320,640]{1,0:T(8,128)(2,1)S(1)}, bf16[320,640]{1,0:T(8,128)(2,1)S(1)}, u32[]{:S(2)}, u32[]{:S(2)}) collective-permute-start(bf16[320,640]{1,0:T(8,128)(2,1)S(1)} %bitcast.79), channel_id=1, source_target_pairs={{0,12},{1,13},{2,14},{3,15},{4,0},{5,1},{6,2},{7,3},{8,4},{9,5},{1... | collective-permute-start | bytes 1228808 | tf_op jit(solution)/shard_map/ppermute | solution.py:666
  83.0 4.7 %place_pieces.1 = bf16[16,40,2688]{2,1,0:T(8,128)(2,1)} custom-call(s32[16]{0:T(128)} %stack.67.refs_0_, bf16[40,2688]{1,0:T(8,128)(2,1)} %copy-done.8, bf16[40,2688]{1,0:T(8,128)(2,1)} %copy-done.26, bf16[40,2688]{1,0:T(8,128)(2,1)} %copy-done.27, bf16[40,2688]{1,0:T(8,128)(2,1)} %copy-done.25, bf16[40,2688]{1,0:T(8,128)(2,1)} %copy-done.24, ...), custom_call_target="tpu_custom_call" | custom-call | flops 4400000000 | bytes 1024 | tf_op jit(solution)/shard_map/place_pieces/pallas_call | solution.py:576
  87.6 16.8 %attention_forward.3 = (f32[4,256,640]{2,1,0:T(8,128)}, bf16[4,256,640]{2,1,0:T(8,128)(2,1)}) custom-call(s32[4]{0:T(128)} %refs_0_.1, bf16[4,256,640]{2,1,0:T(8,128)(2,1)} %refs_1_.7, bf16[640,2688]{1,0:T(8,128)(2,1)} %bitcast.59), custom_call_target="tpu_custom_call" | custom-call | flops 19800000512 | bytes 1024 | tf_op jit(solution)/shard_map/attention_forward/pallas_call | solution.py:131
  106.4 8.6 %collective-permute-done.17.refs_6_ = bf16[320,640]{1,0:T(8,128)(2,1)S(1)} collective-permute-done((bf16[320,640]{1,0:T(8,128)(2,1)S(1)}, bf16[320,640]{1,0:T(8,128)(2,1)S(1)}, u32[]{:S(2)}, u32[]{:S(2)}) %collective-permute-start.17) | collective-permute-done | bytes 409632 | tf_op jit(solution)/shard_map/ppermute | solution.py:666
  117.1 12.7 %feed_forward_up.1.refs_1_.refs_0_ = bf16[1024,5120]{1,0:T(8,128)(2,1)} custom-call(bf16[1024,640]{1,0:T(8,128)(2,1)} %bitcast.92, bf16[640,5120]{1,0:T(8,128)(2,1)} %bitcast.70, f32[1,5120]{1,0:T(1,128)} %reshape.200.refs_2_.refs_5_), custom_call_target="tpu_custom_call" | custom-call | flops 14080000000 | bytes 1024 | tf_op jit(solution)/shard_map/feed_forward_up/pallas_call | solution.py:248
  130.4 5.0 %collective-permute-done.21.refs_11_ = bf16[320,640]{1,0:T(8,128)(2,1)} collective-permute-done((bf16[320,640]{1,0:T(8,128)(2,1)S(1)}, bf16[320,640]{1,0:T(8,128)(2,1)}, u32[]{:S(2)}, u32[]{:S(2)}) %collective-permute-start.21) | collective-permute-done | bytes 409632 | tf_op jit(solution)/shard_map/ppermute | solution.py:666
  140.5 11.0 %place_and_feed_forward_down.1 = (bf16[5120,640]{1,0:T(8,128)(2,1)}, bf16[512,640]{1,0:T(8,128)(2,1)}) custom-call(s32[16]{0:T(128)} %stack.67.refs_0_, bf16[1024,5120]{1,0:T(8,128)(2,1)} %feed_forward_up.1.refs_1_.refs_0_, f32[1024,640]{1,0:T(8,128)} %bitcast.84, f32[8,640]{1,0:T(8,128)} %convert_bitcast_fusion.refs_3_.refs_4_.refs_6_.refs_9_, ...), custom_call_target="tpu_custom_call" | custom-call | flops 11000000512 | bytes 1024 | tf_op jit(solution)/shard_map/place_and_feed_forward_down/pallas_call | solution.py:606
  151.5 3.3 collective-permute-start.31
  154.8 8.8 %feed_forward_down.1 = bf16[512,640]{1,0:T(8,128)(2,1)} custom-call(bf16[1024,5120]{1,0:T(8,128)(2,1)} %feed_forward_up.1.refs_1_.refs_0_, f32[1024,640]{1,0:T(8,128)} %bitcast.85, bf16[5120,640]{1,0:T(8,128)(2,1)} %get-tuple-element.111.refs_2_.refs_4_.refs_3_, f32[8,640]{1,0:T(8,128)} %convert_bitcast_fusion.refs_3_.refs_4_.refs_6_.refs_9_), custom_call_target="tpu_custom_call" | custom-call | flops 9574400000 | bytes 1024 | tf_op jit(solution)/shard_map/feed_forward_down/pallas_call | solution.py:278
  165.1 5.0 %collective-permute-done.31.refs_2_ = bf16[2,256,640]{2,1,0:T(8,128)(2,1)S(1)} collective-permute-done((bf16[2,256,640]{2,1,0:T(8,128)(2,1)}, bf16[2,256,640]{2,1,0:T(8,128)(2,1)S(1)}, u32[]{:S(2)}, u32[]{:S(2)}) %collective-permute-start.31) | collective-permute-done | bytes 655392 | tf_op jit(solution)/shard_map/ppermute | solution.py:784
  171.0 11.7 %attention_forward.4 = (f32[4,256,640]{2,1,0:T(8,128)}, bf16[4,256,640]{2,1,0:T(8,128)(2,1)}, bf16[4,256,1920]{2,1,0:T(8,128)(2,1)}, bf16[4,20,256,256]{3,2,1,0:...) custom-call(s32[5]{0:T(128)} %pad_add_fusion.refs_0_, ...), custom_call_target="tpu_custom_call" | custom-call | flops 9900000256 | bytes 1024 | tf_op jit(solution)/shard_map/attention_forward/pallas_call | solution.py:131
  184.4 11.7 %attention_forward.5 = (f32[4,256,640]{2,1,0:T(8,128)}, bf16[4,256,640]{2,1,0:T(8,128)(2,1)}, bf16[4,256,1920]{2,1,0:T(8,128)(2,1)}, bf16[4,20,256,256]{3,2,1,0:...) custom-call(s32[5]{0:T(128)} %pad_add_fusion.refs_0_, ...), custom_call_target="tpu_custom_call", output_to_operand_aliasing={{0}: (5, {}), {1}: (6, {}), {2}: (7, {}), {3}: (8, {}), {4}... | custom-call | flops 9900000256 | bytes 1024 | tf_op jit(solution)/shard_map/attention_forward/pallas_call | solution.py:131
  196.1 43.6 %feed_forward_both.1 = (bf16[1024,640]{1,0:T(8,128)(2,1)}, bf16[1024,5120]{1,0:T(8,128)(2,1)}, bf16[1024,5120]{1,0:T(8,128)(2,1)}, f32[1024,640]{1,0:T(8,128)}) custom-call(bf16[1024,640]{1,0:T(8,128)(2,1)} %bitcast.93, f32[1024,640]{1,0:T(8,128)} %bitcast.86, bf16[1024,640]{1,0:T(8,128)(2,1)} %bitcast.54, bf16[640,5120]{1,0:T(8,128)(2,1)} %bitcast.71, ...), custom_call_target="tpu_custom_call" | custom-call | flops 46200000512 | bytes 1024 | tf_op jit(solution)/shard_map/feed_forward_both/pallas_call | solution.py:223
  239.7 15.0 %attention_back.4 = bf16[2,256,640]{2,1,0:T(8,128)(2,1)} custom-call(f32[4,256,640]{2,1,0:T(8,128)} %bitcast.88, bf16[4,256,640]{2,1,0:T(8,128)(2,1)} %refs_1_.9, f32[4,256,640]{2,1,0:T(8,128)} %get-tuple-element.123.refs_2_, bf16[4,256,640]{2,1,0:T(8,128)(2,1)} %get-tuple-element.126.refs_3_, bf16[4,256,1920]{2,1,0:T(8,128)(2,1)} %get-tuple-element.127.refs_4_, ...), custom_call_target="tpu_custom_call" | custom-call | flops 15399999488 | bytes 1024 | tf_op jit(solution)/shard_map/attention_back/pallas_call | solution.py:513
  256.1 14.7 %attention_back.3 = bf16[2,256,640]{2,1,0:T(8,128)(2,1)} custom-call(f32[4,256,640]{2,1,0:T(8,128)} %bitcast.89, bf16[4,256,640]{2,1,0:T(8,128)(2,1)} %refs_1_.9, f32[4,256,640]{2,1,0:T(8,128)} %get-tuple-element.123.refs_2_, bf16[4,256,640]{2,1,0:T(8,128)(2,1)} %get-tuple-element.126.refs_3_, bf16[4,256,1920]{2,1,0:T(8,128)(2,1)} %get-tuple-element.127.refs_4_, ...), custom_call_target="tpu_custom_call" | custom-call | flops 15399999488 | bytes 1024 | tf_op jit(solution)/shard_map/attention_back/pallas_call | solution.py:513
  274.0 13.8 %feed_forward_back.1 = (f32[1024,640]{1,0:T(8,128)}, bf16[512,5120]{1,0:T(8,128)(2,1)}) custom-call(bf16[512,640]{1,0:T(8,128)(2,1)} %bitcast.53, bf16[1024,5120]{1,0:T(8,128)(2,1)} %get-tuple-element.131.refs_1_, bf16[640,5120]{1,0:T(8,128)(2,1)} %bitcast.72, bf16[5120,640]{1,0:T(8,128)(2,1)} %get-tuple-element.111.refs_2_.refs_4_.refs_3_), custom_call_target="tpu_custom_call" | custom-call | flops 12099999744 | bytes 1024 | tf_op jit(solution)/shard_map/feed_forward_back/pallas_call | solution.py:315
  290.5 12.4 %down_gradient.1.refs_8_ = bf16[5120,640]{1,0:T(8,128)(2,1)} custom-call(bf16[1024,5120]{1,0:T(8,128)(2,1)} %get-tuple-element.135.refs_0_, bf16[1024,640]{1,0:T(8,128)(2,1)} %bitcast.55), custom_call_target="tpu_custom_call" | custom-call | flops 13200000000 | bytes 1024 | tf_op jit(solution)/shard_map/down_gradient/pallas_call | solution.py:413
  302.9 22.5 %feed_forward_gradients.1 = (f32[1024,640]{1,0:T(8,128)}, bf16[320,5120]{1,0:T(8,128)(2,1)}, bf16[320,5120]{1,0:T(8,128)(2,1)}, f32[8,5120]{1,0:T(8,128)}) custom-call(bf16[512,640]{1,0:T(8,128)(2,1)} %bitcast.52, bf16[1024,5120]{1,0:T(8,128)(2,1)} %get-tuple-element.131.refs_1_, bf16[640,5120]{1,0:T(8,128)(2,1)} %bitcast.73, ...), custom_call_target="tpu_custom_call", output_to_operand_aliasing={{0}: (7, {})} | custom-call | flops 23100000256 | bytes 1024 | tf_op jit(solution)/shard_map/feed_forward_gradients/pallas_call | solution.py:390
  336.6 25.5 %attention_back.5 = (f32[4,256,640]{2,1,0:T(8,128)}, bf16[4,256,640]{2,1,0:T(8,128)(2,1)}, bf16[4,256,1920]{2,1,0:T(8,128)(2,1)}, f32[8,640]{1,0:T(8,128)}) custom-call(f32[4,256,640]{2,1,0:T(8,128)} %bitcast.87, bf16[4,256,640]{2,1,0:T(8,128)(2,1)} %pad_maximum_fusion.refs_1_, f32[4,256,640]{2,1,0:T(8,128)} %get-tuple-element.123.refs_2_, ...), custom_call_target="tpu_custom_call" | custom-call | flops 30799998976 | bytes 1024 | tf_op jit(solution)/shard_map/attention_back/pallas_call | solution.py:513
  365.8 11.7 %projection_gradients.1 = (bf16[320,2688]{1,0:T(8,128)(2,1)}, bf16[320,2688]{1,0:T(8,128)(2,1)}) custom-call(bf16[1024,640]{1,0:T(8,128)(2,1)} %bitcast.96, bf16[1024,1920]{1,0:T(8,128)(2,1)} %bitcast.82, bf16[1024,640]{1,0:T(8,128)(2,1)} %bitcast.95, bf16[1024,640]{1,0:T(8,128)(2,1)} %bitcast.91, f32[8,640]{1,0:T(8,128)} %get-tuple-element.142.refs_4_, ...), custom_call_target="tpu_custom_call" | custom-call | flops 9900000256 | bytes 1024 | tf_op jit(solution)/shard_map/projection_gradients/pallas_call | solution.py:550
  377.5 8.5 %collective-permute-done.36 = bf16[160,2560]{1,0:T(8,128)(2,1)S(1)} collective-permute-done((bf16[160,2560]{1,0:T(8,128)(2,1)S(1)}, bf16[160,2560]{1,0:T(8,128)(2,1)S(1)}, u32[]{:S(2)}, u32[]{:S(2)}) %collective-permute-start.36) | collective-permute-done | bytes 819232 | tf_op jit(solution)/shard_map/ppermute | solution.py:666
  386.1 9.3 %collective-permute-done.38 = bf16[40,2560]{1,0:T(8,128)(2,1)S(1)} collective-permute-done((bf16[40,2560]{1,0:T(8,128)(2,1)S(1)}, bf16[40,2560]{1,0:T(8,128)(2,1)S(1)}, u32[]{:S(2)}, u32[]{:S(2)}) %collective-permute-start.38) | collective-permute-done | bytes 204832 | tf_op jit(solution)/shard_map/ppermute | solution.py:666
  402.6 3.6 collective-permute-done.44
  406.2 24.5 %collective-permute-done.43 = bf16[40,2560]{1,0:T(8,128)(2,1)S(1)} collective-permute-done((bf16[40,2560]{1,0:T(8,128)(2,1)S(1)}, bf16[40,2560]{1,0:T(8,128)(2,1)S(1)}, u32[]{:S(2)}, u32[]{:S(2)}) %collective-permute-start.43) | collective-permute-done | bytes 204832 | tf_op jit(solution)/shard_map/ppermute | solution.py:666
  440.1 13.0 %collective-permute-done.46.refs_4_ = bf16[40,2688]{1,0:T(8,128)(2,1)S(1)} collective-permute-done((bf16[40,2688]{1,0:T(8,128)(2,1)S(1)}, bf16[40,2688]{1,0:T(8,128)(2,1)S(1)}, u32[]{:S(2)}, u32[]{:S(2)}) %collective-permute-start.46) | collective-permute-done | bytes 215072 | tf_op jit(solution)/shard_map/ppermute | solution.py:666
  (187 shorter events, 72.1 us)
Async XLA Ops:
  7.2 109.9 %all-gather.3.cloned.1.call-start = ((), (), s32[]{:S(2)}) async-start(), calls=%async_computation.2 | async-start | bytes 6963200 | tf_op jit(solution)/shard_map/all_gather | solution.py:747
  7.9 449.1 %reduce-scatter.2.cloned.1.call-start = ((), (), s32[]{:S(2)}) async-start(), calls=%async_computation.1 | async-start | bytes 6963200 | tf_op jit(solution)/shard_map/reduce_scatter | solution.py:802
  17.3 15.9 %collective-permute-start = (bf16[40,2688]{1,0:T(8,128)(2,1)S(1)}, bf16[40,2688]{1,0:T(8,128)(2,1)S(1)}, u32[]{:S(2)}, u32[]{:S(2)}) collective-permute-start(bf16[40,2688]{1,0:T(8,128)(2,1)S(1)} %pad_maximum_fusion.1.refs_1_), channel_id=1, source_target_pairs={{0,4},{1,5},{2,6},{3,7},{4,8},{5,9},{6,10},{7,11},{8,12},{9,13},{1... | collective-permute-start | bytes 645128 | tf_op jit(solution)/shard_map/ppermute | solution.py:666
  17.3 19.0 %collective-permute-start.6 = (bf16[320,640]{1,0:T(8,128)(2,1)}, bf16[320,640]{1,0:T(8,128)(2,1)S(1)}, u32[]{:S(2)}, u32[]{:S(2)}) collective-permute-start(bf16[320,640]{1,0:T(8,128)(2,1)} %bitcast.76), channel_id=1, source_target_pairs={{0,2},{1,3},{2,0},{3,1},{4,6},{5,7},{6,4},{7,5},{8,10},{9,11},{10,... | collective-permute-start | bytes 1228808 | tf_op jit(solution)/shard_map/ppermute | solution.py:666
  33.1 16.3 %collective-permute-start.3 = (bf16[40,2688]{1,0:T(8,128)(2,1)S(1)}, bf16[40,2688]{1,0:T(8,128)(2,1)S(1)}, u32[]{:S(2)}, u32[]{:S(2)}) collective-permute-start(bf16[40,2688]{1,0:T(8,128)(2,1)S(1)} %pad_maximum_fusion.1.refs_1_), channel_id=1, source_target_pairs={{0,8},{1,9},{2,10},{3,11},{4,12},{5,13},{6,14},{7,15},{8,0},{9,1},... | collective-permute-start | bytes 645128 | tf_op jit(solution)/shard_map/ppermute | solution.py:666
  34.2 15.3 %collective-permute-start.4 = (bf16[40,2688]{1,0:T(8,128)(2,1)S(1)}, bf16[40,2688]{1,0:T(8,128)(2,1)S(1)}, u32[]{:S(2)}, u32[]{:S(2)}) collective-permute-start(bf16[40,2688]{1,0:T(8,128)(2,1)S(1)} %collective-permute-done.refs_2_), channel_id=1, source_target_pairs={{0,2},{1,3},{2,0},{3,1},{4,6},{5,7},{6,4},{7,5},{8,10},{9,11},{10,... | collective-permute-start | bytes 645128 | tf_op jit(solution)/shard_map/ppermute | solution.py:666
  34.2 15.3 %collective-permute-start.5 = (bf16[40,2688]{1,0:T(8,128)(2,1)S(1)}, bf16[40,2688]{1,0:T(8,128)(2,1)}, u32[]{:S(2)}, u32[]{:S(2)}) collective-permute-start(bf16[40,2688]{1,0:T(8,128)(2,1)S(1)} %collective-permute-done.1.refs_4_), channel_id=1, source_target_pairs={{0,2},{1,3},{2,0},{3,1},{4,6},{5,7},{6,4},{7,5},{8,10},{9,11},{10,... | collective-permute-start | bytes 645128 | tf_op jit(solution)/shard_map/ppermute | solution.py:666
  50.1 19.9 %collective-permute-start.16 = (bf16[320,640]{1,0:T(8,128)(2,1)S(1)}, bf16[320,640]{1,0:T(8,128)(2,1)S(1)}, u32[]{:S(2)}, u32[]{:S(2)}) collective-permute-start(bf16[320,640]{1,0:T(8,128)(2,1)S(1)} %bitcast.78), channel_id=1, source_target_pairs={{0,4},{1,5},{2,6},{3,7},{4,8},{5,9},{6,10},{7,11},{8,12},{9,13},{1... | collective-permute-start | bytes 1228808 | tf_op jit(solution)/shard_map/ppermute | solution.py:666
  58.8 11.7 %collective-permute-start.9 = (bf16[40,2688]{1,0:T(8,128)(2,1)S(1)}, bf16[40,2688]{1,0:T(8,128)(2,1)S(1)}, u32[]{:S(2)}, u32[]{:S(2)}) collective-permute-start(bf16[40,2688]{1,0:T(8,128)(2,1)S(1)} %collective-permute-done.refs_2_), channel_id=1, source_target_pairs={{0,1},{1,0},{2,3},{3,2},{4,5},{5,4},{6,7},{7,6},{8,9},{9,8},{10,11... | collective-permute-start | bytes 645128 | tf_op jit(solution)/shard_map/ppermute | solution.py:666
  59.3 13.0 %collective-permute-start.11 = (bf16[40,2688]{1,0:T(8,128)(2,1)S(1)}, bf16[40,2688]{1,0:T(8,128)(2,1)}, u32[]{:S(2)}, u32[]{:S(2)}) collective-permute-start(bf16[40,2688]{1,0:T(8,128)(2,1)S(1)} %collective-permute-done.1.refs_4_), channel_id=1, source_target_pairs={{0,1},{1,0},{2,3},{3,2},{4,5},{5,4},{6,7},{7,6},{8,9},{9,8},{10,11... | collective-permute-start | bytes 645128 | tf_op jit(solution)/shard_map/ppermute | solution.py:666
  70.0 11.3 %collective-permute-start.13 = (bf16[40,2688]{1,0:T(8,128)(2,1)S(1)}, bf16[40,2688]{1,0:T(8,128)(2,1)}, u32[]{:S(2)}, u32[]{:S(2)}) collective-permute-start(bf16[40,2688]{1,0:T(8,128)(2,1)S(1)} %collective-permute-done.4.refs_6_), channel_id=1, source_target_pairs={{0,1},{1,0},{2,3},{3,2},{4,5},{5,4},{6,7},{7,6},{8,9},{9,8},{10,11... | collective-permute-start | bytes 645128 | tf_op jit(solution)/shard_map/ppermute | solution.py:666
  70.5 12.4 %collective-permute-start.14 = (bf16[40,2688]{1,0:T(8,128)(2,1)}, bf16[40,2688]{1,0:T(8,128)(2,1)}, u32[]{:S(2)}, u32[]{:S(2)}) collective-permute-start(bf16[40,2688]{1,0:T(8,128)(2,1)} %collective-permute-done.7.refs_7_), channel_id=1, source_target_pairs={{0,1},{1,0},{2,3},{3,2},{4,5},{5,4},{6,7},{7,6},{8,9},{9,8},{10,11... | collective-permute-start | bytes 645128 | tf_op jit(solution)/shard_map/ppermute | solution.py:666
  71.3 11.6 %collective-permute-start.15 = (bf16[40,2688]{1,0:T(8,128)(2,1)}, bf16[40,2688]{1,0:T(8,128)(2,1)}, u32[]{:S(2)}, u32[]{:S(2)}) collective-permute-start(bf16[40,2688]{1,0:T(8,128)(2,1)} %collective-permute-done.5.refs_8_), channel_id=1, source_target_pairs={{0,1},{1,0},{2,3},{3,2},{4,5},{5,4},{6,7},{7,6},{8,9},{9,8},{10,11... | collective-permute-start | bytes 645128 | tf_op jit(solution)/shard_map/ppermute | solution.py:666
  72.4 34.0 %collective-permute-start.18 = (bf16[320,640]{1,0:T(8,128)(2,1)S(1)}, bf16[320,640]{1,0:T(8,128)(2,1)S(1)}, u32[]{:S(2)}, u32[]{:S(2)}) collective-permute-start(bf16[320,640]{1,0:T(8,128)(2,1)S(1)} %bitcast.79), channel_id=1, source_target_pairs={{0,12},{1,13},{2,14},{3,15},{4,0},{5,1},{6,2},{7,3},{8,4},{9,5},{1... | collective-permute-start | bytes 1228808 | tf_op jit(solution)/shard_map/ppermute | solution.py:666
  81.3 33.6 %collective-permute-start.17 = (bf16[320,640]{1,0:T(8,128)(2,1)S(1)}, bf16[320,640]{1,0:T(8,128)(2,1)S(1)}, u32[]{:S(2)}, u32[]{:S(2)}) collective-permute-start(bf16[320,640]{1,0:T(8,128)(2,1)S(1)} %bitcast.80), channel_id=1, source_target_pairs={{0,8},{1,9},{2,10},{3,11},{4,12},{5,13},{6,14},{7,15},{8,0},{9,1},... | collective-permute-start | bytes 1228808 | tf_op jit(solution)/shard_map/ppermute | solution.py:666
  81.3 33.6 %collective-permute-start.19 = (bf16[320,640]{1,0:T(8,128)(2,1)S(1)}, bf16[320,640]{1,0:T(8,128)(2,1)S(1)}, u32[]{:S(2)}, u32[]{:S(2)}) collective-permute-start(bf16[320,640]{1,0:T(8,128)(2,1)S(1)} %collective-permute-done.16.refs_5_), channel_id=1, source_target_pairs={{0,2},{1,3},{2,0},{3,1},{4,6},{5,7},{6,4},{7,5},{8,10},{9,11},{10,... | collective-permute-start | bytes 1228808 | tf_op jit(solution)/shard_map/ppermute | solution.py:666
  115.0 20.4 %collective-permute-start.20 = (bf16[320,640]{1,0:T(8,128)(2,1)S(1)}, bf16[320,640]{1,0:T(8,128)(2,1)S(1)}, u32[]{:S(2)}, u32[]{:S(2)}) collective-permute-start(bf16[320,640]{1,0:T(8,128)(2,1)S(1)} %collective-permute-done.17.refs_6_), channel_id=1, source_target_pairs={{0,2},{1,3},{2,0},{3,1},{4,6},{5,7},{6,4},{7,5},{8,10},{9,11},{10,... | collective-permute-start | bytes 1228808 | tf_op jit(solution)/shard_map/ppermute | solution.py:666
  116.7 18.7 %collective-permute-start.21 = (bf16[320,640]{1,0:T(8,128)(2,1)S(1)}, bf16[320,640]{1,0:T(8,128)(2,1)}, u32[]{:S(2)}, u32[]{:S(2)}) collective-permute-start(bf16[320,640]{1,0:T(8,128)(2,1)S(1)} %collective-permute-done.18.refs_7_), channel_id=1, source_target_pairs={{0,2},{1,3},{2,0},{3,1},{4,6},{5,7},{6,4},{7,5},{8,10},{9,11},{10,... | collective-permute-start | bytes 1228808 | tf_op jit(solution)/shard_map/ppermute | solution.py:666
  151.5 18.6 %collective-permute-start.31 = (bf16[2,256,640]{2,1,0:T(8,128)(2,1)}, bf16[2,256,640]{2,1,0:T(8,128)(2,1)S(1)}, u32[]{:S(2)}, u32[]{:S(2)}) collective-permute-start(bf16[2,256,640]{2,1,0:T(8,128)(2,1)} %bitcast.74), channel_id=1, source_target_pairs={{0,16},{1,17},{2,18},{3,19},{4,20},{5,21},{6,22},{7,23},{8,24},{9,... | collective-permute-start | bytes 1966088 | tf_op jit(solution)/shard_map/ppermute | solution.py:784
  163.6 19.9 %collective-permute-start.30 = (bf16[2,256,640]{2,1,0:T(8,128)(2,1)}, bf16[2,256,640]{2,1,0:T(8,128)(2,1)S(1)}, u32[]{:S(2)}, u32[]{:S(2)}) collective-permute-start(bf16[2,256,640]{2,1,0:T(8,128)(2,1)} %bitcast.75), channel_id=1, source_target_pairs={{0,16},{1,17},{2,18},{3,19},{4,20},{5,21},{6,22},{7,23},{8,24},{9,... | collective-permute-start | bytes 1966088 | tf_op jit(solution)/shard_map/ppermute | solution.py:784
  254.7 18.4 %collective-permute-start.33 = (bf16[2,256,640]{2,1,0:T(8,128)(2,1)}, bf16[2,256,640]{2,1,0:T(8,128)(2,1)S(1)}, u32[]{:S(2)}, u32[]{:S(2)}) collective-permute-start(bf16[2,256,640]{2,1,0:T(8,128)(2,1)} %attention_back.4), channel_id=1, source_target_pairs={{16,0},{17,1},{18,2},{19,3},{20,4},{21,5},{22,6},{23,7},{24,8},{25... | collective-permute-start | bytes 1966088 | tf_op jit(solution)/shard_map/ppermute | solution.py:795
  270.9 18.3 %collective-permute-start.32 = (bf16[2,256,640]{2,1,0:T(8,128)(2,1)}, bf16[2,256,640]{2,1,0:T(8,128)(2,1)S(1)}, u32[]{:S(2)}, u32[]{:S(2)}) collective-permute-start(bf16[2,256,640]{2,1,0:T(8,128)(2,1)} %attention_back.3), channel_id=1, source_target_pairs={{16,0},{17,1},{18,2},{19,3},{20,4},{21,5},{22,6},{23,7},{24,8},{25... | collective-permute-start | bytes 1966088 | tf_op jit(solution)/shard_map/ppermute | solution.py:795
  333.0 29.0 %collective-permute-start.35 = (bf16[160,2560]{1,0:T(8,128)(2,1)S(1)}, bf16[160,2560]{1,0:T(8,128)(2,1)S(1)}, u32[]{:S(2)}, u32[]{:S(2)}) collective-permute-start(bf16[160,2560]{1,0:T(8,128)(2,1)S(1)} %add_convert_fusion.2), channel_id=1, source_target_pairs={{0,2},{1,3},{2,0},{3,1},{4,6},{5,7},{6,4},{7,5},{8,10},{9,11},{10,... | collective-permute-start | bytes 2457608 | tf_op jit(solution)/shard_map/ppermute | solution.py:666
  335.9 50.2 %collective-permute-start.36 = (bf16[160,2560]{1,0:T(8,128)(2,1)S(1)}, bf16[160,2560]{1,0:T(8,128)(2,1)S(1)}, u32[]{:S(2)}, u32[]{:S(2)}) collective-permute-start(bf16[160,2560]{1,0:T(8,128)(2,1)S(1)} %add_convert_fusion.1), channel_id=1, source_target_pairs={{0,2},{1,3},{2,0},{3,1},{4,6},{5,7},{6,4},{7,5},{8,10},{9,11},{10,... | collective-permute-start | bytes 2457608 | tf_op jit(solution)/shard_map/ppermute | solution.py:666
  363.7 22.4 %collective-permute-start.39 = (bf16[40,2560]{1,0:T(8,128)(2,1)S(1)}, bf16[40,2560]{1,0:T(8,128)(2,1)S(1)}, u32[]{:S(2)}, u32[]{:S(2)}) collective-permute-start(bf16[40,2560]{1,0:T(8,128)(2,1)S(1)} %get-tuple-element.161), channel_id=1, source_target_pairs={{0,12},{1,13},{2,14},{3,15},{4,0},{5,1},{6,2},{7,3},{8,4},{9,5},{1... | collective-permute-start | bytes 614408 | tf_op jit(solution)/shard_map/ppermute | solution.py:666
  363.8 31.6 %collective-permute-start.38 = (bf16[40,2560]{1,0:T(8,128)(2,1)S(1)}, bf16[40,2560]{1,0:T(8,128)(2,1)S(1)}, u32[]{:S(2)}, u32[]{:S(2)}) collective-permute-start(bf16[40,2560]{1,0:T(8,128)(2,1)S(1)} %get-tuple-element.162), channel_id=1, source_target_pairs={{0,8},{1,9},{2,10},{3,11},{4,12},{5,13},{6,14},{7,15},{8,0},{9,1},... | collective-permute-start | bytes 614408 | tf_op jit(solution)/shard_map/ppermute | solution.py:666
  363.9 31.5 %collective-permute-start.37 = (bf16[40,2560]{1,0:T(8,128)(2,1)S(1)}, bf16[40,2560]{1,0:T(8,128)(2,1)S(1)}, u32[]{:S(2)}, u32[]{:S(2)}) collective-permute-start(bf16[40,2560]{1,0:T(8,128)(2,1)S(1)} %get-tuple-element.163), channel_id=1, source_target_pairs={{0,4},{1,5},{2,6},{3,7},{4,8},{5,9},{6,10},{7,11},{8,12},{9,13},{1... | collective-permute-start | bytes 614408 | tf_op jit(solution)/shard_map/ppermute | solution.py:666
  397.3 33.4 %collective-permute-start.43 = (bf16[40,2560]{1,0:T(8,128)(2,1)S(1)}, bf16[40,2560]{1,0:T(8,128)(2,1)S(1)}, u32[]{:S(2)}, u32[]{:S(2)}) collective-permute-start(bf16[40,2560]{1,0:T(8,128)(2,1)S(1)} %get-tuple-element.159), channel_id=1, source_target_pairs={{0,8},{1,9},{2,10},{3,11},{4,12},{5,13},{6,14},{7,15},{8,0},{9,1},... | collective-permute-start | bytes 614408 | tf_op jit(solution)/shard_map/ppermute | solution.py:666
  397.8 33.0 %collective-permute-start.42 = (bf16[40,2560]{1,0:T(8,128)(2,1)S(1)}, bf16[40,2560]{1,0:T(8,128)(2,1)S(1)}, u32[]{:S(2)}, u32[]{:S(2)}) collective-permute-start(bf16[40,2560]{1,0:T(8,128)(2,1)S(1)} %get-tuple-element.160), channel_id=1, source_target_pairs={{0,4},{1,5},{2,6},{3,7},{4,8},{5,9},{6,10},{7,11},{8,12},{9,13},{1... | collective-permute-start | bytes 614408 | tf_op jit(solution)/shard_map/ppermute | solution.py:666
  399.9 31.9 %collective-permute-start.41 = (bf16[160,2688]{1,0:T(8,128)(2,1)S(1)}, bf16[160,2688]{1,0:T(8,128)(2,1)S(1)}, u32[]{:S(2)}, u32[]{:S(2)}) collective-permute-start(bf16[160,2688]{1,0:T(8,128)(2,1)S(1)} %add_convert_fusion), channel_id=1, source_target_pairs={{0,2},{1,3},{2,0},{3,1},{4,6},{5,7},{6,4},{7,5},{8,10},{9,11},{10,... | collective-permute-start | bytes 2580488 | tf_op jit(solution)/shard_map/ppermute | solution.py:666
  432.2 20.9 %collective-permute-start.46 = (bf16[40,2688]{1,0:T(8,128)(2,1)S(1)}, bf16[40,2688]{1,0:T(8,128)(2,1)S(1)}, u32[]{:S(2)}, u32[]{:S(2)}) collective-permute-start(bf16[40,2688]{1,0:T(8,128)(2,1)S(1)} %get-tuple-element.166), channel_id=1, source_target_pairs={{0,8},{1,9},{2,10},{3,11},{4,12},{5,13},{6,14},{7,15},{8,0},{9,1},... | collective-permute-start | bytes 645128 | tf_op jit(solution)/shard_map/ppermute | solution.py:666
  434.7 18.4 %collective-permute-start.45 = (bf16[40,2688]{1,0:T(8,128)(2,1)S(1)}, bf16[40,2688]{1,0:T(8,128)(2,1)S(1)}, u32[]{:S(2)}, u32[]{:S(2)}) collective-permute-start(bf16[40,2688]{1,0:T(8,128)(2,1)S(1)} %get-tuple-element.167), channel_id=1, source_target_pairs={{0,4},{1,5},{2,6},{3,7},{4,8},{5,9},{6,10},{7,11},{8,12},{9,13},{1... | collective-permute-start | bytes 645128 | tf_op jit(solution)/shard_map/ppermute | solution.py:666
  (54 other events, 837.7 us)
Sparse Core Ops, SparseCore 0:
  10.3 86.0 all-gather.2
  325.6 107.5 reduce-scatter.1
